TPU v7x, 128 devices: a whole 4x4x4 slice. The times are simulated.
128 devices in a mesh: row: 16 (over x, z), col: 8 (over y, core).
Axes of the slice: x: 4, y: 4, z: 4, core: 2. Of those that a mesh axis runs over, the one named last changes fastest.
Arguments:
- inputs: bfloat16 [1024, 12288], P('row', 'col'), may hold values from -0.1875 to 0.1875
- pre_act: bfloat16 [1024, 49152], P('col', 'row'), may hold values from -6 to 6
- grad_out: bfloat16 [1024, 49152], P('col', 'row'), may hold values from -6 to 6
- weight: bfloat16 [12288, 49152], P('col', 'row'), may hold values from -0.02734375 to 0.02734375
Outputs:
- grad_input: bfloat16 [1024, 12288], P('row', 'col')
- grad_weight: bfloat16 [12288, 49152], P('col', 'row')
All inputs are finite; a program needn't handle non-finite values.
Results may differ from a plain program's by a relative error of at most 0.019.
Values may be sent and summed in bfloat16 or wider, within the bound.
No kernel may reach another device: no remote copies, remote signals or barrier semaphores. Data moves between devices by JAX's collectives and lax.ppermute only.
A program may use at most 128 MiB of HBM per device.

v0:
```python
import jax
import jax.numpy as jnp
from jax import lax
from jax.sharding import PartitionSpec as P


def gelu_slope(value):
    coeff = 0.7978845608
    inner = coeff * (value + 0.044715 * value * value * value)
    tanh_u = jnp.tanh(inner)
    return 0.5 * (1.0 + tanh_u) + 0.5 * value * (1.0 - tanh_u * tanh_u) * coeff * (
        1.0 + 3.0 * 0.044715 * value * value
    )


def hidden_cotangent(pre_values, out_values):
    return (out_values.astype(jnp.float32) * gelu_slope(pre_values.astype(jnp.float32))).astype(
        jnp.bfloat16
    )


def on_device(inputs, pre_act, grad_out, weight):
    local_grad = hidden_cotangent(pre_act, grad_out)
    grad_hidden = lax.all_gather(local_grad, "col", axis=0, tiled=True)
    weight_total = lax.dot_general(
        lax.all_gather(inputs, "row", axis=0, tiled=True),
        grad_hidden,
        (((0,), (0,)), ((), ())),
        preferred_element_type=jnp.float32,
    )
    grad_weight = weight_total.astype(jnp.bfloat16)
    partial_input = lax.dot_general(
        grad_hidden, weight, (((1,), (1,)), ((), ())), preferred_element_type=jnp.float32
    )
    grad_input = lax.psum_scatter(
        partial_input.astype(jnp.bfloat16), "row", scatter_dimension=0, tiled=True
    )
    return (grad_input, grad_weight)


def solution(mesh):
    return jax.shard_map(
        on_device,
        mesh=mesh,
        in_specs=(P("row", "col"), P("col", "row"), P("col", "row"), P("col", "row")),
        out_specs=(P("row", "col"), P("col", "row")),
        check_vma=False,
    )
```

profile of v0, /device:TPU:0, one launch (start us, length us, event | category | flops | bytes accessed | tf_op | source)
XLA Modules:
  0.0 189.7 jit_solution(15668657228104262698)
XLA Ops:
  7.2 0.0 all-gather.3.cloned.1.call-start
  7.2 3.3 %fusion.8 = bf16[128,3072]{1,0:T(8,128)(2,1)} fusion(bf16[128,3072]{1,0:T(8,128)(2,1)} %param.5, bf16[128,3072]{1,0:T(8,128)(2,1)} %param.6), kind=kLoop, calls=%fused_computation.17 | loop fusion | flops 8257536 | bytes 2359296 | tf_op jit(solution)/shard_map/convert_element_type | solution.py:17
  10.6 0.0 all-gather.3.cloned.1.call-update
  10.6 0.0 all-gather.5.cloned.1.call-start
  10.6 0.7 all-gather.5.cloned.1.call-update
  11.3 0.0 reduce-scatter.2.cloned.1.call-start
  11.4 42.7 %all-gather.3.cloned.1.call-done = bf16[1024,3072]{1,0:T(8,128)(2,1)} async-done(((bf16[128,3072]{1,0:T(8,128)(2,1)}), bf16[1024,3072]{1,0:T(8,128)(2,1)}) %all-gather.3.cloned.1.call-update) | async-done | bytes 6291472 | tf_op jit(solution)/shard_map/all_gather | solution.py:24
  54.1 15.6 %convolution_convert_fusion.1 = bf16[1024,1536]{1,0:T(8,128)(2,1)} fusion(bf16[1024,3072]{1,0:T(8,128)(2,1)} %all-gather.3.cloned.1.call-done, bf16[1536,3072]{1,0:T(8,128)(2,1)} %param.7), kind=kOutput, calls=%fused_computation.9 | convolution fusion | flops 9665249280 | bytes 18874368 | tf_op jit(solution)/shard_map/dot_general | solution.py:32
  69.7 0.0 reduce-scatter.2.cloned.1.call-update
  69.8 34.7 %all-gather.5.cloned.1.call-done = bf16[1024,1536]{1,0:T(8,128)(2,1)} async-done(((bf16[64,1536]{1,0:T(8,128)(2,1)}), bf16[1024,1536]{1,0:T(8,128)(2,1)}) %all-gather.5.cloned.1.call-update) | async-done | bytes 3145744 | tf_op jit(solution)/shard_map/all_gather | solution.py:26
  104.5 15.2 %fusion = bf16[1536,3072]{0,1:T(8,128)(2,1)} fusion(bf16[1024,3072]{1,0:T(8,128)(2,1)} %all-gather.3.cloned.1.call-done, bf16[1024,1536]{1,0:T(8,128)(2,1)} %all-gather.5.cloned.1.call-done), kind=kOutput, calls=%fused_computation.1 | convolution fusion | flops 9668395008 | bytes 18874368 | tf_op jit(solution)/shard_map/dot_general | solution.py:25
  119.7 12.6 %copy.6 = bf16[1536,3072]{1,0:T(8,128)(2,1)} copy(bf16[1536,3072]{0,1:T(8,128)(2,1)} %fusion) | data formatting | bytes 18874368
  132.3 50.8 %reduce-scatter.2.cloned.1.call-done = bf16[64,1536]{1,0:T(8,128)(2,1)} async-done(((bf16[1024,1536]{1,0:T(8,128)(2,1)}), bf16[64,1536]{1,0:T(8,128)(2,1)}) %reduce-scatter.2.cloned.1.call-update) | async-done | bytes 196624 | tf_op jit(solution)/shard_map/reduce_scatter | solution.py:35
Async XLA Ops:
  7.2 47.0 %all-gather.3.cloned.1.call-start = ((), (), s32[]{:S(2)}) async-start(), calls=%async_computation.1 | async-start | bytes 7077888 | tf_op jit(solution)/shard_map/all_gather | solution.py:24
  10.6 93.9 %all-gather.5.cloned.1.call-start = ((), (), s32[]{:S(2)}) async-start(), calls=%async_computation.3 | async-start | bytes 3342336 | tf_op jit(solution)/shard_map/all_gather | solution.py:26
  11.3 171.8 %reduce-scatter.2.cloned.1.call-start = ((), (), s32[]{:S(2)}) async-start(), calls=%async_computation.2 | async-start | bytes 3342336 | tf_op jit(solution)/shard_map/reduce_scatter | solution.py:35
Sparse Core Ops, SparseCore 0:
  10.7 43.3 all-gather.2
  56.3 48.1 all-gather.4
  108.4 74.6 reduce-scatter.1
where the time goes:
time: 190 us
  waiting for transfers between devices  129 us (68%)
  matrix products  30.8 us (16%)
  between operations  13.7 us (7%)
  local copies, waits for them, and re-layouts  12.6 us (7%)
  other arithmetic  3.34 us (2%)
    reduce_scatter x1, waiting for transfers between devices, on_device(): lax.psum_scatter(partial_input.astype(jnp.bfloat16), 'row', scatter_dimen...  50.8 us
    all_gather x1, waiting for transfers between devices, on_device(): grad_hidden = lax.all_gather(local_grad, 'col', axis=0, tiled=True)  42.7 us
    all_gather x1, waiting for transfers between devices, on_device(): lax.all_gather(inputs, 'row', axis=0, tiled=True)  34.7 us
    dot_general x1, matrix products, on_device(): lax.dot_general(grad_hidden, weight, (((1,), (1,)), ((), ())), preferred_...  15.6 us
    dot_general x1, matrix products, on_device(): lax.dot_general(lax.all_gather(inputs, 'row', axis=0, tiled=True), grad_h...  15.2 us
    unnamed x1, local copies, waits for them, and re-layouts  12.6 us
  transfers between devices with their start and end apart: 3, of which 3 were waited for; matrix products, arithmetic and copies ran while one was open for 23% of the time, Pallas kernels for 0%

commit v1 on v0

v1 whole, which is shorter than its diff:
```python
import functools

import jax
import jax.numpy as jnp
from jax import lax
from jax.experimental import pallas as pl
from jax.experimental.pallas import tpu as pltpu
from jax.sharding import PartitionSpec as P

BF = jnp.bfloat16
F32 = jnp.float32
SIDE = 4
TILE = 768
WHOLE = pl.BlockSpec(memory_space=pltpu.VMEM)
FAR = pl.BlockSpec(memory_space=pltpu.HBM)
CHEAP = pl.CostEstimate(flops=1, bytes_accessed=1, transcendentals=0)


def gelu_slope(value):
    coeff = 0.7978845608
    inner = coeff * (value + 0.044715 * value * value * value)
    tanh_u = jnp.tanh(inner)
    return 0.5 * (1.0 + tanh_u) + 0.5 * value * (1.0 - tanh_u * tanh_u) * coeff * (
        1.0 + 3.0 * 0.044715 * value * value
    )


def hidden_cotangent(pre_values, out_values):
    return (out_values.astype(F32) * gelu_slope(pre_values.astype(F32))).astype(BF)


def move(array, step):
    pairs = []
    for x in range(SIDE):
        for z in range(SIDE):
            for y in range(SIDE):
                for c in range(2):
                    to_x, to_y, to_z, to_c = step(x, y, z, c)
                    to = ((to_x % SIDE * SIDE + to_z % SIDE) * SIDE + to_y % SIDE) * 2 + to_c
                    pairs.append((((x * SIDE + z) * SIDE + y) * 2 + c, to))
    return lax.ppermute(array, ("row", "col"), pairs)


def ring(array):
    return move(array, lambda x, y, z, c: (x, y + 1 - 2 * c, z, c))


def swap_core(array):
    return move(array, lambda x, y, z, c: (x, y, z, 1 - c))


def near(array, by):
    return move(array, lambda x, y, z, c: (x + by * c, y, z + by * (1 - c), c))


def far(array, by):
    return move(array, lambda x, y, z, c: (x + by * (1 - c), y, z + by * c, c))


def after(value, *others):
    return lax.optimization_barrier((value, *others))[0]


def fetch_kernel(source, target, sem):
    copy = pltpu.make_async_copy(source, target, sem)
    copy.start()
    copy.wait()


def fetch(array):
    return pl.pallas_call(
        fetch_kernel,
        out_shape=pltpu.VMEM(array.shape, array.dtype),
        in_specs=[FAR],
        out_specs=WHOLE,
        scratch_shapes=[pltpu.SemaphoreType.DMA],
        compiler_params=pltpu.CompilerParams(vmem_limit_bytes=12 * 2**20),
        cost_estimate=CHEAP,
    )(pltpu.with_memory_space_constraint(array, pltpu.HBM))


def partial_kernel(hops, has_store, *refs):
    count = 2 * len(hops)
    blocks, weight = refs[:count], refs[count]
    refs = refs[count + 1 :]
    if has_store:
        refs = refs[1 + SIDE :]
    store, outs, rows, sems = refs[0], refs[1 : 1 + SIDE], refs[-2], refs[-1]
    x, z = lax.axis_index("row") // SIDE, lax.axis_index("row") % SIDE
    y, c = lax.axis_index("col") // 2, lax.axis_index("col") % 2
    tokens = blocks[0].shape[1]
    places, copies = [], []
    for i, hop in enumerate(hops):
        for other in range(2):
            owner = 1 - c if other else c
            to_x = lax.rem(y + SIDE + jnp.where(owner == 0, -hop, hop), SIDE)
            for h in range(2):
                to_z = 2 * owner + h
                x_off, z_off = lax.rem(to_x + SIDE - x, SIDE), lax.rem(to_z + SIDE - z, SIDE)
                n_off, f_off = jnp.where(c == 0, z_off, x_off), jnp.where(c == 0, x_off, z_off)
                block, at = blocks[2 * i + other].at[h], len(places)
                copies.append(pltpu.make_async_copy(block, store.at[n_off, f_off], sems.at[at]))
                copies[-1].start()
                rows[at] = block[...]
                places.append((n_off, f_off))
    hidden = rows[...].reshape(len(places) * tokens, -1)
    for d in range(0, weight.shape[0], TILE):
        total = lax.dot_general(
            hidden, weight[d : d + TILE, :], (((1,), (1,)), ((), ())), preferred_element_type=F32
        ).astype(BF).reshape(len(places), tokens, TILE)
        for i, (n_off, f_off) in enumerate(places):
            for k in range(SIDE):

                @pl.when(n_off == k)
                def _():
                    outs[k][f_off, :, d : d + TILE] = total[i]

    for copy in copies:
        copy.wait()


def partial_input(hops, blocks, weight, store, outs):
    wide, hidden = weight.shape
    tokens = blocks[0].shape[1]
    given = [] if store is None else [store, *outs]
    first = len(blocks) + 1
    result = pl.pallas_call(
        functools.partial(partial_kernel, hops, bool(given)),
        out_shape=[pltpu.HBM((SIDE, SIDE, tokens, hidden), BF)]
        + [pltpu.VMEM((SIDE, tokens, wide), BF)] * SIDE,
        in_specs=[WHOLE] * first + ([FAR] + [WHOLE] * SIDE if given else []),
        out_specs=[FAR] + [WHOLE] * SIDE,
        scratch_shapes=[
            pltpu.VMEM((2 * len(blocks), tokens, hidden), BF),
            pltpu.SemaphoreType.DMA((2 * len(blocks),)),
        ],
        input_output_aliases={first + i: i for i in range(len(given))},
        compiler_params=pltpu.CompilerParams(vmem_limit_bytes=28 * 2**20),
        cost_estimate=CHEAP,
    )(*blocks, weight, *given)
    return result[0], list(result[1:])


def sum_kernel(*refs):
    terms, outs = refs[:SIDE], refs[SIDE:]
    for k in range(len(outs)):
        total = terms[0][k].astype(F32)
        for term in terms[1:]:
            total += term[k].astype(F32)
        outs[k][...] = total.astype(BF)


def sum_terms(terms):
    shape = terms[0].shape
    return pl.pallas_call(
        sum_kernel,
        out_shape=[pltpu.VMEM(shape[1:], BF)] * shape[0],
        in_specs=[WHOLE] * len(terms),
        out_specs=[WHOLE] * shape[0],
        cost_estimate=CHEAP,
    )(*terms)


def last_sum(terms):
    total = terms[0].astype(F32)
    for term in terms[1:]:
        total += term.astype(F32)
    return total.astype(BF)


def transpose_kernel(*refs):
    blocks, out, rows = refs[:SIDE], refs[SIDE], refs[SIDE + 1]
    tokens = blocks[0].shape[1]
    for n_off in range(SIDE):
        for f_off in range(SIDE):
            at = (n_off * SIDE + f_off) * tokens
            rows[at : at + tokens, :] = blocks[f_off][n_off]
    out[...] = rows[...].T


def transposed_inputs(blocks):
    _, tokens, wide = blocks[0].shape
    tokens *= SIDE * SIDE
    return pl.pallas_call(
        transpose_kernel,
        out_shape=pltpu.VMEM((wide, tokens), BF),
        in_specs=[WHOLE] * SIDE,
        out_specs=WHOLE,
        scratch_shapes=[pltpu.VMEM((tokens, wide), BF)],
        compiler_params=pltpu.CompilerParams(vmem_limit_bytes=24 * 2**20),
        cost_estimate=CHEAP,
    )(*blocks)


def weight_kernel(inputs_t, hidden, out):
    out[...] = jnp.dot(inputs_t[...], hidden[...], preferred_element_type=F32).astype(BF)


def weight_cotangent(inputs_t, hidden, tile=512):
    wide, tokens = inputs_t.shape
    units = hidden.shape[1]
    return pl.pallas_call(
        weight_kernel,
        grid=(units // tile,),
        out_shape=jax.ShapeDtypeStruct((wide, units), BF),
        in_specs=[WHOLE, pl.BlockSpec((tokens, tile), lambda i: (0, i))],
        out_specs=pl.BlockSpec((wide, tile), lambda i: (0, i)),
        compiler_params=pltpu.CompilerParams(vmem_limit_bytes=30 * 2**20),
        cost_estimate=CHEAP,
    )(inputs_t, pltpu.with_memory_space_constraint(hidden, pltpu.HBM))


def on_device(inputs, pre_act, grad_out, weight):
    hop0 = hidden_cotangent(pre_act, grad_out).reshape(2, -1, pre_act.shape[1])
    hop1 = ring(hop0)
    held_weight = fetch(after(weight, hop0))
    beside = [inputs] + [near(inputs, -k) for k in (1, 2, 3)]

    hop1, held_weight, *beside = lax.optimization_barrier((hop1, held_weight, *beside))
    hop2 = ring(hop1)
    stacked = jnp.stack(beside)
    gathered = {0: stacked, 1: far(stacked, -1), 3: far(stacked, -3)}
    blocks = [hop0, swap_core(hop0), hop1, swap_core(hop1)]

    hop2, stacked, gathered[1], gathered[3], *blocks = lax.optimization_barrier(
        (hop2, stacked, gathered[1], gathered[3], *blocks)
    )
    hop3 = ring(hop2)
    gathered[2] = far(stacked, -2)
    store, outs = partial_input((0, 1, 2), [*blocks, hop2, swap_core(hop2)], held_weight, None, None)

    hop3, gathered[2], *outs = lax.optimization_barrier((hop3, gathered[2], *outs))
    store, outs = partial_input((3,), [hop3, swap_core(hop3)], held_weight, store, outs)
    terms = [outs[0]] + [near(outs[k], k) for k in (1, 2, 3)]

    inputs_t = transposed_inputs([gathered[k] for k in range(SIDE)])
    grad_weight = weight_cotangent(inputs_t, store.reshape(-1, store.shape[-1]))
    grad_weight, *terms = lax.optimization_barrier((grad_weight, *terms))
    sums = sum_terms(terms)
    grad_input = last_sum([sums[0]] + [far(sums[k], k) for k in (1, 2, 3)])
    return (grad_input, grad_weight)


def solution(mesh):
    return jax.shard_map(
        on_device,
        mesh=mesh,
        in_specs=(P("row", "col"), P("col", "row"), P("col", "row"), P("col", "row")),
        out_specs=(P("row", "col"), P("col", "row")),
        check_vma=False,
    )
```

time: 190 us -> 92.7 us (0.49)
  waiting for transfers between devices: 129 us -> 26.3 us
  Pallas kernels: 0 us -> 35 us
  matrix products: 30.8 us -> 0 us
  starting transfers between devices: 0.12 us -> 25.7 us
  between operations: 13.7 us -> 0.72 us
  local copies, waits for them, and re-layouts: 12.6 us -> 1.21 us
    all_gather x2 -> x0, waiting for transfers between devices: 77.5 us -> none  [the longest x1 42.7 us: on_device(): grad_hidden = lax.all_gather(local_grad, 'col', axis=0, tiled=True)]
    reduce_scatter x1 -> x0, waiting for transfers between devices: 50.8 us -> none  [on_device(): lax.psum_scatter(partial_input.astype(jnp.bfloat16), 'row', scatter_dimen...]
    pallas_call x0 -> x6, Pallas kernels: none -> 35 us  [the longest x2 15 us: partial_input(): pl.pallas_call(functools.partial(partial_kernel, hops, bool(given)), out_...]
    dot_general x2 -> x0, matrix products: 30.8 us -> none  [the longest x1 15.6 us: on_device(): lax.dot_general(grad_hidden, weight, (((1,), (1,)), ((), ())), preferred_...]
    ppermute x0 -> x19, waiting for transfers between devices: none -> 26.3 us  [move(): return lax.ppermute(array, ('row', 'col'), pairs)]
    ppermute x0 -> x19, starting transfers between devices: none -> 25.7 us  [move(): return lax.ppermute(array, ('row', 'col'), pairs)]
    unnamed x1 -> x10, local copies, waits for them, and re-layouts: 12.6 us -> 1.21 us
  transfers between devices with their start and end apart: 3 -> 19, of which waited for: 3 -> 13; matrix products, arithmetic and copies ran while one was open for 23% -> 0% of each run, Pallas kernels for 0% -> 31%
where the time goes in v1:
time: 92.7 us; the launch traced here: 92.4 us
  Pallas kernels  35 us (38%)
  waiting for transfers between devices  26.3 us (28%)
  starting transfers between devices  25.7 us (28%)
  other arithmetic  3.38 us (4%)
  local copies, waits for them, and re-layouts  1.21 us (1%)
    ppermute x19, waiting for transfers between devices, move(): return lax.ppermute(array, ('row', 'col'), pairs)  26.3 us
    ppermute x19, starting transfers between devices, move(): return lax.ppermute(array, ('row', 'col'), pairs)  25.7 us
    pallas_call x2, Pallas kernels, partial_input(): pl.pallas_call(functools.partial(partial_kernel, hops, bool(given)), out_...  15 us
    pallas_call x1, Pallas kernels, weight_cotangent(): pl.pallas_call(weight_kernel, grid=(units // tile,), out_shape=jax.ShapeD...  13.2 us
    pallas_call x1, Pallas kernels, fetch(): pl.pallas_call(fetch_kernel, out_shape=pltpu.VMEM(array.shape, array.dtyp...  3.69 us
    convert_element_type x1, other arithmetic, hidden_cotangent(): (out_values.astype(F32) * gelu_slope(pre_values.astype(F32))).astype(BF)  2.5 us
    pallas_call x1, Pallas kernels, sum_terms(): pl.pallas_call(sum_kernel, out_shape=[pltpu.VMEM(shape[1:], BF)] * shape[...  2.23 us
  transfers between devices with their start and end apart: 19, of which 13 were waited for; matrix products, arithmetic and copies ran while one was open for 0% of the time, Pallas kernels for 31%

profile of v1, /device:TPU:0, one launch (start us, length us, event | category | flops | bytes accessed | tf_op | source)
XLA Modules:
  0.0 92.4 jit_solution(14837741929782361734)
XLA Ops:
  0.6 2.5 %fusion.7 = bf16[128,3072]{1,0:T(8,128)(2,1)S(1)} fusion(bf16[128,3072]{1,0:T(8,128)(2,1)} %param.5, bf16[128,3072]{1,0:T(8,128)(2,1)} %param.6), kind=kLoop, calls=%fused_computation.14 | loop fusion | flops 8257536 | bytes 2359296 | tf_op jit(solution)/shard_map/convert_element_type | solution.py:29
  3.1 1.7 %collective-permute-start = (bf16[2,64,3072]{2,1,0:T(8,128)(2,1)S(1)}, bf16[2,64,3072]{2,1,0:T(8,128)(2,1)S(1)}, u32[]{:S(2)}, u32[]{:S(2)}) collective-permute-start(bf16[2,64,3072]{2,1,0:T(8,128)(2,1)S(1)} %bitcast.6), channel_id=1, source_target_pairs={{0,2},{1,7},{2,4},{3,1},{4,6},{5,3},{6,0},{7,5},{8,10},{9,15},{10,... | collective-permute-start | bytes 2359304 | tf_op jit(solution)/shard_map/ppermute | solution.py:41
  4.9 3.9 %collective-permute-start.2 = (bf16[64,1536]{1,0:T(8,128)(2,1)S(1)}, bf16[64,1536]{1,0:T(8,128)(2,1)S(1)}, u32[]{:S(2)}, u32[]{:S(2)}) collective-permute-start(bf16[64,1536]{1,0:T(8,128)(2,1)S(1)} %copy-done.4), channel_id=1, source_target_pairs={{0,16},{1,65},{2,18},{3,67},{4,20},{5,69},{6,22},{7,71},{8,24},{9,... | collective-permute-start | bytes 589832 | tf_op jit(solution)/shard_map/ppermute | solution.py:41
  8.8 0.7 collective-permute-start.1
  9.5 1.3 %collective-permute-start.3 = (bf16[64,1536]{1,0:T(8,128)(2,1)S(1)}, bf16[64,1536]{1,0:T(8,128)(2,1)S(1)}, u32[]{:S(2)}, u32[]{:S(2)}) collective-permute-start(bf16[64,1536]{1,0:T(8,128)(2,1)S(1)} %copy-done.4), channel_id=1, source_target_pairs={{0,8},{1,33},{2,10},{3,35},{4,12},{5,37},{6,14},{7,39},{8,16},{9,4... | collective-permute-start | bytes 589832 | tf_op jit(solution)/shard_map/ppermute | solution.py:41
  10.8 3.7 %shard_map.59.refs_6_.refs_2_ = bf16[1536,3072]{1,0:T(8,128)(2,1)S(1)} custom-call(bf16[1536,3072]{1,0:T(8,128)(2,1)} %source), custom_call_target="tpu_custom_call" | custom-call | flops 1 | bytes 1 | tf_op jit(solution)/shard_map/pallas_call | solution.py:71
  14.5 1.1 %collective-permute-done.1 = bf16[64,1536]{1,0:T(8,128)(2,1)S(1)} collective-permute-done((bf16[64,1536]{1,0:T(8,128)(2,1)S(1)}, bf16[64,1536]{1,0:T(8,128)(2,1)S(1)}, u32[]{:S(2)}, u32[]{:S(2)}) %collective-permute-start.1) | collective-permute-done | bytes 196640 | tf_op jit(solution)/shard_map/ppermute | solution.py:41
  15.6 0.8 collective-permute-done.3
  16.5 1.6 %collective-permute-start.6 = (bf16[4,64,1536]{2,1,0:T(8,128)(2,1)S(1)}, bf16[4,64,1536]{2,1,0:T(8,128)(2,1)S(1)}, u32[]{:S(2)}, u32[]{:S(2)}) collective-permute-start(bf16[4,64,1536]{2,1,0:T(8,128)(2,1)S(1)} %pad_maximum_fusion.refs_0_), channel_id=1, source_target_pairs={{0,32},{1,9},{2,34},{3,11},{4,36},{5,13},{6,38},{7,15},{8,40},{9,1... | collective-permute-start | bytes 2359304 | tf_op jit(solution)/shard_map/ppermute | solution.py:41
  18.2 1.7 %collective-permute-start.5 = (bf16[4,64,1536]{2,1,0:T(8,128)(2,1)S(1)}, bf16[4,64,1536]{2,1,0:T(8,128)(2,1)S(1)}, u32[]{:S(2)}, u32[]{:S(2)}) collective-permute-start(bf16[4,64,1536]{2,1,0:T(8,128)(2,1)S(1)} %pad_maximum_fusion.refs_0_), channel_id=1, source_target_pairs={{0,96},{1,25},{2,98},{3,27},{4,100},{5,29},{6,102},{7,31},{8,104},... | collective-permute-start | bytes 2359304 | tf_op jit(solution)/shard_map/ppermute | solution.py:41
  19.8 1.5 %collective-permute-start.4 = (bf16[2,64,3072]{2,1,0:T(8,128)(2,1)S(1)}, bf16[2,64,3072]{2,1,0:T(8,128)(2,1)S(1)}, u32[]{:S(2)}, u32[]{:S(2)}) collective-permute-start(bf16[2,64,3072]{2,1,0:T(8,128)(2,1)S(1)} %collective-permute-done.refs_2_), channel_id=1, source_target_pairs={{0,2},{1,7},{2,4},{3,1},{4,6},{5,3},{6,0},{7,5},{8,10},{9,15},{10,... | collective-permute-start | bytes 2359304 | tf_op jit(solution)/shard_map/ppermute | solution.py:41
  21.3 8.4 %collective-permute-done.6.refs_3_ = bf16[4,64,1536]{2,1,0:T(8,128)(2,1)S(1)} collective-permute-done((bf16[4,64,1536]{2,1,0:T(8,128)(2,1)S(1)}, bf16[4,64,1536]{2,1,0:T(8,128)(2,1)S(1)}, u32[]{:S(2)}, u32[]{:S(2)}) %collective-permute-start.6) | collective-permute-done | bytes 786464 | tf_op jit(solution)/shard_map/ppermute | solution.py:41
  30.2 2.9 %collective-permute-done.4.refs_4_ = bf16[2,64,3072]{2,1,0:T(8,128)(2,1)S(1)} collective-permute-done((bf16[2,64,3072]{2,1,0:T(8,128)(2,1)S(1)}, bf16[2,64,3072]{2,1,0:T(8,128)(2,1)S(1)}, u32[]{:S(2)}, u32[]{:S(2)}) %collective-permute-start.4) | collective-permute-done | bytes 786464 | tf_op jit(solution)/shard_map/ppermute | solution.py:41
  33.0 2.2 %collective-permute-start.10 = (bf16[4,64,1536]{2,1,0:T(8,128)(2,1)S(1)}, bf16[4,64,1536]{2,1,0:T(8,128)(2,1)S(1)}, u32[]{:S(2)}, u32[]{:S(2)}) collective-permute-start(bf16[4,64,1536]{2,1,0:T(8,128)(2,1)S(1)} %pad_maximum_fusion.refs_0_), channel_id=1, source_target_pairs={{0,64},{1,17},{2,66},{3,19},{4,68},{5,21},{6,70},{7,23},{8,72},{9,... | collective-permute-start | bytes 2359304 | tf_op jit(solution)/shard_map/ppermute | solution.py:41
  35.3 11.1 %shard_map.60 = (bf16[4,4,64,3072]{3,2,1,0:T(8,128)(2,1)}, bf16[4,64,1536]{2,1,0:T(8,128)(2,1)S(1)}, bf16[4,64,1536]{2,1,0:T(8,128)(2,1)S(1)}, bf16[4,64,1536]{2,1,0:T(8,128)(2,1)S(1)}, bf16[4,64,1536]{2,1,0:T(8,128)(2,1)S(1)}) custom-call(bf16[2,64,3072]{2,1,0:T(8,128)(2,1)S(1)} %bitcast.8, bf16[2,64,3072]{2,1,0:T(8,128)(2,1)S(1)} %collective-permute-done.7.refs_1_, ...), custom_call_target="tpu_custom_call" | custom-call | flops 1 | bytes 1 | tf_op jit(solution)/shard_map/pallas_call | solution.py:127
  46.5 1.9 %collective-permute-done.9.refs_0_ = bf16[2,64,3072]{2,1,0:T(8,128)(2,1)S(1)} collective-permute-done((bf16[2,64,3072]{2,1,0:T(8,128)(2,1)S(1)}, bf16[2,64,3072]{2,1,0:T(8,128)(2,1)S(1)}, u32[]{:S(2)}, u32[]{:S(2)}) %collective-permute-start.9) | collective-permute-done | bytes 786464 | tf_op jit(solution)/shard_map/ppermute | solution.py:41
  48.8 1.9 %collective-permute-done.12.refs_1_ = bf16[2,64,3072]{2,1,0:T(8,128)(2,1)S(1)} collective-permute-done((bf16[2,64,3072]{2,1,0:T(8,128)(2,1)S(1)}, bf16[2,64,3072]{2,1,0:T(8,128)(2,1)S(1)}, u32[]{:S(2)}, u32[]{:S(2)}) %collective-permute-start.12) | collective-permute-done | bytes 786464 | tf_op jit(solution)/shard_map/ppermute | solution.py:41
  50.7 3.9 %shard_map.62 = (bf16[4,4,64,3072]{3,2,1,0:T(8,128)(2,1)}, bf16[4,64,1536]{2,1,0:T(8,128)(2,1)S(1)}, bf16[4,64,1536]{2,1,0:T(8,128)(2,1)S(1)}, bf16[4,64,1536]{2,1,0:T(8,128)(2,1)S(1)}, bf16[4,64,1536]{2,1,0:T(8,128)(2,1)S(1)}) custom-call(bf16[2,64,3072]{2,1,0:T(8,128)(2,1)S(1)} %collective-per, ...), custom_call_target="tpu_custom_call", output_to_operand_aliasing={{0}: (3, {}), {1}: (4, {}), {2}: (5, {}), {3}: (6, {}), {4}... | custom-call | flops 1 | bytes 1 | tf_op jit(solution)/shard_map/pallas_call | solution.py:127
  54.6 1.7 %collective-permute-start.13 = (bf16[4,64,1536]{2,1,0:T(8,128)(2,1)S(1)}, bf16[4,64,1536]{2,1,0:T(8,128)(2,1)S(1)}, u32[]{:S(2)}, u32[]{:S(2)}) collective-permute-start(bf16[4,64,1536]{2,1,0:T(8,128)(2,1)S(1)} %get-tuple-element.70), channel_id=1, source_target_pairs={{0,8},{1,33},{2,10},{3,35},{4,12},{5,37},{6,14},{7,39},{8,16},{9,4... | collective-permute-start | bytes 2359304 | tf_op jit(solution)/shard_map/ppermute | solution.py:41
  56.3 3.6 %collective-permute-start.14 = (bf16[4,64,1536]{2,1,0:T(8,128)(2,1)S(1)}, bf16[4,64,1536]{2,1,0:T(8,128)(2,1)S(1)}, u32[]{:S(2)}, u32[]{:S(2)}) collective-permute-start(bf16[4,64,1536]{2,1,0:T(8,128)(2,1)S(1)} %get-tuple-element.71), channel_id=1, source_target_pairs={{0,16},{1,65},{2,18},{3,67},{4,20},{5,69},{6,22},{7,71},{8,24},{9,... | collective-permute-start | bytes 2359304 | tf_op jit(solution)/shard_map/ppermute | solution.py:41
  59.9 1.0 %collective-permute-start.15 = (bf16[4,64,1536]{2,1,0:T(8,128)(2,1)S(1)}, bf16[4,64,1536]{2,1,0:T(8,128)(2,1)S(1)}, u32[]{:S(2)}, u32[]{:S(2)}) collective-permute-start(bf16[4,64,1536]{2,1,0:T(8,128)(2,1)S(1)} %get-tuple-element.72), channel_id=1, source_target_pairs={{0,24},{1,97},{2,26},{3,99},{4,28},{5,101},{6,30},{7,103},{8,0},{9... | collective-permute-start | bytes 2359304 | tf_op jit(solution)/shard_map/ppermute | solution.py:41
  60.9 0.9 %shard_map.61.inputs_t = bf16[1536,1024]{1,0:T(8,128)(2,1)S(1)} custom-call(bf16[4,64,1536]{2,1,0:T(8,128)(2,1)S(1)} %pad_maximum_fusion.refs_0_, bf16[4,64,1536]{2,1,0:T(8,128)(2,1)S(1)} %collective-permute-done.5.refs_1_, bf16[4,64,1536]{2,1,0:T(8,128)(2,1)S(1)} %collective-permute-done.10.refs_2_, bf16[4,64,1536]{2,1,0:T(8,128)(2,1)S(1)} %collective-permute-done.6.refs_3_), custom_call_target="tpu_custom_call" | custom-call | flops 1 | bytes 1 | tf_op jit(solution)/shard_map/pallas_call | solution.py:184
  61.8 13.2 %shard_map.63 = bf16[1536,3072]{1,0:T(8,128)(2,1)} custom-call(bf16[1536,1024]{1,0:T(8,128)(2,1)S(1)} %shard_map.61.inputs_t, bf16[1024,3072]{1,0:T(8,128)(2,1)} %bitcast.9), custom_call_target="tpu_custom_call" | custom-call | flops 1 | bytes 1 | tf_op jit(solution)/shard_map/pallas_call | solution.py:202
  75.0 3.2 %collective-permute-done.14.refs_2_ = bf16[4,64,1536]{2,1,0:T(8,128)(2,1)S(1)} collective-permute-done((bf16[4,64,1536]{2,1,0:T(8,128)(2,1)S(1)}, bf16[4,64,1536]{2,1,0:T(8,128)(2,1)S(1)}, u32[]{:S(2)}, u32[]{:S(2)}) %collective-permute-start.14) | collective-permute-done | bytes 786464 | tf_op jit(solution)/shard_map/ppermute | solution.py:41
  78.3 0.9 copy-done.3
  79.5 2.2 %shard_map.64 = (bf16[64,1536]{1,0:T(8,128)(2,1)S(1)}, bf16[64,1536]{1,0:T(8,128)(2,1)S(1)}, bf16[64,1536]{1,0:T(8,128)(2,1)S(1)}, bf16[64,1536]{1,0:T(8,128)(2,1)S(1)}) custom-call(bf16[4,64,1536]{2,1,0:T(8,128)(2,1)} %copy-done, bf16[4,64,1536]{2,1,0:T(8,128)(2,1)} %copy-done.1, bf16[4,64,1536]{2,1,0:T(8,128)(2,1)} %copy-done.2, bf16[4,64,1536]{2,1,0:T(8,128)(2,1)} %copy-done.3), custom_call_target="tpu_custom_call" | custom-call | flops 1 | bytes 1 | tf_op jit(solution)/shard_map/pallas_call | solution.py:155
  81.7 0.7 collective-permute-start.16
  82.4 2.0 %collective-permute-start.17 = (bf16[64,1536]{1,0:T(8,128)(2,1)S(1)}, bf16[64,1536]{1,0:T(8,128)(2,1)S(1)}, u32[]{:S(2)}, u32[]{:S(2)}) collective-permute-start(bf16[64,1536]{1,0:T(8,128)(2,1)S(1)} %get-tuple-element.79), channel_id=1, source_target_pairs={{0,64},{1,17},{2,66},{3,19},{4,68},{5,21},{6,70},{7,23},{8,72},{9,... | collective-permute-start | bytes 589832 | tf_op jit(solution)/shard_map/ppermute | solution.py:41
  84.4 1.8 %collective-permute-start.18 = (bf16[64,1536]{1,0:T(8,128)(2,1)S(1)}, bf16[64,1536]{1,0:T(8,128)(2,1)S(1)}, u32[]{:S(2)}, u32[]{:S(2)}) collective-permute-start(bf16[64,1536]{1,0:T(8,128)(2,1)S(1)} %get-tuple-element.80), channel_id=1, source_target_pairs={{0,96},{1,25},{2,98},{3,27},{4,100},{5,29},{6,102},{7,31},{8,104},... | collective-permute-start | bytes 589832 | tf_op jit(solution)/shard_map/ppermute | solution.py:41
  86.1 4.6 %collective-permute-done.16 = bf16[64,1536]{1,0:T(8,128)(2,1)S(1)} collective-permute-done((bf16[64,1536]{1,0:T(8,128)(2,1)S(1)}, bf16[64,1536]{1,0:T(8,128)(2,1)S(1)}, u32[]{:S(2)}, u32[]{:S(2)}) %collective-permute-start.16) | collective-permute-done | bytes 196640 | tf_op jit(solution)/shard_map/ppermute | solution.py:41
  90.7 0.9 collective-permute-done.18
  91.6 0.8 add_convert_fusion
  (25 shorter events, 1.5 us)
Async XLA Ops:
  0.6 4.2 %copy-start.4 = (bf16[64,1536]{1,0:T(8,128)(2,1)S(1)}, bf16[64,1536]{1,0:T(8,128)(2,1)}, u32[]{:S(2)}) copy-start(bf16[64,1536]{1,0:T(8,128)(2,1)} %param.4) | copy-start | bytes 589828
  3.1 13.3 %collective-permute-start = (bf16[2,64,3072]{2,1,0:T(8,128)(2,1)S(1)}, bf16[2,64,3072]{2,1,0:T(8,128)(2,1)S(1)}, u32[]{:S(2)}, u32[]{:S(2)}) collective-permute-start(bf16[2,64,3072]{2,1,0:T(8,128)(2,1)S(1)} %bitcast.6), channel_id=1, source_target_pairs={{0,2},{1,7},{2,4},{3,1},{4,6},{5,3},{6,0},{7,5},{8,10},{9,15},{10,... | collective-permute-start | bytes 2359304 | tf_op jit(solution)/shard_map/ppermute | solution.py:41
  4.9 9.6 %collective-permute-start.2 = (bf16[64,1536]{1,0:T(8,128)(2,1)S(1)}, bf16[64,1536]{1,0:T(8,128)(2,1)S(1)}, u32[]{:S(2)}, u32[]{:S(2)}) collective-permute-start(bf16[64,1536]{1,0:T(8,128)(2,1)S(1)} %copy-done.4), channel_id=1, source_target_pairs={{0,16},{1,65},{2,18},{3,67},{4,20},{5,69},{6,22},{7,71},{8,24},{9,... | collective-permute-start | bytes 589832 | tf_op jit(solution)/shard_map/ppermute | solution.py:41
  8.8 6.8 %collective-permute-start.1 = (bf16[64,1536]{1,0:T(8,128)(2,1)S(1)}, bf16[64,1536]{1,0:T(8,128)(2,1)S(1)}, u32[]{:S(2)}, u32[]{:S(2)}) collective-permute-start(bf16[64,1536]{1,0:T(8,128)(2,1)S(1)} %copy-done.4), channel_id=1, source_target_pairs={{0,24},{1,97},{2,26},{3,99},{4,28},{5,101},{6,30},{7,103},{8,0},{9... | collective-permute-start | bytes 589832 | tf_op jit(solution)/shard_map/ppermute | solution.py:41
  9.5 6.9 %collective-permute-start.3 = (bf16[64,1536]{1,0:T(8,128)(2,1)S(1)}, bf16[64,1536]{1,0:T(8,128)(2,1)S(1)}, u32[]{:S(2)}, u32[]{:S(2)}) collective-permute-start(bf16[64,1536]{1,0:T(8,128)(2,1)S(1)} %copy-done.4), channel_id=1, source_target_pairs={{0,8},{1,33},{2,10},{3,35},{4,12},{5,37},{6,14},{7,39},{8,16},{9,4... | collective-permute-start | bytes 589832 | tf_op jit(solution)/shard_map/ppermute | solution.py:41
  10.8 10.6 %collective-permute-start.7 = (bf16[2,64,3072]{2,1,0:T(8,128)(2,1)S(1)}, bf16[2,64,3072]{2,1,0:T(8,128)(2,1)S(1)}, u32[]{:S(2)}, u32[]{:S(2)}) collective-permute-start(bf16[2,64,3072]{2,1,0:T(8,128)(2,1)S(1)} %bitcast.7), channel_id=1, source_target_pairs={{0,1},{1,0},{2,3},{3,2},{4,5},{5,4},{6,7},{7,6},{8,9},{9,8},{10,11... | collective-permute-start | bytes 2359304 | tf_op jit(solution)/shard_map/ppermute | solution.py:41
  16.5 13.3 %collective-permute-start.6 = (bf16[4,64,1536]{2,1,0:T(8,128)(2,1)S(1)}, bf16[4,64,1536]{2,1,0:T(8,128)(2,1)S(1)}, u32[]{:S(2)}, u32[]{:S(2)}) collective-permute-start(bf16[4,64,1536]{2,1,0:T(8,128)(2,1)S(1)} %pad_maximum_fusion.refs_0_), channel_id=1, source_target_pairs={{0,32},{1,9},{2,34},{3,11},{4,36},{5,13},{6,38},{7,15},{8,40},{9,1... | collective-permute-start | bytes 2359304 | tf_op jit(solution)/shard_map/ppermute | solution.py:41
  18.2 12.0 %collective-permute-start.5 = (bf16[4,64,1536]{2,1,0:T(8,128)(2,1)S(1)}, bf16[4,64,1536]{2,1,0:T(8,128)(2,1)S(1)}, u32[]{:S(2)}, u32[]{:S(2)}) collective-permute-start(bf16[4,64,1536]{2,1,0:T(8,128)(2,1)S(1)} %pad_maximum_fusion.refs_0_), channel_id=1, source_target_pairs={{0,96},{1,25},{2,98},{3,27},{4,100},{5,29},{6,102},{7,31},{8,104},... | collective-permute-start | bytes 2359304 | tf_op jit(solution)/shard_map/ppermute | solution.py:41
  19.8 10.3 %collective-permute-start.8 = (bf16[2,64,3072]{2,1,0:T(8,128)(2,1)S(1)}, bf16[2,64,3072]{2,1,0:T(8,128)(2,1)S(1)}, u32[]{:S(2)}, u32[]{:S(2)}) collective-permute-start(bf16[2,64,3072]{2,1,0:T(8,128)(2,1)S(1)} %collective-permute-done.refs_2_), channel_id=1, source_target_pairs={{0,1},{1,0},{2,3},{3,2},{4,5},{5,4},{6,7},{7,6},{8,9},{9,8},{10,11... | collective-permute-start | bytes 2359304 | tf_op jit(solution)/shard_map/ppermute | solution.py:41
  19.8 13.2 %collective-permute-start.4 = (bf16[2,64,3072]{2,1,0:T(8,128)(2,1)S(1)}, bf16[2,64,3072]{2,1,0:T(8,128)(2,1)S(1)}, u32[]{:S(2)}, u32[]{:S(2)}) collective-permute-start(bf16[2,64,3072]{2,1,0:T(8,128)(2,1)S(1)} %collective-permute-done.refs_2_), channel_id=1, source_target_pairs={{0,2},{1,7},{2,4},{3,1},{4,6},{5,3},{6,0},{7,5},{8,10},{9,15},{10,... | collective-permute-start | bytes 2359304 | tf_op jit(solution)/shard_map/ppermute | solution.py:41
  33.0 2.3 %collective-permute-start.11 = (bf16[2,64,3072]{2,1,0:T(8,128)(2,1)S(1)}, bf16[2,64,3072]{2,1,0:T(8,128)(2,1)S(1)}, u32[]{:S(2)}, u32[]{:S(2)}) collective-permute-start(bf16[2,64,3072]{2,1,0:T(8,128)(2,1)S(1)} %collective-permute-done.4.refs_4_), channel_id=1, source_target_pairs={{0,1},{1,0},{2,3},{3,2},{4,5},{5,4},{6,7},{7,6},{8,9},{9,8},{10,11... | collective-permute-start | bytes 2359304 | tf_op jit(solution)/shard_map/ppermute | solution.py:41
  33.0 13.5 %collective-permute-start.10 = (bf16[4,64,1536]{2,1,0:T(8,128)(2,1)S(1)}, bf16[4,64,1536]{2,1,0:T(8,128)(2,1)S(1)}, u32[]{:S(2)}, u32[]{:S(2)}) collective-permute-start(bf16[4,64,1536]{2,1,0:T(8,128)(2,1)S(1)} %pad_maximum_fusion.refs_0_), channel_id=1, source_target_pairs={{0,64},{1,17},{2,66},{3,19},{4,68},{5,21},{6,70},{7,23},{8,72},{9,... | collective-permute-start | bytes 2359304 | tf_op jit(solution)/shard_map/ppermute | solution.py:41
  35.2 13.2 %collective-permute-start.9 = (bf16[2,64,3072]{2,1,0:T(8,128)(2,1)S(1)}, bf16[2,64,3072]{2,1,0:T(8,128)(2,1)S(1)}, u32[]{:S(2)}, u32[]{:S(2)}) collective-permute-start(bf16[2,64,3072]{2,1,0:T(8,128)(2,1)S(1)} %collective-permute-done.4.refs_4_), channel_id=1, source_target_pairs={{0,2},{1,7},{2,4},{3,1},{4,6},{5,3},{6,0},{7,5},{8,10},{9,15},{10,... | collective-permute-start | bytes 2359304 | tf_op jit(solution)/shard_map/ppermute | solution.py:41
  48.4 2.3 %collective-permute-start.12 = (bf16[2,64,3072]{2,1,0:T(8,128)(2,1)S(1)}, bf16[2,64,3072]{2,1,0:T(8,128)(2,1)S(1)}, u32[]{:S(2)}, u32[]{:S(2)}) collective-permute-start(bf16[2,64,3072]{2,1,0:T(8,128)(2,1)S(1)} %collective-permute-done.9.refs_0_), channel_id=1, source_target_pairs={{0,1},{1,0},{2,3},{3,2},{4,5},{5,4},{6,7},{7,6},{8,9},{9,8},{10,11... | collective-permute-start | bytes 2359304 | tf_op jit(solution)/shard_map/ppermute | solution.py:41
  54.6 7.2 %copy-start = (bf16[4,64,1536]{2,1,0:T(8,128)(2,1)}, bf16[4,64,1536]{2,1,0:T(8,128)(2,1)S(1)}, u32[]{:S(2)}) copy-start(bf16[4,64,1536]{2,1,0:T(8,128)(2,1)S(1)} %get-tuple-element.73.refs_0_) | copy-start | bytes 2359300
  54.6 20.4 %collective-permute-start.13 = (bf16[4,64,1536]{2,1,0:T(8,128)(2,1)S(1)}, bf16[4,64,1536]{2,1,0:T(8,128)(2,1)S(1)}, u32[]{:S(2)}, u32[]{:S(2)}) collective-permute-start(bf16[4,64,1536]{2,1,0:T(8,128)(2,1)S(1)} %get-tuple-element.70), channel_id=1, source_target_pairs={{0,8},{1,33},{2,10},{3,35},{4,12},{5,37},{6,14},{7,39},{8,16},{9,4... | collective-permute-start | bytes 2359304 | tf_op jit(solution)/shard_map/ppermute | solution.py:41
  56.3 22.0 %collective-permute-start.14 = (bf16[4,64,1536]{2,1,0:T(8,128)(2,1)S(1)}, bf16[4,64,1536]{2,1,0:T(8,128)(2,1)S(1)}, u32[]{:S(2)}, u32[]{:S(2)}) collective-permute-start(bf16[4,64,1536]{2,1,0:T(8,128)(2,1)S(1)} %get-tuple-element.71), channel_id=1, source_target_pairs={{0,16},{1,65},{2,18},{3,67},{4,20},{5,69},{6,22},{7,71},{8,24},{9,... | collective-permute-start | bytes 2359304 | tf_op jit(solution)/shard_map/ppermute | solution.py:41
  59.9 18.4 %collective-permute-start.15 = (bf16[4,64,1536]{2,1,0:T(8,128)(2,1)S(1)}, bf16[4,64,1536]{2,1,0:T(8,128)(2,1)S(1)}, u32[]{:S(2)}, u32[]{:S(2)}) collective-permute-start(bf16[4,64,1536]{2,1,0:T(8,128)(2,1)S(1)} %get-tuple-element.72), channel_id=1, source_target_pairs={{0,24},{1,97},{2,26},{3,99},{4,28},{5,101},{6,30},{7,103},{8,0},{9... | collective-permute-start | bytes 2359304 | tf_op jit(solution)/shard_map/ppermute | solution.py:41
  75.0 4.1 %copy-start.1 = (bf16[4,64,1536]{2,1,0:T(8,128)(2,1)}, bf16[4,64,1536]{2,1,0:T(8,128)(2,1)S(1)}, u32[]{:S(2)}) copy-start(bf16[4,64,1536]{2,1,0:T(8,128)(2,1)S(1)} %collective-permute-done.13.refs_1_) | copy-start | bytes 2359300
  78.3 1.2 %copy-start.2 = (bf16[4,64,1536]{2,1,0:T(8,128)(2,1)}, bf16[4,64,1536]{2,1,0:T(8,128)(2,1)S(1)}, u32[]{:S(2)}) copy-start(bf16[4,64,1536]{2,1,0:T(8,128)(2,1)S(1)} %collective-permute-done.14.refs_2_) | copy-start | bytes 2359300
  78.3 0.9 copy-start.3
  81.7 9.1 %collective-permute-start.16 = (bf16[64,1536]{1,0:T(8,128)(2,1)S(1)}, bf16[64,1536]{1,0:T(8,128)(2,1)S(1)}, u32[]{:S(2)}, u32[]{:S(2)}) collective-permute-start(bf16[64,1536]{1,0:T(8,128)(2,1)S(1)} %get-tuple-element.78), channel_id=1, source_target_pairs={{0,32},{1,9},{2,34},{3,11},{4,36},{5,13},{6,38},{7,15},{8,40},{9,1... | collective-permute-start | bytes 589832 | tf_op jit(solution)/shard_map/ppermute | solution.py:41
  82.4 8.4 %collective-permute-start.17 = (bf16[64,1536]{1,0:T(8,128)(2,1)S(1)}, bf16[64,1536]{1,0:T(8,128)(2,1)S(1)}, u32[]{:S(2)}, u32[]{:S(2)}) collective-permute-start(bf16[64,1536]{1,0:T(8,128)(2,1)S(1)} %get-tuple-element.79), channel_id=1, source_target_pairs={{0,64},{1,17},{2,66},{3,19},{4,68},{5,21},{6,70},{7,23},{8,72},{9,... | collective-permute-start | bytes 589832 | tf_op jit(solution)/shard_map/ppermute | solution.py:41
  84.4 7.2 %collective-permute-start.18 = (bf16[64,1536]{1,0:T(8,128)(2,1)S(1)}, bf16[64,1536]{1,0:T(8,128)(2,1)S(1)}, u32[]{:S(2)}, u32[]{:S(2)}) collective-permute-start(bf16[64,1536]{1,0:T(8,128)(2,1)S(1)} %get-tuple-element.80), channel_id=1, source_target_pairs={{0,96},{1,25},{2,98},{3,27},{4,100},{5,29},{6,102},{7,31},{8,104},... | collective-permute-start | bytes 589832 | tf_op jit(solution)/shard_map/ppermute | solution.py:41

commit v2 on v1

v2 whole, which is shorter than its diff:
```python
import functools

import jax
import jax.numpy as jnp
from jax import lax
from jax.experimental import pallas as pl
from jax.experimental.pallas import tpu as pltpu
from jax.sharding import PartitionSpec as P

BF = jnp.bfloat16
F32 = jnp.float32
SIDE = 4
TILE = 768
WHOLE = pl.BlockSpec(memory_space=pltpu.VMEM)
FAR = pl.BlockSpec(memory_space=pltpu.HBM)
CHEAP = pl.CostEstimate(flops=1, bytes_accessed=1, transcendentals=0)


def gelu_slope(value):
    coeff = 0.7978845608
    square = value * value
    tanh_u = jnp.tanh(value * (coeff + (coeff * 0.044715) * square))
    slope = value * (coeff + (3.0 * 0.044715 * coeff) * square)
    return (0.5 + 0.5 * tanh_u) * (1.0 + (1.0 - tanh_u) * slope)


def hidden_cotangent(pre_values, out_values):
    return (out_values.astype(F32) * gelu_slope(pre_values.astype(F32))).astype(BF)


def move(array, step):
    pairs = []
    for x in range(SIDE):
        for z in range(SIDE):
            for y in range(SIDE):
                for c in range(2):
                    to_x, to_y, to_z, to_c = step(x, y, z, c)
                    to = ((to_x % SIDE * SIDE + to_z % SIDE) * SIDE + to_y % SIDE) * 2 + to_c
                    pairs.append((((x * SIDE + z) * SIDE + y) * 2 + c, to))
    return lax.ppermute(array, ("row", "col"), pairs)


def ring(array, by=1):
    return move(array, lambda x, y, z, c: (x, y + by * (1 - 2 * c), z, c))


def swap_core(array):
    return move(array, lambda x, y, z, c: (x, y, z, 1 - c))


def near(array, by):
    return move(array, lambda x, y, z, c: (x + by * c, y, z + by * (1 - c), c))


def far(array, by):
    return move(array, lambda x, y, z, c: (x + by * (1 - c), y, z + by * c, c))


def after(value, *others):
    return lax.optimization_barrier((value, *others))[0]


def fetch_kernel(source, target, sem):
    copy = pltpu.make_async_copy(source, target, sem)
    copy.start()
    copy.wait()


def fetch(array):
    return pl.pallas_call(
        fetch_kernel,
        out_shape=pltpu.VMEM(array.shape, array.dtype),
        in_specs=[FAR],
        out_specs=WHOLE,
        scratch_shapes=[pltpu.SemaphoreType.DMA],
        compiler_params=pltpu.CompilerParams(vmem_limit_bytes=12 * 2**20),
        cost_estimate=CHEAP,
    )(pltpu.with_memory_space_constraint(array, pltpu.HBM))


def block_offset(hop, swapped, h):
    x, z = lax.axis_index("row") // SIDE, lax.axis_index("row") % SIDE
    y, c = lax.axis_index("col") // 2, lax.axis_index("col") % 2
    owner = 1 - c if swapped else c
    to_x, to_z = lax.rem(y + SIDE + jnp.where(owner == 0, -hop, hop), SIDE), 2 * owner + h
    x_off, z_off = lax.rem(to_x + SIDE - x, SIDE), lax.rem(to_z + SIDE - z, SIDE)
    return jnp.where(c == 0, z_off, x_off), jnp.where(c == 0, x_off, z_off)


def partial_kernel(keys, has_outs, *refs):
    blocks, weight = refs[: len(keys)], refs[len(keys)]
    outs, found = refs[-1 - SIDE : -1], refs[-1]
    tokens = outs[0].shape[1]
    hidden = jnp.concatenate([block[...].reshape(2 * tokens, -1) for block in blocks])
    for d in range(0, weight.shape[0], TILE):
        found[:, d : d + TILE] = lax.dot_general(
            hidden, weight[d : d + TILE, :], (((1,), (1,)), ((), ())), preferred_element_type=F32
        ).astype(BF)
    for i, key in enumerate(keys):
        for h in range(2):
            n_off, f_off = block_offset(*key, h)
            at = (2 * i + h) * tokens
            for k in range(SIDE):

                @pl.when(n_off == k)
                def _():
                    outs[k][f_off] = found[at : at + tokens, :]


def partial_input(keys, pieces, weight, outs):
    blocks = [pieces[key] for key in keys]
    tokens = blocks[0].shape[1]
    first = len(blocks) + 1
    return list(
        pl.pallas_call(
            functools.partial(partial_kernel, keys, bool(outs)),
            out_shape=[pltpu.VMEM((SIDE, tokens, weight.shape[0]), BF)] * SIDE,
            in_specs=[WHOLE] * (first + len(outs)),
            out_specs=[WHOLE] * SIDE,
            scratch_shapes=[pltpu.VMEM((2 * tokens * len(blocks), weight.shape[0]), BF)],
            input_output_aliases={first + i: i for i in range(len(outs))},
            compiler_params=pltpu.CompilerParams(vmem_limit_bytes=16 * 2**20),
            cost_estimate=CHEAP,
        )(*blocks, weight, *outs)
    )


def sum_kernel(*refs):
    terms, outs = refs[:SIDE], refs[SIDE:]
    for k in range(len(outs)):
        total = terms[0][k].astype(F32)
        for term in terms[1:]:
            total += term[k].astype(F32)
        outs[k][...] = total.astype(BF)


def sum_terms(terms):
    shape = terms[0].shape
    return pl.pallas_call(
        sum_kernel,
        out_shape=[pltpu.VMEM(shape[1:], BF)] * shape[0],
        in_specs=[WHOLE] * len(terms),
        out_specs=[WHOLE] * shape[0],
        compiler_params=pltpu.CompilerParams(vmem_limit_bytes=6 * 2**20),
        cost_estimate=CHEAP,
    )(*terms)


def last_sum(terms):
    total = terms[0].astype(F32)
    for term in terms[1:]:
        total += term.astype(F32)
    return total.astype(BF)


def transpose_kernel(keys, *refs):
    blocks, out, rows = refs[:SIDE], refs[SIDE], refs[SIDE + 1]
    tokens = blocks[0].shape[1]
    for i, key in enumerate(keys):
        for h in range(2):
            n_off, f_off = block_offset(*key, h)
            at = (2 * i + h) * tokens
            for k in range(SIDE):

                @pl.when(f_off == k)
                def _():
                    rows[at : at + tokens, :] = blocks[k][n_off]

    out[...] = rows[...].T


def transposed_inputs(keys, blocks):
    _, tokens, wide = blocks[0].shape
    tokens *= SIDE * SIDE
    return pl.pallas_call(
        functools.partial(transpose_kernel, keys),
        out_shape=pltpu.VMEM((wide, tokens), BF),
        in_specs=[WHOLE] * SIDE,
        out_specs=WHOLE,
        scratch_shapes=[pltpu.VMEM((tokens, wide), BF)],
        compiler_params=pltpu.CompilerParams(vmem_limit_bytes=16 * 2**20),
        cost_estimate=CHEAP,
    )(*blocks)


def weight_kernel(inputs_t, *refs):
    pieces, out = refs[:-1], refs[-1]
    tile = out.shape[1]
    columns = pl.ds(pl.multiple_of(pl.program_id(0) * tile, tile), tile)
    hidden = jnp.concatenate([piece[:, columns] for piece in pieces])
    out[...] = jnp.dot(inputs_t[...], hidden, preferred_element_type=F32).astype(BF)


def weight_cotangent(inputs_t, pieces, tile=512):
    wide, units = inputs_t.shape[0], pieces[0].shape[-1]
    pieces = [piece.reshape(-1, units) for piece in pieces]
    return pl.pallas_call(
        weight_kernel,
        grid=(units // tile,),
        out_shape=jax.ShapeDtypeStruct((wide, units), BF),
        in_specs=[WHOLE] * (1 + len(pieces)),
        out_specs=pl.BlockSpec((wide, tile), lambda i: (0, i)),
        compiler_params=pltpu.CompilerParams(vmem_limit_bytes=18 * 2**20),
        cost_estimate=CHEAP,
    )(inputs_t, *pieces)


def on_device(inputs, pre_act, grad_out, weight):
    barrier = lax.optimization_barrier
    hop0 = hidden_cotangent(pre_act, grad_out).reshape(2, -1, pre_act.shape[1])
    beside = [inputs] + [near(inputs, -k) for k in (1, 2, 3)]
    swap0 = swap_core(hop0)
    hop1 = ring(hop0)
    held_weight = fetch(after(weight, hop0))

    hop1, swap0, held_weight, *beside = barrier((hop1, swap0, held_weight, *beside))
    swap1 = swap_core(hop1)
    stacked = jnp.stack(beside)
    gathered = {0: stacked, 1: far(stacked, -1), 3: far(stacked, -3), 2: far(stacked, -2)}
    hop2 = ring(hop1)
    pieces = {(0, False): hop0, (0, True): swap0, (1, False): hop1}
    outs = partial_input([(0, False), (0, True)], pieces, held_weight, [])

    hop2, swap1, *outs = barrier((hop2, swap1, *outs))
    hop3 = ring(hop2)
    swap2 = swap_core(hop2)
    pieces |= {(1, True): swap1, (2, False): hop2}
    outs = partial_input([(1, False), (1, True)], pieces, held_weight, outs)

    hop3, swap2, gathered[1], gathered[3], *outs = barrier((hop3, swap2, gathered[1], gathered[3], *outs))
    swap3 = swap_core(hop3)
    pieces |= {(2, True): swap2, (3, False): hop3}
    outs = partial_input([(2, False), (2, True)], pieces, held_weight, outs)
    swap3, gathered[2], *outs = barrier((swap3, gathered[2], *outs))
    pieces |= {(3, True): swap3}
    outs = partial_input([(3, False), (3, True)], pieces, held_weight, outs)
    terms = [outs[0]] + [near(outs[k], k) for k in (1, 2, 3)]

    inputs_t = transposed_inputs(list(pieces), [gathered[k] for k in range(SIDE)])
    grad_weight = weight_cotangent(inputs_t, list(pieces.values()))
    grad_weight, *terms = barrier((grad_weight, *terms))
    sums = sum_terms(terms)
    grad_input = last_sum([sums[0]] + [far(sums[k], k) for k in (1, 2, 3)])
    return (grad_input, grad_weight)


def solution(mesh):
    return jax.shard_map(
        on_device,
        mesh=mesh,
        in_specs=(P("row", "col"), P("col", "row"), P("col", "row"), P("col", "row")),
        out_specs=(P("row", "col"), P("col", "row")),
        check_vma=False,
    )
```

time: 92.7 us -> 84 us (0.906)
  Pallas kernels: 35 us -> 28.6 us
  waiting for transfers between devices: 26.3 us -> 22.6 us
  starting transfers between devices: 25.7 us -> 28.4 us
  local copies, waits for them, and re-layouts: 1.21 us -> 0.01 us
    ppermute x19, waiting for transfers between devices: 26.3 us -> 22.6 us  [move(): return lax.ppermute(array, ('row', 'col'), pairs)]
    pallas_call x3 -> x5, Pallas kernels: 15.9 us -> 12.5 us  [the longest x4 11 us: partial_input(): pl.pallas_call(functools.partial(partial_kernel, keys, bool(outs)), out_s...]
    ppermute x19, starting transfers between devices: 25.7 us -> 28.4 us  [move(): return lax.ppermute(array, ('row', 'col'), pairs)]
    pallas_call x1, Pallas kernels: 2.23 us -> 0.38 us  [sum_terms(): pl.pallas_call(sum_kernel, out_shape=[pltpu.VMEM(shape[1:], BF)] * shape[...]
    pallas_call x1, Pallas kernels: 13.2 us -> 12 us  [weight_cotangent(): pl.pallas_call(weight_kernel, grid=(units // tile,), out_shape=jax.ShapeD...]
    unnamed x10 -> x2, local copies, waits for them, and re-layouts: 1.21 us -> 0.01 us
  transfers between devices with their start and end apart: 19 -> 19, of which waited for: 13 -> 8; matrix products, arithmetic and copies ran while one was open for 0% -> 0% of each run, Pallas kernels for 31% -> 30%
where the time goes in v2:
time: 84 us; the launch traced here: 83.5 us
  Pallas kernels  28.6 us (34%)
  starting transfers between devices  28.4 us (34%)
  waiting for transfers between devices  22.6 us (27%)
  other arithmetic  3.18 us (4%)
    ppermute x19, starting transfers between devices, move(): return lax.ppermute(array, ('row', 'col'), pairs)  28.4 us
    ppermute x19, waiting for transfers between devices, move(): return lax.ppermute(array, ('row', 'col'), pairs)  22.6 us
    pallas_call x1, Pallas kernels, weight_cotangent(): pl.pallas_call(weight_kernel, grid=(units // tile,), out_shape=jax.ShapeD...  12 us
    pallas_call x4, Pallas kernels, partial_input(): pl.pallas_call(functools.partial(partial_kernel, keys, bool(outs)), out_s...  11 us
    pallas_call x1, Pallas kernels, fetch(): pl.pallas_call(fetch_kernel, out_shape=pltpu.VMEM(array.shape, array.dtyp...  3.69 us
    convert_element_type x1, other arithmetic, hidden_cotangent(): (out_values.astype(F32) * gelu_slope(pre_values.astype(F32))).astype(BF)  2.3 us
  transfers between devices with their start and end apart: 19, of which 8 were waited for; matrix products, arithmetic and copies ran while one was open for 0% of the time, Pallas kernels for 30%

profile of v2, /device:TPU:0, one launch (start us, length us, event | category | flops | bytes accessed | tf_op | source)
XLA Modules:
  0.0 83.5 jit_solution(6039285665099519053)
XLA Ops:
  0.6 2.3 %fusion.9.refs_0_ = bf16[128,3072]{1,0:T(8,128)(2,1)S(1)} fusion(bf16[128,3072]{1,0:T(8,128)(2,1)} %param.5, bf16[128,3072]{1,0:T(8,128)(2,1)} %param.6), kind=kLoop, calls=%fused_computation.12 | loop fusion | flops 6684672 | bytes 2359296 | tf_op jit(solution)/shard_map/convert_element_type | solution.py:28
  3.0 1.7 %collective-permute-start = (bf16[2,64,3072]{2,1,0:T(8,128)(2,1)S(1)}, bf16[2,64,3072]{2,1,0:T(8,128)(2,1)S(1)}, u32[]{:S(2)}, u32[]{:S(2)}) collective-permute-start(bf16[2,64,3072]{2,1,0:T(8,128)(2,1)S(1)} %bitcast.13), channel_id=1, source_target_pairs={{0,2},{1,7},{2,4},{3,1},{4,6},{5,3},{6,0},{7,5},{8,10},{9,15},{10,... | collective-permute-start | bytes 2359304 | tf_op jit(solution)/shard_map/ppermute | solution.py:40
  4.8 3.9 %collective-permute-start.3 = (bf16[64,1536]{1,0:T(8,128)(2,1)S(1)}, bf16[64,1536]{1,0:T(8,128)(2,1)S(1)}, u32[]{:S(2)}, u32[]{:S(2)}) collective-permute-start(bf16[64,1536]{1,0:T(8,128)(2,1)S(1)} %copy-done), channel_id=1, source_target_pairs={{0,16},{1,65},{2,18},{3,67},{4,20},{5,69},{6,22},{7,71},{8,24},{9,... | collective-permute-start | bytes 589832 | tf_op jit(solution)/shard_map/ppermute | solution.py:40
  8.6 0.7 collective-permute-start.2
  9.4 1.3 %collective-permute-start.4 = (bf16[64,1536]{1,0:T(8,128)(2,1)S(1)}, bf16[64,1536]{1,0:T(8,128)(2,1)S(1)}, u32[]{:S(2)}, u32[]{:S(2)}) collective-permute-start(bf16[64,1536]{1,0:T(8,128)(2,1)S(1)} %copy-done), channel_id=1, source_target_pairs={{0,8},{1,33},{2,10},{3,35},{4,12},{5,37},{6,14},{7,39},{8,16},{9,4... | collective-permute-start | bytes 589832 | tf_op jit(solution)/shard_map/ppermute | solution.py:40
  10.7 3.7 %shard_map.59.refs_2_ = bf16[1536,3072]{1,0:T(8,128)(2,1)S(1)} custom-call(bf16[1536,3072]{1,0:T(8,128)(2,1)} %source), custom_call_target="tpu_custom_call" | custom-call | flops 1 | bytes 1 | tf_op jit(solution)/shard_map/pallas_call | solution.py:70
  14.4 1.1 %collective-permute-done.2 = bf16[64,1536]{1,0:T(8,128)(2,1)S(1)} collective-permute-done((bf16[64,1536]{1,0:T(8,128)(2,1)S(1)}, bf16[64,1536]{1,0:T(8,128)(2,1)S(1)}, u32[]{:S(2)}, u32[]{:S(2)}) %collective-permute-start.2) | collective-permute-done | bytes 196640 | tf_op jit(solution)/shard_map/ppermute | solution.py:40
  15.5 0.8 collective-permute-done.4
  16.3 1.6 %collective-permute-start.5 = (bf16[2,64,3072]{2,1,0:T(8,128)(2,1)S(1)}, bf16[2,64,3072]{2,1,0:T(8,128)(2,1)S(1)}, u32[]{:S(2)}, u32[]{:S(2)}) collective-permute-start(bf16[2,64,3072]{2,1,0:T(8,128)(2,1)S(1)} %collective-permute-done.refs_0_), channel_id=1, source_target_pairs={{0,2},{1,7},{2,4},{3,1},{4,6},{5,3},{6,0},{7,5},{8,10},{9,15},{10,... | collective-permute-start | bytes 2359304 | tf_op jit(solution)/shard_map/ppermute | solution.py:40
  18.0 1.6 %collective-permute-start.10 = (bf16[4,64,1536]{2,1,0:T(8,128)(2,1)S(1)}, bf16[4,64,1536]{2,1,0:T(8,128)(2,1)S(1)}, u32[]{:S(2)}, u32[]{:S(2)}) collective-permute-start(bf16[4,64,1536]{2,1,0:T(8,128)(2,1)S(1)} %pad_maximum_fusion.refs_0_), channel_id=1, source_target_pairs={{0,32},{1,9},{2,34},{3,11},{4,36},{5,13},{6,38},{7,15},{8,40},{9,1... | collective-permute-start | bytes 2359304 | tf_op jit(solution)/shard_map/ppermute | solution.py:40
  19.6 1.7 %collective-permute-start.9 = (bf16[4,64,1536]{2,1,0:T(8,128)(2,1)S(1)}, bf16[4,64,1536]{2,1,0:T(8,128)(2,1)S(1)}, u32[]{:S(2)}, u32[]{:S(2)}) collective-permute-start(bf16[4,64,1536]{2,1,0:T(8,128)(2,1)S(1)} %pad_maximum_fusion.refs_0_), channel_id=1, source_target_pairs={{0,96},{1,25},{2,98},{3,27},{4,100},{5,29},{6,102},{7,31},{8,104},... | collective-permute-start | bytes 2359304 | tf_op jit(solution)/shard_map/ppermute | solution.py:40
  21.3 2.8 %shard_map.60 = (bf16[4,64,1536]{2,1,0:T(8,128)(2,1)S(1)}, bf16[4,64,1536]{2,1,0:T(8,128)(2,1)S(1)}, bf16[4,64,1536]{2,1,0:T(8,128)(2,1)S(1)}, bf16[4,64,1536]{2,1,0:T(8,128)(2,1)S(1)}) custom-call(bf16[2,64,3072]{2,1,0:T(8,128)(2,1)S(1)} %bitcast.14, bf16[2,64,3072]{2,1,0:T(8,128)(2,1)S(1)} %collective-permute-done.1.refs_1_, ...), custom_call_target="tpu_custom_call" | custom-call | flops 1 | bytes 1 | tf_op jit(solution)/shard_map/pallas_call | solution.py:115
  24.1 5.4 %collective-permute-done.5.refs_0_ = bf16[2,64,3072]{2,1,0:T(8,128)(2,1)S(1)} collective-permute-done((bf16[2,64,3072]{2,1,0:T(8,128)(2,1)S(1)}, bf16[2,64,3072]{2,1,0:T(8,128)(2,1)S(1)}, u32[]{:S(2)}, u32[]{:S(2)}) %collective-permute-start.5) | collective-permute-done | bytes 786464 | tf_op jit(solution)/shard_map/ppermute | solution.py:40
  29.5 0.4 collective-permute-start.7
  29.9 3.0 %collective-permute-start.12 = (bf16[4,64,1536]{2,1,0:T(8,128)(2,1)S(1)}, bf16[4,64,1536]{2,1,0:T(8,128)(2,1)S(1)}, u32[]{:S(2)}, u32[]{:S(2)}) collective-permute-start(bf16[4,64,1536]{2,1,0:T(8,128)(2,1)S(1)} %pad_maximum_fusion.refs_0_), channel_id=1, source_target_pairs={{0,64},{1,17},{2,66},{3,19},{4,68},{5,21},{6,70},{7,23},{8,72},{9,... | collective-permute-start | bytes 2359304 | tf_op jit(solution)/shard_map/ppermute | solution.py:40
  32.9 2.8 %shard_map.61 = (bf16[4,64,1536]{2,1,0:T(8,128)(2,1)S(1)}, bf16[4,64,1536]{2,1,0:T(8,128)(2,1)S(1)}, bf16[4,64,1536]{2,1,0:T(8,128)(2,1)S(1)}, bf16[4,64,1536]{2,1,0:T(8,128)(2,1)S(1)}) custom-call(bf16[2,64,3072]{2,1,0:T(8,128)(2,1)S(1)} %collective-permute-done.refs_0_, ...), custom_call_target="tpu_custom_call", output_to_operand_aliasing={{0}: (3, {}), {1}: (4, {}), {2}: (5, {}), {3}: (6, {})} | custom-call | flops 1 | bytes 1 | tf_op jit(solution)/shard_map/pallas_call | solution.py:115
  35.7 7.0 %collective-permute-done.7.refs_0_ = bf16[2,64,3072]{2,1,0:T(8,128)(2,1)S(1)} collective-permute-done((bf16[2,64,3072]{2,1,0:T(8,128)(2,1)S(1)}, bf16[2,64,3072]{2,1,0:T(8,128)(2,1)S(1)}, u32[]{:S(2)}, u32[]{:S(2)}) %collective-permute-start.7) | collective-permute-done | bytes 786464 | tf_op jit(solution)/shard_map/ppermute | solution.py:40
  42.7 2.8 %shard_map.62 = (bf16[4,64,1536]{2,1,0:T(8,128)(2,1)S(1)}, bf16[4,64,1536]{2,1,0:T(8,128)(2,1)S(1)}, bf16[4,64,1536]{2,1,0:T(8,128)(2,1)S(1)}, bf16[4,64,1536]{2,1,0:T(8,128)(2,1)S(1)}) custom-call(bf16[2,64,3072]{2,1,0:T(8,128)(2,1)S(1)} %collective-permute-done.5.refs_0_, ...), custom_call_target="tpu_custom_call", output_to_operand_aliasing={{0}: (3, {}), {1}: (4, {}), {2}: (5, {}), {3}: (6, {})} | custom-call | flops 1 | bytes 1 | tf_op jit(solution)/shard_map/pallas_call | solution.py:115
  45.5 2.8 %shard_map.65 = (bf16[4,64,1536]{2,1,0:T(8,128)(2,1)S(1)}, bf16[4,64,1536]{2,1,0:T(8,128)(2,1)S(1)}, bf16[4,64,1536]{2,1,0:T(8,128)(2,1)S(1)}, bf16[4,64,1536]{2,1,0:T(8,128)(2,1)S(1)}) custom-call(bf16[2,64,3072]{2,1,0:T(8,128)(2,1)S(1)} %collective-permute-done.7.refs_0_, ...), custom_call_target="tpu_custom_call", output_to_operand_aliasing={{0}: (3, {}), {1}: (4, {}), {2}: (5, {}), {3}: (6, {})} | custom-call | flops 1 | bytes 1 | tf_op jit(solution)/shard_map/pallas_call | solution.py:115
  48.3 2.1 %collective-permute-start.13 = (bf16[4,64,1536]{2,1,0:T(8,128)(2,1)S(1)}, bf16[4,64,1536]{2,1,0:T(8,128)(2,1)S(1)}, u32[]{:S(2)}, u32[]{:S(2)}) collective-permute-start(bf16[4,64,1536]{2,1,0:T(8,128)(2,1)S(1)} %get-tuple-element.96), channel_id=1, source_target_pairs={{0,8},{1,33},{2,10},{3,35},{4,12},{5,37},{6,14},{7,39},{8,16},{9,4... | collective-permute-start | bytes 2359304 | tf_op jit(solution)/shard_map/ppermute | solution.py:40
  50.4 3.6 %collective-permute-start.14 = (bf16[4,64,1536]{2,1,0:T(8,128)(2,1)S(1)}, bf16[4,64,1536]{2,1,0:T(8,128)(2,1)S(1)}, u32[]{:S(2)}, u32[]{:S(2)}) collective-permute-start(bf16[4,64,1536]{2,1,0:T(8,128)(2,1)S(1)} %get-tuple-element.97), channel_id=1, source_target_pairs={{0,16},{1,65},{2,18},{3,67},{4,20},{5,69},{6,22},{7,71},{8,24},{9,... | collective-permute-start | bytes 2359304 | tf_op jit(solution)/shard_map/ppermute | solution.py:40
  53.9 1.0 %collective-permute-start.15 = (bf16[4,64,1536]{2,1,0:T(8,128)(2,1)S(1)}, bf16[4,64,1536]{2,1,0:T(8,128)(2,1)S(1)}, u32[]{:S(2)}, u32[]{:S(2)}) collective-permute-start(bf16[4,64,1536]{2,1,0:T(8,128)(2,1)S(1)} %get-tuple-element.98), channel_id=1, source_target_pairs={{0,24},{1,97},{2,26},{3,99},{4,28},{5,101},{6,30},{7,103},{8,0},{9... | collective-permute-start | bytes 2359304 | tf_op jit(solution)/shard_map/ppermute | solution.py:40
  55.0 1.5 %shard_map.63.inputs_t = bf16[1536,1024]{1,0:T(8,128)(2,1)S(1)} custom-call(bf16[4,64,1536]{2,1,0:T(8,128)(2,1)S(1)} %pad_maximum_fusion.refs_0_, bf16[4,64,1536]{2,1,0:T(8,128)(2,1)S(1)} %collective-permute-done.9.refs_1_, bf16[4,64,1536]{2,1,0:T(8,128)(2,1)S(1)} %collective-permute-done.12.refs_2_, bf16[4,64,1536]{2,1,0:T(8,128)(2,1)S(1)} %collective-permute-done.10.refs_3_), custom_call_target="tpu_custom_call" | custom-call | flops 1 | bytes 1 | tf_op jit(solution)/shard_map/pallas_call | solution.py:175
  56.5 12.0 %shard_map.64 = bf16[1536,3072]{1,0:T(8,128)(2,1)} custom-call(bf16[1536,1024]{1,0:T(8,128)(2,1)S(1)} %shard_map.63.inputs_t, bf16[128,3072]{1,0:T(8,128)(2,1)S(1)} %fusion.9.refs_0_, bf16[128,3072]{1,0:T(8,128)(2,1)S(1)} %bitcast.21, bf16[128,3072]{1,0:T(8,128)(2,1)S(1)} %bitcast.15, bf16[128,3072]{1,0:T(8,128)(2,1)S(1)} %bitcast.16, ...), custom_call_target="tpu_custom_call" | custom-call | flops 1 | bytes 1 | tf_op jit(solution)/shard_map/pallas_call | solution.py:197
  68.5 3.9 %collective-permute-done.14.refs_2_ = bf16[4,64,1536]{2,1,0:T(8,128)(2,1)S(1)} collective-permute-done((bf16[4,64,1536]{2,1,0:T(8,128)(2,1)S(1)}, bf16[4,64,1536]{2,1,0:T(8,128)(2,1)S(1)}, u32[]{:S(2)}, u32[]{:S(2)}) %collective-permute-start.14) | collective-permute-done | bytes 786464 | tf_op jit(solution)/shard_map/ppermute | solution.py:40
  72.3 0.4 shard_map.66
  72.7 1.6 %collective-permute-start.16 = (bf16[64,1536]{1,0:T(8,128)(2,1)S(1)}, bf16[64,1536]{1,0:T(8,128)(2,1)S(1)}, u32[]{:S(2)}, u32[]{:S(2)}) collective-permute-start(bf16[64,1536]{1,0:T(8,128)(2,1)S(1)} %get-tuple-element.104), channel_id=1, source_target_pairs={{0,32},{1,9},{2,34},{3,11},{4,36},{5,13},{6,38},{7,15},{8,40},{9,1... | collective-permute-start | bytes 589832 | tf_op jit(solution)/shard_map/ppermute | solution.py:40
  74.3 2.7 %collective-permute-start.17 = (bf16[64,1536]{1,0:T(8,128)(2,1)S(1)}, bf16[64,1536]{1,0:T(8,128)(2,1)S(1)}, u32[]{:S(2)}, u32[]{:S(2)}) collective-permute-start(bf16[64,1536]{1,0:T(8,128)(2,1)S(1)} %get-tuple-element.105), channel_id=1, source_target_pairs={{0,64},{1,17},{2,66},{3,19},{4,68},{5,21},{6,70},{7,23},{8,72},{9,... | collective-permute-start | bytes 589832 | tf_op jit(solution)/shard_map/ppermute | solution.py:40
  77.0 1.4 %collective-permute-start.18 = (bf16[64,1536]{1,0:T(8,128)(2,1)S(1)}, bf16[64,1536]{1,0:T(8,128)(2,1)S(1)}, u32[]{:S(2)}, u32[]{:S(2)}) collective-permute-start(bf16[64,1536]{1,0:T(8,128)(2,1)S(1)} %get-tuple-element.106), channel_id=1, source_target_pairs={{0,96},{1,25},{2,98},{3,27},{4,100},{5,29},{6,102},{7,31},{8,104},... | collective-permute-start | bytes 589832 | tf_op jit(solution)/shard_map/ppermute | solution.py:40
  78.5 1.2 %collective-permute-done.16 = bf16[64,1536]{1,0:T(8,128)(2,1)S(1)} collective-permute-done((bf16[64,1536]{1,0:T(8,128)(2,1)S(1)}, bf16[64,1536]{1,0:T(8,128)(2,1)S(1)}, u32[]{:S(2)}, u32[]{:S(2)}) %collective-permute-start.16) | collective-permute-done | bytes 196640 | tf_op jit(solution)/shard_map/ppermute | solution.py:40
  79.7 3.1 %collective-permute-done.17 = bf16[64,1536]{1,0:T(8,128)(2,1)S(1)} collective-permute-done((bf16[64,1536]{1,0:T(8,128)(2,1)S(1)}, bf16[64,1536]{1,0:T(8,128)(2,1)S(1)}, u32[]{:S(2)}, u32[]{:S(2)}) %collective-permute-start.17) | collective-permute-done | bytes 196640 | tf_op jit(solution)/shard_map/ppermute | solution.py:40
  82.8 0.8 add_convert_fusion
  (19 shorter events, 0.3 us)
Async XLA Ops:
  0.6 4.1 %copy-start = (bf16[64,1536]{1,0:T(8,128)(2,1)S(1)}, bf16[64,1536]{1,0:T(8,128)(2,1)}, u32[]{:S(2)}) copy-start(bf16[64,1536]{1,0:T(8,128)(2,1)} %param.4) | copy-start | bytes 589828
  2.9 13.3 %collective-permute-start.1 = (bf16[2,64,3072]{2,1,0:T(8,128)(2,1)S(1)}, bf16[2,64,3072]{2,1,0:T(8,128)(2,1)S(1)}, u32[]{:S(2)}, u32[]{:S(2)}) collective-permute-start(bf16[2,64,3072]{2,1,0:T(8,128)(2,1)S(1)} %bitcast.12), channel_id=1, source_target_pairs={{0,1},{1,0},{2,3},{3,2},{4,5},{5,4},{6,7},{7,6},{8,9},{9,8},{10,11... | collective-permute-start | bytes 2359304 | tf_op jit(solution)/shard_map/ppermute | solution.py:40
  3.0 13.3 %collective-permute-start = (bf16[2,64,3072]{2,1,0:T(8,128)(2,1)S(1)}, bf16[2,64,3072]{2,1,0:T(8,128)(2,1)S(1)}, u32[]{:S(2)}, u32[]{:S(2)}) collective-permute-start(bf16[2,64,3072]{2,1,0:T(8,128)(2,1)S(1)} %bitcast.13), channel_id=1, source_target_pairs={{0,2},{1,7},{2,4},{3,1},{4,6},{5,3},{6,0},{7,5},{8,10},{9,15},{10,... | collective-permute-start | bytes 2359304 | tf_op jit(solution)/shard_map/ppermute | solution.py:40
  4.8 9.6 %collective-permute-start.3 = (bf16[64,1536]{1,0:T(8,128)(2,1)S(1)}, bf16[64,1536]{1,0:T(8,128)(2,1)S(1)}, u32[]{:S(2)}, u32[]{:S(2)}) collective-permute-start(bf16[64,1536]{1,0:T(8,128)(2,1)S(1)} %copy-done), channel_id=1, source_target_pairs={{0,16},{1,65},{2,18},{3,67},{4,20},{5,69},{6,22},{7,71},{8,24},{9,... | collective-permute-start | bytes 589832 | tf_op jit(solution)/shard_map/ppermute | solution.py:40
  8.6 6.8 %collective-permute-start.2 = (bf16[64,1536]{1,0:T(8,128)(2,1)S(1)}, bf16[64,1536]{1,0:T(8,128)(2,1)S(1)}, u32[]{:S(2)}, u32[]{:S(2)}) collective-permute-start(bf16[64,1536]{1,0:T(8,128)(2,1)S(1)} %copy-done), channel_id=1, source_target_pairs={{0,24},{1,97},{2,26},{3,99},{4,28},{5,101},{6,30},{7,103},{8,0},{9... | collective-permute-start | bytes 589832 | tf_op jit(solution)/shard_map/ppermute | solution.py:40
  9.4 6.9 %collective-permute-start.4 = (bf16[64,1536]{1,0:T(8,128)(2,1)S(1)}, bf16[64,1536]{1,0:T(8,128)(2,1)S(1)}, u32[]{:S(2)}, u32[]{:S(2)}) collective-permute-start(bf16[64,1536]{1,0:T(8,128)(2,1)S(1)} %copy-done), channel_id=1, source_target_pairs={{0,8},{1,33},{2,10},{3,35},{4,12},{5,37},{6,14},{7,39},{8,16},{9,4... | collective-permute-start | bytes 589832 | tf_op jit(solution)/shard_map/ppermute | solution.py:40
  16.3 7.8 %collective-permute-start.6 = (bf16[2,64,3072]{2,1,0:T(8,128)(2,1)S(1)}, bf16[2,64,3072]{2,1,0:T(8,128)(2,1)S(1)}, u32[]{:S(2)}, u32[]{:S(2)}) collective-permute-start(bf16[2,64,3072]{2,1,0:T(8,128)(2,1)S(1)} %collective-permute-done.refs_0_), channel_id=1, source_target_pairs={{0,1},{1,0},{2,3},{3,2},{4,5},{5,4},{6,7},{7,6},{8,9},{9,8},{10,11... | collective-permute-start | bytes 2359304 | tf_op jit(solution)/shard_map/ppermute | solution.py:40
  16.3 13.2 %collective-permute-start.5 = (bf16[2,64,3072]{2,1,0:T(8,128)(2,1)S(1)}, bf16[2,64,3072]{2,1,0:T(8,128)(2,1)S(1)}, u32[]{:S(2)}, u32[]{:S(2)}) collective-permute-start(bf16[2,64,3072]{2,1,0:T(8,128)(2,1)S(1)} %collective-permute-done.refs_0_), channel_id=1, source_target_pairs={{0,2},{1,7},{2,4},{3,1},{4,6},{5,3},{6,0},{7,5},{8,10},{9,15},{10,... | collective-permute-start | bytes 2359304 | tf_op jit(solution)/shard_map/ppermute | solution.py:40
  18.0 17.7 %collective-permute-start.10 = (bf16[4,64,1536]{2,1,0:T(8,128)(2,1)S(1)}, bf16[4,64,1536]{2,1,0:T(8,128)(2,1)S(1)}, u32[]{:S(2)}, u32[]{:S(2)}) collective-permute-start(bf16[4,64,1536]{2,1,0:T(8,128)(2,1)S(1)} %pad_maximum_fusion.refs_0_), channel_id=1, source_target_pairs={{0,32},{1,9},{2,34},{3,11},{4,36},{5,13},{6,38},{7,15},{8,40},{9,1... | collective-permute-start | bytes 2359304 | tf_op jit(solution)/shard_map/ppermute | solution.py:40
  19.6 16.1 %collective-permute-start.9 = (bf16[4,64,1536]{2,1,0:T(8,128)(2,1)S(1)}, bf16[4,64,1536]{2,1,0:T(8,128)(2,1)S(1)}, u32[]{:S(2)}, u32[]{:S(2)}) collective-permute-start(bf16[4,64,1536]{2,1,0:T(8,128)(2,1)S(1)} %pad_maximum_fusion.refs_0_), channel_id=1, source_target_pairs={{0,96},{1,25},{2,98},{3,27},{4,100},{5,29},{6,102},{7,31},{8,104},... | collective-permute-start | bytes 2359304 | tf_op jit(solution)/shard_map/ppermute | solution.py:40
  29.5 6.2 %collective-permute-start.8 = (bf16[2,64,3072]{2,1,0:T(8,128)(2,1)S(1)}, bf16[2,64,3072]{2,1,0:T(8,128)(2,1)S(1)}, u32[]{:S(2)}, u32[]{:S(2)}) collective-permute-start(bf16[2,64,3072]{2,1,0:T(8,128)(2,1)S(1)} %collective-permute-done.5.refs_0_), channel_id=1, source_target_pairs={{0,1},{1,0},{2,3},{3,2},{4,5},{5,4},{6,7},{7,6},{8,9},{9,8},{10,11... | collective-permute-start | bytes 2359304 | tf_op jit(solution)/shard_map/ppermute | solution.py:40
  29.5 13.2 %collective-permute-start.7 = (bf16[2,64,3072]{2,1,0:T(8,128)(2,1)S(1)}, bf16[2,64,3072]{2,1,0:T(8,128)(2,1)S(1)}, u32[]{:S(2)}, u32[]{:S(2)}) collective-permute-start(bf16[2,64,3072]{2,1,0:T(8,128)(2,1)S(1)} %collective-permute-done.5.refs_0_), channel_id=1, source_target_pairs={{0,2},{1,7},{2,4},{3,1},{4,6},{5,3},{6,0},{7,5},{8,10},{9,15},{10,... | collective-permute-start | bytes 2359304 | tf_op jit(solution)/shard_map/ppermute | solution.py:40
  29.9 15.6 %collective-permute-start.12 = (bf16[4,64,1536]{2,1,0:T(8,128)(2,1)S(1)}, bf16[4,64,1536]{2,1,0:T(8,128)(2,1)S(1)}, u32[]{:S(2)}, u32[]{:S(2)}) collective-permute-start(bf16[4,64,1536]{2,1,0:T(8,128)(2,1)S(1)} %pad_maximum_fusion.refs_0_), channel_id=1, source_target_pairs={{0,64},{1,17},{2,66},{3,19},{4,68},{5,21},{6,70},{7,23},{8,72},{9,... | collective-permute-start | bytes 2359304 | tf_op jit(solution)/shard_map/ppermute | solution.py:40
  42.7 2.8 %collective-permute-start.11 = (bf16[2,64,3072]{2,1,0:T(8,128)(2,1)S(1)}, bf16[2,64,3072]{2,1,0:T(8,128)(2,1)S(1)}, u32[]{:S(2)}, u32[]{:S(2)}) collective-permute-start(bf16[2,64,3072]{2,1,0:T(8,128)(2,1)S(1)} %collective-permute-done.7.refs_0_), channel_id=1, source_target_pairs={{0,1},{1,0},{2,3},{3,2},{4,5},{5,4},{6,7},{7,6},{8,9},{9,8},{10,11... | collective-permute-start | bytes 2359304 | tf_op jit(solution)/shard_map/ppermute | solution.py:40
  48.3 20.2 %collective-permute-start.13 = (bf16[4,64,1536]{2,1,0:T(8,128)(2,1)S(1)}, bf16[4,64,1536]{2,1,0:T(8,128)(2,1)S(1)}, u32[]{:S(2)}, u32[]{:S(2)}) collective-permute-start(bf16[4,64,1536]{2,1,0:T(8,128)(2,1)S(1)} %get-tuple-element.96), channel_id=1, source_target_pairs={{0,8},{1,33},{2,10},{3,35},{4,12},{5,37},{6,14},{7,39},{8,16},{9,4... | collective-permute-start | bytes 2359304 | tf_op jit(solution)/shard_map/ppermute | solution.py:40
  50.4 22.0 %collective-permute-start.14 = (bf16[4,64,1536]{2,1,0:T(8,128)(2,1)S(1)}, bf16[4,64,1536]{2,1,0:T(8,128)(2,1)S(1)}, u32[]{:S(2)}, u32[]{:S(2)}) collective-permute-start(bf16[4,64,1536]{2,1,0:T(8,128)(2,1)S(1)} %get-tuple-element.97), channel_id=1, source_target_pairs={{0,16},{1,65},{2,18},{3,67},{4,20},{5,69},{6,22},{7,71},{8,24},{9,... | collective-permute-start | bytes 2359304 | tf_op jit(solution)/shard_map/ppermute | solution.py:40
  53.9 18.4 %collective-permute-start.15 = (bf16[4,64,1536]{2,1,0:T(8,128)(2,1)S(1)}, bf16[4,64,1536]{2,1,0:T(8,128)(2,1)S(1)}, u32[]{:S(2)}, u32[]{:S(2)}) collective-permute-start(bf16[4,64,1536]{2,1,0:T(8,128)(2,1)S(1)} %get-tuple-element.98), channel_id=1, source_target_pairs={{0,24},{1,97},{2,26},{3,99},{4,28},{5,101},{6,30},{7,103},{8,0},{9... | collective-permute-start | bytes 2359304 | tf_op jit(solution)/shard_map/ppermute | solution.py:40
  72.7 6.9 %collective-permute-start.16 = (bf16[64,1536]{1,0:T(8,128)(2,1)S(1)}, bf16[64,1536]{1,0:T(8,128)(2,1)S(1)}, u32[]{:S(2)}, u32[]{:S(2)}) collective-permute-start(bf16[64,1536]{1,0:T(8,128)(2,1)S(1)} %get-tuple-element.104), channel_id=1, source_target_pairs={{0,32},{1,9},{2,34},{3,11},{4,36},{5,13},{6,38},{7,15},{8,40},{9,1... | collective-permute-start | bytes 589832 | tf_op jit(solution)/shard_map/ppermute | solution.py:40
  74.3 8.5 %collective-permute-start.17 = (bf16[64,1536]{1,0:T(8,128)(2,1)S(1)}, bf16[64,1536]{1,0:T(8,128)(2,1)S(1)}, u32[]{:S(2)}, u32[]{:S(2)}) collective-permute-start(bf16[64,1536]{1,0:T(8,128)(2,1)S(1)} %get-tuple-element.105), channel_id=1, source_target_pairs={{0,64},{1,17},{2,66},{3,19},{4,68},{5,21},{6,70},{7,23},{8,72},{9,... | collective-permute-start | bytes 589832 | tf_op jit(solution)/shard_map/ppermute | solution.py:40
  77.0 5.8 %collective-permute-start.18 = (bf16[64,1536]{1,0:T(8,128)(2,1)S(1)}, bf16[64,1536]{1,0:T(8,128)(2,1)S(1)}, u32[]{:S(2)}, u32[]{:S(2)}) collective-permute-start(bf16[64,1536]{1,0:T(8,128)(2,1)S(1)} %get-tuple-element.106), channel_id=1, source_target_pairs={{0,96},{1,25},{2,98},{3,27},{4,100},{5,29},{6,102},{7,31},{8,104},... | collective-permute-start | bytes 589832 | tf_op jit(solution)/shard_map/ppermute | solution.py:40

commit v3 on v2

--- a/solution.py
+++ b/solution.py
@@ -58,6 +58,19 @@
 
 def after(value, *others):
     return lax.optimization_barrier((value, *others))[0]
+
+
+def passed(array):
+    anywhere = pl.BlockSpec(memory_space=pl.ANY)
+    return pl.pallas_call(
+        lambda given, same: None,
+        out_shape=jax.ShapeDtypeStruct(array.shape, array.dtype),
+        in_specs=[anywhere],
+        out_specs=anywhere,
+        input_output_aliases={0: 0},
+        compiler_params=pltpu.CompilerParams(vmem_limit_bytes=2**20),
+        cost_estimate=pl.CostEstimate(flops=0, bytes_accessed=6 * 2**20, transcendentals=0),
+    )(array)
 
 
 def fetch_kernel(source, target, sem):
@@ -213,27 +226,29 @@
     hop1 = ring(hop0)
     held_weight = fetch(after(weight, hop0))
 
-    hop1, swap0, held_weight, *beside = barrier((hop1, swap0, held_weight, *beside))
+    swap0, hop1, held_weight, *beside = barrier((swap0, hop1, held_weight, *beside))
     swap1 = swap_core(hop1)
     stacked = jnp.stack(beside)
     gathered = {0: stacked, 1: far(stacked, -1), 3: far(stacked, -3), 2: far(stacked, -2)}
+    hop3 = ring(after(hop0, hop1), -1)
     hop2 = ring(hop1)
     pieces = {(0, False): hop0, (0, True): swap0, (1, False): hop1}
     outs = partial_input([(0, False), (0, True)], pieces, held_weight, [])
 
-    hop2, swap1, *outs = barrier((hop2, swap1, *outs))
-    hop3 = ring(hop2)
-    swap2 = swap_core(hop2)
-    pieces |= {(1, True): swap1, (2, False): hop2}
+    swap1, *outs = barrier((swap1, *outs))
+    pieces |= {(1, True): swap1}
     outs = partial_input([(1, False), (1, True)], pieces, held_weight, outs)
 
-    hop3, swap2, gathered[1], gathered[3], *outs = barrier((hop3, swap2, gathered[1], gathered[3], *outs))
-    swap3 = swap_core(hop3)
-    pieces |= {(2, True): swap2, (3, False): hop3}
-    outs = partial_input([(2, False), (2, True)], pieces, held_weight, outs)
-    swap3, gathered[2], *outs = barrier((swap3, gathered[2], *outs))
-    pieces |= {(3, True): swap3}
-    outs = partial_input([(3, False), (3, True)], pieces, held_weight, outs)
+    hop3, hop2, *outs = barrier((hop3, hop2, *outs))
+    swap2, swap3 = swap_core(hop2), swap_core(hop3)
+    pieces |= {(2, False): hop2, (3, False): hop3}
+    outs = partial_input([(2, False), (3, False)], pieces, held_weight, outs)
+    gathered[2], gathered[3], gathered[1], *outs = barrier((gathered[2], gathered[3], gathered[1], *outs))
+    gathered[2] = passed(gathered[2])
+
+    swap2, swap3, gathered[2], *outs = barrier((swap2, swap3, gathered[2], *outs))
+    pieces |= {(2, True): swap2, (3, True): swap3}
+    outs = partial_input([(2, True), (3, True)], pieces, held_weight, outs)
     terms = [outs[0]] + [near(outs[k], k) for k in (1, 2, 3)]
 
     inputs_t = transposed_inputs(list(pieces), [gathered[k] for k in range(SIDE)])

time: 84 us -> 80.9 us (0.963)
  starting transfers between devices: 28.4 us -> 25.8 us
    ppermute x19, starting transfers between devices: 28.4 us -> 25.8 us  [move(): return lax.ppermute(array, ('row', 'col'), pairs)]
  transfers between devices with their start and end apart: 19 -> 19, of which waited for: 8 -> 8; matrix products, arithmetic and copies ran while one was open for 0% -> 0% of each run, Pallas kernels for 30% -> 32%
where the time goes in v3:
time: 80.9 us; the launch traced here: 80.8 us
  Pallas kernels  28.6 us (35%)
  starting transfers between devices  25.8 us (32%)
  waiting for transfers between devices  22.4 us (28%)
  other arithmetic  3.18 us (4%)
    ppermute x19, starting transfers between devices, move(): return lax.ppermute(array, ('row', 'col'), pairs)  25.8 us
    ppermute x19, waiting for transfers between devices, move(): return lax.ppermute(array, ('row', 'col'), pairs)  22.4 us
    pallas_call x1, Pallas kernels, weight_cotangent(): pl.pallas_call(weight_kernel, grid=(units // tile,), out_shape=jax.ShapeD...  12 us
    pallas_call x4, Pallas kernels, partial_input(): pl.pallas_call(functools.partial(partial_kernel, keys, bool(outs)), out_s...  11 us
    pallas_call x1, Pallas kernels, fetch(): pl.pallas_call(fetch_kernel, out_shape=pltpu.VMEM(array.shape, array.dtyp...  3.69 us
    convert_element_type x1, other arithmetic, hidden_cotangent(): (out_values.astype(F32) * gelu_slope(pre_values.astype(F32))).astype(BF)  2.3 us
  transfers between devices with their start and end apart: 19, of which 8 were waited for; matrix products, arithmetic and copies ran while one was open for 0% of the time, Pallas kernels for 32%

profile of v3, /device:TPU:0, one launch (start us, length us, event | category | flops | bytes accessed | tf_op | source)
XLA Modules:
  0.0 80.8 jit_solution(5334945527180162875)
XLA Ops:
  0.6 2.3 %fusion.9.refs_0_ = bf16[128,3072]{1,0:T(8,128)(2,1)S(1)} fusion(bf16[128,3072]{1,0:T(8,128)(2,1)} %param.5, bf16[128,3072]{1,0:T(8,128)(2,1)} %param.6), kind=kLoop, calls=%fused_computation.12 | loop fusion | flops 6684672 | bytes 2359296 | tf_op jit(solution)/shard_map/convert_element_type | solution.py:28
  2.9 1.7 %collective-permute-start.1 = (bf16[2,64,3072]{2,1,0:T(8,128)(2,1)S(1)}, bf16[2,64,3072]{2,1,0:T(8,128)(2,1)S(1)}, u32[]{:S(2)}, u32[]{:S(2)}) collective-permute-start(bf16[2,64,3072]{2,1,0:T(8,128)(2,1)S(1)} %bitcast.12), channel_id=1, source_target_pairs={{0,2},{1,7},{2,4},{3,1},{4,6},{5,3},{6,0},{7,5},{8,10},{9,15},{10,... | collective-permute-start | bytes 2359304 | tf_op jit(solution)/shard_map/ppermute | solution.py:40
  4.7 1.0 %collective-permute-start = (bf16[2,64,3072]{2,1,0:T(8,128)(2,1)S(1)}, bf16[2,64,3072]{2,1,0:T(8,128)(2,1)S(1)}, u32[]{:S(2)}, u32[]{:S(2)}) collective-permute-start(bf16[2,64,3072]{2,1,0:T(8,128)(2,1)S(1)} %bitcast.13), channel_id=1, source_target_pairs={{0,1},{1,0},{2,3},{3,2},{4,5},{5,4},{6,7},{7,6},{8,9},{9,8},{10,11... | collective-permute-start | bytes 2359304 | tf_op jit(solution)/shard_map/ppermute | solution.py:40
  5.7 3.9 %collective-permute-start.3 = (bf16[64,1536]{1,0:T(8,128)(2,1)S(1)}, bf16[64,1536]{1,0:T(8,128)(2,1)S(1)}, u32[]{:S(2)}, u32[]{:S(2)}) collective-permute-start(bf16[64,1536]{1,0:T(8,128)(2,1)S(1)} %copy-done), channel_id=1, source_target_pairs={{0,16},{1,65},{2,18},{3,67},{4,20},{5,69},{6,22},{7,71},{8,24},{9,... | collective-permute-start | bytes 589832 | tf_op jit(solution)/shard_map/ppermute | solution.py:40
  9.5 0.7 collective-permute-start.2
  10.3 1.3 %collective-permute-start.4 = (bf16[64,1536]{1,0:T(8,128)(2,1)S(1)}, bf16[64,1536]{1,0:T(8,128)(2,1)S(1)}, u32[]{:S(2)}, u32[]{:S(2)}) collective-permute-start(bf16[64,1536]{1,0:T(8,128)(2,1)S(1)} %copy-done), channel_id=1, source_target_pairs={{0,8},{1,33},{2,10},{3,35},{4,12},{5,37},{6,14},{7,39},{8,16},{9,4... | collective-permute-start | bytes 589832 | tf_op jit(solution)/shard_map/ppermute | solution.py:40
  11.6 3.7 %shard_map.59.refs_2_ = bf16[1536,3072]{1,0:T(8,128)(2,1)S(1)} custom-call(bf16[1536,3072]{1,0:T(8,128)(2,1)} %source), custom_call_target="tpu_custom_call" | custom-call | flops 1 | bytes 1 | tf_op jit(solution)/shard_map/pallas_call | solution.py:83
  15.3 1.1 %collective-permute-done.2 = bf16[64,1536]{1,0:T(8,128)(2,1)S(1)} collective-permute-done((bf16[64,1536]{1,0:T(8,128)(2,1)S(1)}, bf16[64,1536]{1,0:T(8,128)(2,1)S(1)}, u32[]{:S(2)}, u32[]{:S(2)}) %collective-permute-start.2) | collective-permute-done | bytes 196640 | tf_op jit(solution)/shard_map/ppermute | solution.py:40
  16.4 0.8 collective-permute-done.4
  17.2 1.0 %collective-permute-start.8 = (bf16[2,64,3072]{2,1,0:T(8,128)(2,1)S(1)}, bf16[2,64,3072]{2,1,0:T(8,128)(2,1)S(1)}, u32[]{:S(2)}, u32[]{:S(2)}) collective-permute-start(bf16[2,64,3072]{2,1,0:T(8,128)(2,1)S(1)} %bitcast.14), channel_id=1, source_target_pairs={{0,6},{1,3},{2,0},{3,5},{4,2},{5,7},{6,4},{7,1},{8,14},{9,11},{10,... | collective-permute-start | bytes 2359304 | tf_op jit(solution)/shard_map/ppermute | solution.py:40
  18.1 1.1 %collective-permute-start.9 = (bf16[2,64,3072]{2,1,0:T(8,128)(2,1)S(1)}, bf16[2,64,3072]{2,1,0:T(8,128)(2,1)S(1)}, u32[]{:S(2)}, u32[]{:S(2)}) collective-permute-start(bf16[2,64,3072]{2,1,0:T(8,128)(2,1)S(1)} %collective-permute-done.1.refs_0_), channel_id=1, source_target_pairs={{0,2},{1,7},{2,4},{3,1},{4,6},{5,3},{6,0},{7,5},{8,10},{9,15},{10,... | collective-permute-start | bytes 2359304 | tf_op jit(solution)/shard_map/ppermute | solution.py:40
  19.4 2.8 %collective-permute-start.7 = (bf16[4,64,1536]{2,1,0:T(8,128)(2,1)S(1)}, bf16[4,64,1536]{2,1,0:T(8,128)(2,1)S(1)}, u32[]{:S(2)}, u32[]{:S(2)}) collective-permute-start(bf16[4,64,1536]{2,1,0:T(8,128)(2,1)S(1)} %pad_maximum_fusion.refs_0_), channel_id=1, source_target_pairs={{0,96},{1,25},{2,98},{3,27},{4,100},{5,29},{6,102},{7,31},{8,104},... | collective-permute-start | bytes 2359304 | tf_op jit(solution)/shard_map/ppermute | solution.py:40
  22.2 2.8 %shard_map.60 = (bf16[4,64,1536]{2,1,0:T(8,128)(2,1)S(1)}, bf16[4,64,1536]{2,1,0:T(8,128)(2,1)S(1)}, bf16[4,64,1536]{2,1,0:T(8,128)(2,1)S(1)}, bf16[4,64,1536]{2,1,0:T(8,128)(2,1)S(1)}) custom-call(bf16[2,64,3072]{2,1,0:T(8,128)(2,1)S(1)} %bitcast.15, bf16[2,64,3072]{2,1,0:T(8,128)(2,1)S(1)} %collective-permute-done.refs_1_, ...), custom_call_target="tpu_custom_call" | custom-call | flops 1 | bytes 1 | tf_op jit(solution)/shard_map/pallas_call | solution.py:128
  25.0 2.4 %collective-permute-start.5 = (bf16[4,64,1536]{2,1,0:T(8,128)(2,1)S(1)}, bf16[4,64,1536]{2,1,0:T(8,128)(2,1)S(1)}, u32[]{:S(2)}, u32[]{:S(2)}) collective-permute-start(bf16[4,64,1536]{2,1,0:T(8,128)(2,1)S(1)} %pad_maximum_fusion.refs_0_), channel_id=1, source_target_pairs={{0,64},{1,17},{2,66},{3,19},{4,68},{5,21},{6,70},{7,23},{8,72},{9,... | collective-permute-start | bytes 2359304 | tf_op jit(solution)/shard_map/ppermute | solution.py:40
  27.3 2.8 %shard_map.61 = (bf16[4,64,1536]{2,1,0:T(8,128)(2,1)S(1)}, bf16[4,64,1536]{2,1,0:T(8,128)(2,1)S(1)}, bf16[4,64,1536]{2,1,0:T(8,128)(2,1)S(1)}, bf16[4,64,1536]{2,1,0:T(8,128)(2,1)S(1)}) custom-call(bf16[2,64,3072]{2,1,0:T(8,128)(2,1)S(1)} %collective-permute-done.1.refs_0_, ...), custom_call_target="tpu_custom_call", output_to_operand_aliasing={{0}: (3, {}), {1}: (4, {}), {2}: (5, {}), {3}: (6, {})} | custom-call | flops 1 | bytes 1 | tf_op jit(solution)/shard_map/pallas_call | solution.py:128
  30.1 7.3 %collective-permute-done.8.refs_1_ = bf16[2,64,3072]{2,1,0:T(8,128)(2,1)S(1)} collective-permute-done((bf16[2,64,3072]{2,1,0:T(8,128)(2,1)S(1)}, bf16[2,64,3072]{2,1,0:T(8,128)(2,1)S(1)}, u32[]{:S(2)}, u32[]{:S(2)}) %collective-permute-start.8) | collective-permute-done | bytes 786464 | tf_op jit(solution)/shard_map/ppermute | solution.py:40
  37.4 0.9 %collective-permute-done.9.refs_0_ = bf16[2,64,3072]{2,1,0:T(8,128)(2,1)S(1)} collective-permute-done((bf16[2,64,3072]{2,1,0:T(8,128)(2,1)S(1)}, bf16[2,64,3072]{2,1,0:T(8,128)(2,1)S(1)}, u32[]{:S(2)}, u32[]{:S(2)}) %collective-permute-start.9) | collective-permute-done | bytes 786464 | tf_op jit(solution)/shard_map/ppermute | solution.py:40
  38.3 0.5 collective-permute-start.12
  38.8 2.8 %shard_map.62 = (bf16[4,64,1536]{2,1,0:T(8,128)(2,1)S(1)}, bf16[4,64,1536]{2,1,0:T(8,128)(2,1)S(1)}, bf16[4,64,1536]{2,1,0:T(8,128)(2,1)S(1)}, bf16[4,64,1536]{2,1,0:T(8,128)(2,1)S(1)}) custom-call(bf16[2,64,3072]{2,1,0:T(8,128)(2,1)S(1)} %collective-permute-done.9.refs_0_, ...), custom_call_target="tpu_custom_call", output_to_operand_aliasing={{0}: (3, {}), {1}: (4, {}), {2}: (5, {}), {3}: (6, {})} | custom-call | flops 1 | bytes 1 | tf_op jit(solution)/shard_map/pallas_call | solution.py:128
  41.6 2.2 %collective-permute-done.6.refs_3_ = bf16[4,64,1536]{2,1,0:T(8,128)(2,1)S(1)} collective-permute-done((bf16[4,64,1536]{2,1,0:T(8,128)(2,1)S(1)}, bf16[4,64,1536]{2,1,0:T(8,128)(2,1)S(1)}, u32[]{:S(2)}, u32[]{:S(2)}) %collective-permute-start.6) | collective-permute-done | bytes 786464 | tf_op jit(solution)/shard_map/ppermute | solution.py:40
  43.8 2.8 %shard_map.66 = (bf16[4,64,1536]{2,1,0:T(8,128)(2,1)S(1)}, bf16[4,64,1536]{2,1,0:T(8,128)(2,1)S(1)}, bf16[4,64,1536]{2,1,0:T(8,128)(2,1)S(1)}, bf16[4,64,1536]{2,1,0:T(8,128)(2,1)S(1)}) custom-call(bf16[2,64,3072]{2,1,0:T(8,128)(2,1)S(1)} %collective-permute-done.11.refs_0_, ...), custom_call_target="tpu_custom_call", output_to_operand_aliasing={{0}: (3, {}), {1}: (4, {}), {2}: (5, {}), {3}: (6, {})} | custom-call | flops 1 | bytes 1 | tf_op jit(solution)/shard_map/pallas_call | solution.py:128
  46.6 1.1 %collective-permute-start.13 = (bf16[4,64,1536]{2,1,0:T(8,128)(2,1)S(1)}, bf16[4,64,1536]{2,1,0:T(8,128)(2,1)S(1)}, u32[]{:S(2)}, u32[]{:S(2)}) collective-permute-start(bf16[4,64,1536]{2,1,0:T(8,128)(2,1)S(1)} %get-tuple-element.108), channel_id=1, source_target_pairs={{0,8},{1,33},{2,10},{3,35},{4,12},{5,37},{6,14},{7,39},{8,16},{9,4... | collective-permute-start | bytes 2359304 | tf_op jit(solution)/shard_map/ppermute | solution.py:40
  47.7 3.6 %collective-permute-start.14 = (bf16[4,64,1536]{2,1,0:T(8,128)(2,1)S(1)}, bf16[4,64,1536]{2,1,0:T(8,128)(2,1)S(1)}, u32[]{:S(2)}, u32[]{:S(2)}) collective-permute-start(bf16[4,64,1536]{2,1,0:T(8,128)(2,1)S(1)} %get-tuple-element.109), channel_id=1, source_target_pairs={{0,16},{1,65},{2,18},{3,67},{4,20},{5,69},{6,22},{7,71},{8,24},{9,... | collective-permute-start | bytes 2359304 | tf_op jit(solution)/shard_map/ppermute | solution.py:40
  51.2 1.0 %collective-permute-start.15 = (bf16[4,64,1536]{2,1,0:T(8,128)(2,1)S(1)}, bf16[4,64,1536]{2,1,0:T(8,128)(2,1)S(1)}, u32[]{:S(2)}, u32[]{:S(2)}) collective-permute-start(bf16[4,64,1536]{2,1,0:T(8,128)(2,1)S(1)} %get-tuple-element.110), channel_id=1, source_target_pairs={{0,24},{1,97},{2,26},{3,99},{4,28},{5,101},{6,30},{7,103},{8,0},{9... | collective-permute-start | bytes 2359304 | tf_op jit(solution)/shard_map/ppermute | solution.py:40
  52.2 1.5 %shard_map.64.inputs_t = bf16[1536,1024]{1,0:T(8,128)(2,1)S(1)} custom-call(bf16[4,64,1536]{2,1,0:T(8,128)(2,1)S(1)} %pad_maximum_fusion.refs_0_, bf16[4,64,1536]{2,1,0:T(8,128)(2,1)S(1)} %collective-permute-done.7.refs_1_, bf16[4,64,1536]{2,1,0:T(8,128)(2,1)S(1)} %shard_map.63.refs_2_, bf16[4,64,1536]{2,1,0:T(8,128)(2,1)S(1)} %collective-permute-done.6.refs_3_), custom_call_target="tpu_custom_call" | custom-call | flops 1 | bytes 1 | tf_op jit(solution)/shard_map/pallas_call | solution.py:188
  53.8 12.0 %shard_map.65 = bf16[1536,3072]{1,0:T(8,128)(2,1)} custom-call(bf16[1536,1024]{1,0:T(8,128)(2,1)S(1)} %shard_map.64.inputs_t, bf16[128,3072]{1,0:T(8,128)(2,1)S(1)} %fusion.9.refs_0_, bf16[128,3072]{1,0:T(8,128)(2,1)S(1)} %bitcast.22, bf16[128,3072]{1,0:T(8,128)(2,1)S(1)} %bitcast.16, bf16[128,3072]{1,0:T(8,128)(2,1)S(1)} %bitcast.17, ...), custom_call_target="tpu_custom_call" | custom-call | flops 1 | bytes 1 | tf_op jit(solution)/shard_map/pallas_call | solution.py:210
  65.8 3.9 %collective-permute-done.14.refs_2_ = bf16[4,64,1536]{2,1,0:T(8,128)(2,1)S(1)} collective-permute-done((bf16[4,64,1536]{2,1,0:T(8,128)(2,1)S(1)}, bf16[4,64,1536]{2,1,0:T(8,128)(2,1)S(1)}, u32[]{:S(2)}, u32[]{:S(2)}) %collective-permute-start.14) | collective-permute-done | bytes 786464 | tf_op jit(solution)/shard_map/ppermute | solution.py:40
  70.1 2.2 %collective-permute-start.17 = (bf16[64,1536]{1,0:T(8,128)(2,1)S(1)}, bf16[64,1536]{1,0:T(8,128)(2,1)S(1)}, u32[]{:S(2)}, u32[]{:S(2)}) collective-permute-start(bf16[64,1536]{1,0:T(8,128)(2,1)S(1)} %get-tuple-element.117), channel_id=1, source_target_pairs={{0,64},{1,17},{2,66},{3,19},{4,68},{5,21},{6,70},{7,23},{8,72},{9,... | collective-permute-start | bytes 589832 | tf_op jit(solution)/shard_map/ppermute | solution.py:40
  72.3 1.4 %collective-permute-start.18 = (bf16[64,1536]{1,0:T(8,128)(2,1)S(1)}, bf16[64,1536]{1,0:T(8,128)(2,1)S(1)}, u32[]{:S(2)}, u32[]{:S(2)}) collective-permute-start(bf16[64,1536]{1,0:T(8,128)(2,1)S(1)} %get-tuple-element.118), channel_id=1, source_target_pairs={{0,96},{1,25},{2,98},{3,27},{4,100},{5,29},{6,102},{7,31},{8,104},... | collective-permute-start | bytes 589832 | tf_op jit(solution)/shard_map/ppermute | solution.py:40
  73.7 5.4 %collective-permute-done.16 = bf16[64,1536]{1,0:T(8,128)(2,1)S(1)} collective-permute-done((bf16[64,1536]{1,0:T(8,128)(2,1)S(1)}, bf16[64,1536]{1,0:T(8,128)(2,1)S(1)}, u32[]{:S(2)}, u32[]{:S(2)}) %collective-permute-start.16) | collective-permute-done | bytes 196640 | tf_op jit(solution)/shard_map/ppermute | solution.py:40
  79.1 0.9 %collective-permute-done.18 = bf16[64,1536]{1,0:T(8,128)(2,1)S(1)} collective-permute-done((bf16[64,1536]{1,0:T(8,128)(2,1)S(1)}, bf16[64,1536]{1,0:T(8,128)(2,1)S(1)}, u32[]{:S(2)}, u32[]{:S(2)}) %collective-permute-start.18) | collective-permute-done | bytes 196640 | tf_op jit(solution)/shard_map/ppermute | solution.py:40
  80.0 0.8 add_convert_fusion
  (20 shorter events, 0.6 us)
Async XLA Ops:
  0.6 5.0 %copy-start = (bf16[64,1536]{1,0:T(8,128)(2,1)S(1)}, bf16[64,1536]{1,0:T(8,128)(2,1)}, u32[]{:S(2)}) copy-start(bf16[64,1536]{1,0:T(8,128)(2,1)} %param.4) | copy-start | bytes 589828
  2.9 14.2 %collective-permute-start.1 = (bf16[2,64,3072]{2,1,0:T(8,128)(2,1)S(1)}, bf16[2,64,3072]{2,1,0:T(8,128)(2,1)S(1)}, u32[]{:S(2)}, u32[]{:S(2)}) collective-permute-start(bf16[2,64,3072]{2,1,0:T(8,128)(2,1)S(1)} %bitcast.12), channel_id=1, source_target_pairs={{0,2},{1,7},{2,4},{3,1},{4,6},{5,3},{6,0},{7,5},{8,10},{9,15},{10,... | collective-permute-start | bytes 2359304 | tf_op jit(solution)/shard_map/ppermute | solution.py:40
  4.7 12.5 %collective-permute-start = (bf16[2,64,3072]{2,1,0:T(8,128)(2,1)S(1)}, bf16[2,64,3072]{2,1,0:T(8,128)(2,1)S(1)}, u32[]{:S(2)}, u32[]{:S(2)}) collective-permute-start(bf16[2,64,3072]{2,1,0:T(8,128)(2,1)S(1)} %bitcast.13), channel_id=1, source_target_pairs={{0,1},{1,0},{2,3},{3,2},{4,5},{5,4},{6,7},{7,6},{8,9},{9,8},{10,11... | collective-permute-start | bytes 2359304 | tf_op jit(solution)/shard_map/ppermute | solution.py:40
  5.7 9.6 %collective-permute-start.3 = (bf16[64,1536]{1,0:T(8,128)(2,1)S(1)}, bf16[64,1536]{1,0:T(8,128)(2,1)S(1)}, u32[]{:S(2)}, u32[]{:S(2)}) collective-permute-start(bf16[64,1536]{1,0:T(8,128)(2,1)S(1)} %copy-done), channel_id=1, source_target_pairs={{0,16},{1,65},{2,18},{3,67},{4,20},{5,69},{6,22},{7,71},{8,24},{9,... | collective-permute-start | bytes 589832 | tf_op jit(solution)/shard_map/ppermute | solution.py:40
  9.5 6.8 %collective-permute-start.2 = (bf16[64,1536]{1,0:T(8,128)(2,1)S(1)}, bf16[64,1536]{1,0:T(8,128)(2,1)S(1)}, u32[]{:S(2)}, u32[]{:S(2)}) collective-permute-start(bf16[64,1536]{1,0:T(8,128)(2,1)S(1)} %copy-done), channel_id=1, source_target_pairs={{0,24},{1,97},{2,26},{3,99},{4,28},{5,101},{6,30},{7,103},{8,0},{9... | collective-permute-start | bytes 589832 | tf_op jit(solution)/shard_map/ppermute | solution.py:40
  10.3 6.9 %collective-permute-start.4 = (bf16[64,1536]{1,0:T(8,128)(2,1)S(1)}, bf16[64,1536]{1,0:T(8,128)(2,1)S(1)}, u32[]{:S(2)}, u32[]{:S(2)}) collective-permute-start(bf16[64,1536]{1,0:T(8,128)(2,1)S(1)} %copy-done), channel_id=1, source_target_pairs={{0,8},{1,33},{2,10},{3,35},{4,12},{5,37},{6,14},{7,39},{8,16},{9,4... | collective-permute-start | bytes 589832 | tf_op jit(solution)/shard_map/ppermute | solution.py:40
  17.1 7.8 %collective-permute-start.10 = (bf16[2,64,3072]{2,1,0:T(8,128)(2,1)S(1)}, bf16[2,64,3072]{2,1,0:T(8,128)(2,1)S(1)}, u32[]{:S(2)}, u32[]{:S(2)}) collective-permute-start(bf16[2,64,3072]{2,1,0:T(8,128)(2,1)S(1)} %collective-permute-done.1.refs_0_), channel_id=1, source_target_pairs={{0,1},{1,0},{2,3},{3,2},{4,5},{5,4},{6,7},{7,6},{8,9},{9,8},{10,11... | collective-permute-start | bytes 2359304 | tf_op jit(solution)/shard_map/ppermute | solution.py:40
  17.2 20.3 %collective-permute-start.8 = (bf16[2,64,3072]{2,1,0:T(8,128)(2,1)S(1)}, bf16[2,64,3072]{2,1,0:T(8,128)(2,1)S(1)}, u32[]{:S(2)}, u32[]{:S(2)}) collective-permute-start(bf16[2,64,3072]{2,1,0:T(8,128)(2,1)S(1)} %bitcast.14), channel_id=1, source_target_pairs={{0,6},{1,3},{2,0},{3,5},{4,2},{5,7},{6,4},{7,1},{8,14},{9,11},{10,... | collective-permute-start | bytes 2359304 | tf_op jit(solution)/shard_map/ppermute | solution.py:40
  18.1 20.2 %collective-permute-start.9 = (bf16[2,64,3072]{2,1,0:T(8,128)(2,1)S(1)}, bf16[2,64,3072]{2,1,0:T(8,128)(2,1)S(1)}, u32[]{:S(2)}, u32[]{:S(2)}) collective-permute-start(bf16[2,64,3072]{2,1,0:T(8,128)(2,1)S(1)} %collective-permute-done.1.refs_0_), channel_id=1, source_target_pairs={{0,2},{1,7},{2,4},{3,1},{4,6},{5,3},{6,0},{7,5},{8,10},{9,15},{10,... | collective-permute-start | bytes 2359304 | tf_op jit(solution)/shard_map/ppermute | solution.py:40
  19.4 22.2 %collective-permute-start.7 = (bf16[4,64,1536]{2,1,0:T(8,128)(2,1)S(1)}, bf16[4,64,1536]{2,1,0:T(8,128)(2,1)S(1)}, u32[]{:S(2)}, u32[]{:S(2)}) collective-permute-start(bf16[4,64,1536]{2,1,0:T(8,128)(2,1)S(1)} %pad_maximum_fusion.refs_0_), channel_id=1, source_target_pairs={{0,96},{1,25},{2,98},{3,27},{4,100},{5,29},{6,102},{7,31},{8,104},... | collective-permute-start | bytes 2359304 | tf_op jit(solution)/shard_map/ppermute | solution.py:40
  22.2 21.6 %collective-permute-start.6 = (bf16[4,64,1536]{2,1,0:T(8,128)(2,1)S(1)}, bf16[4,64,1536]{2,1,0:T(8,128)(2,1)S(1)}, u32[]{:S(2)}, u32[]{:S(2)}) collective-permute-start(bf16[4,64,1536]{2,1,0:T(8,128)(2,1)S(1)} %pad_maximum_fusion.refs_0_), channel_id=1, source_target_pairs={{0,32},{1,9},{2,34},{3,11},{4,36},{5,13},{6,38},{7,15},{8,40},{9,1... | collective-permute-start | bytes 2359304 | tf_op jit(solution)/shard_map/ppermute | solution.py:40
  25.0 18.9 %collective-permute-start.5 = (bf16[4,64,1536]{2,1,0:T(8,128)(2,1)S(1)}, bf16[4,64,1536]{2,1,0:T(8,128)(2,1)S(1)}, u32[]{:S(2)}, u32[]{:S(2)}) collective-permute-start(bf16[4,64,1536]{2,1,0:T(8,128)(2,1)S(1)} %pad_maximum_fusion.refs_0_), channel_id=1, source_target_pairs={{0,64},{1,17},{2,66},{3,19},{4,68},{5,21},{6,70},{7,23},{8,72},{9,... | collective-permute-start | bytes 2359304 | tf_op jit(solution)/shard_map/ppermute | solution.py:40
  38.3 5.5 %collective-permute-start.11 = (bf16[2,64,3072]{2,1,0:T(8,128)(2,1)S(1)}, bf16[2,64,3072]{2,1,0:T(8,128)(2,1)S(1)}, u32[]{:S(2)}, u32[]{:S(2)}) collective-permute-start(bf16[2,64,3072]{2,1,0:T(8,128)(2,1)S(1)} %collective-permute-done.9.refs_0_), channel_id=1, source_target_pairs={{0,1},{1,0},{2,3},{3,2},{4,5},{5,4},{6,7},{7,6},{8,9},{9,8},{10,11... | collective-permute-start | bytes 2359304 | tf_op jit(solution)/shard_map/ppermute | solution.py:40
  38.3 5.5 %collective-permute-start.12 = (bf16[2,64,3072]{2,1,0:T(8,128)(2,1)S(1)}, bf16[2,64,3072]{2,1,0:T(8,128)(2,1)S(1)}, u32[]{:S(2)}, u32[]{:S(2)}) collective-permute-start(bf16[2,64,3072]{2,1,0:T(8,128)(2,1)S(1)} %collective-permute-done.8.refs_1_), channel_id=1, source_target_pairs={{0,1},{1,0},{2,3},{3,2},{4,5},{5,4},{6,7},{7,6},{8,9},{9,8},{10,11... | collective-permute-start | bytes 2359304 | tf_op jit(solution)/shard_map/ppermute | solution.py:40
  46.6 19.2 %collective-permute-start.13 = (bf16[4,64,1536]{2,1,0:T(8,128)(2,1)S(1)}, bf16[4,64,1536]{2,1,0:T(8,128)(2,1)S(1)}, u32[]{:S(2)}, u32[]{:S(2)}) collective-permute-start(bf16[4,64,1536]{2,1,0:T(8,128)(2,1)S(1)} %get-tuple-element.108), channel_id=1, source_target_pairs={{0,8},{1,33},{2,10},{3,35},{4,12},{5,37},{6,14},{7,39},{8,16},{9,4... | collective-permute-start | bytes 2359304 | tf_op jit(solution)/shard_map/ppermute | solution.py:40
  47.7 22.0 %collective-permute-start.14 = (bf16[4,64,1536]{2,1,0:T(8,128)(2,1)S(1)}, bf16[4,64,1536]{2,1,0:T(8,128)(2,1)S(1)}, u32[]{:S(2)}, u32[]{:S(2)}) collective-permute-start(bf16[4,64,1536]{2,1,0:T(8,128)(2,1)S(1)} %get-tuple-element.109), channel_id=1, source_target_pairs={{0,16},{1,65},{2,18},{3,67},{4,20},{5,69},{6,22},{7,71},{8,24},{9,... | collective-permute-start | bytes 2359304 | tf_op jit(solution)/shard_map/ppermute | solution.py:40
  51.2 18.4 %collective-permute-start.15 = (bf16[4,64,1536]{2,1,0:T(8,128)(2,1)S(1)}, bf16[4,64,1536]{2,1,0:T(8,128)(2,1)S(1)}, u32[]{:S(2)}, u32[]{:S(2)}) collective-permute-start(bf16[4,64,1536]{2,1,0:T(8,128)(2,1)S(1)} %get-tuple-element.110), channel_id=1, source_target_pairs={{0,24},{1,97},{2,26},{3,99},{4,28},{5,101},{6,30},{7,103},{8,0},{9... | collective-permute-start | bytes 2359304 | tf_op jit(solution)/shard_map/ppermute | solution.py:40
  70.0 9.1 %collective-permute-start.16 = (bf16[64,1536]{1,0:T(8,128)(2,1)S(1)}, bf16[64,1536]{1,0:T(8,128)(2,1)S(1)}, u32[]{:S(2)}, u32[]{:S(2)}) collective-permute-start(bf16[64,1536]{1,0:T(8,128)(2,1)S(1)} %get-tuple-element.116), channel_id=1, source_target_pairs={{0,32},{1,9},{2,34},{3,11},{4,36},{5,13},{6,38},{7,15},{8,40},{9,1... | collective-permute-start | bytes 589832 | tf_op jit(solution)/shard_map/ppermute | solution.py:40
  70.1 9.0 %collective-permute-start.17 = (bf16[64,1536]{1,0:T(8,128)(2,1)S(1)}, bf16[64,1536]{1,0:T(8,128)(2,1)S(1)}, u32[]{:S(2)}, u32[]{:S(2)}) collective-permute-start(bf16[64,1536]{1,0:T(8,128)(2,1)S(1)} %get-tuple-element.117), channel_id=1, source_target_pairs={{0,64},{1,17},{2,66},{3,19},{4,68},{5,21},{6,70},{7,23},{8,72},{9,... | collective-permute-start | bytes 589832 | tf_op jit(solution)/shard_map/ppermute | solution.py:40
  72.3 7.7 %collective-permute-start.18 = (bf16[64,1536]{1,0:T(8,128)(2,1)S(1)}, bf16[64,1536]{1,0:T(8,128)(2,1)S(1)}, u32[]{:S(2)}, u32[]{:S(2)}) collective-permute-start(bf16[64,1536]{1,0:T(8,128)(2,1)S(1)} %get-tuple-element.118), channel_id=1, source_target_pairs={{0,96},{1,25},{2,98},{3,27},{4,100},{5,29},{6,102},{7,31},{8,104},... | collective-permute-start | bytes 589832 | tf_op jit(solution)/shard_map/ppermute | solution.py:40

commit v4 on v3

--- a/solution.py
+++ b/solution.py
@@ -11,6 +11,7 @@
 F32 = jnp.float32
 SIDE = 4
 TILE = 768
+LOADS = 4
 WHOLE = pl.BlockSpec(memory_space=pltpu.VMEM)
 FAR = pl.BlockSpec(memory_space=pltpu.HBM)
 CHEAP = pl.CostEstimate(flops=1, bytes_accessed=1, transcendentals=0)
@@ -24,8 +25,37 @@
     return (0.5 + 0.5 * tanh_u) * (1.0 + (1.0 - tanh_u) * slope)
 
 
-def hidden_cotangent(pre_values, out_values):
-    return (out_values.astype(F32) * gelu_slope(pre_values.astype(F32))).astype(BF)
+def hidden_kernel(pre_act, grad_out, out, pre_held, grad_held, sems):
+    width = out.shape[1] // LOADS
+    loads = []
+    for i in range(LOADS):
+        columns = pl.ds(i * width, width)
+        for j, (source, held) in enumerate(((pre_act, pre_held), (grad_out, grad_held))):
+            loads.append(pltpu.make_async_copy(source.at[:, columns], held.at[:, columns], sems.at[j, i]))
+            loads[-1].start()
+    for i in range(LOADS):
+        loads[2 * i].wait()
+        loads[2 * i + 1].wait()
+        for at in range(i * width, (i + 1) * width, 256):
+            columns = pl.ds(at, 256)
+            slope = gelu_slope(pre_held[:, columns].astype(F32))
+            out[:, columns] = (grad_held[:, columns].astype(F32) * slope).astype(BF)
+
+
+def hidden_cotangent(pre_act, grad_out):
+    shape = pre_act.shape
+    return pl.pallas_call(
+        hidden_kernel,
+        out_shape=pltpu.VMEM(shape, BF),
+        in_specs=[FAR, FAR],
+        out_specs=WHOLE,
+        scratch_shapes=[pltpu.VMEM(shape, BF), pltpu.VMEM(shape, BF), pltpu.SemaphoreType.DMA((2, LOADS))],
+        compiler_params=pltpu.CompilerParams(vmem_limit_bytes=8 * 2**20),
+        cost_estimate=CHEAP,
+    )(
+        pltpu.with_memory_space_constraint(pre_act, pltpu.HBM),
+        pltpu.with_memory_space_constraint(grad_out, pltpu.HBM),
+    )
 
 
 def move(array, step):

time: 80.9 us -> 80.7 us (level)
  other arithmetic: 3.18 us -> 0.88 us
  Pallas kernels: 28.6 us -> 30.6 us
    convert_element_type x1 -> x0, other arithmetic: 2.3 us -> none  [hidden_cotangent(): (out_values.astype(F32) * gelu_slope(pre_values.astype(F32))).astype(BF)]
    pallas_call x0 -> x1, Pallas kernels: none -> 2.02 us  [hidden_cotangent(): pl.pallas_call(hidden_kernel, out_shape=pltpu.VMEM(shape, BF), in_specs=[...]
where the time goes in v4:
time: 80.7 us; the launch traced here: 80.5 us
  Pallas kernels  30.6 us (38%)
  starting transfers between devices  25.6 us (32%)
  waiting for transfers between devices  22.7 us (28%)
  other arithmetic  0.88 us (1%)
    ppermute x19, starting transfers between devices, move(): return lax.ppermute(array, ('row', 'col'), pairs)  25.6 us
    ppermute x19, waiting for transfers between devices, move(): return lax.ppermute(array, ('row', 'col'), pairs)  22.7 us
    pallas_call x1, Pallas kernels, weight_cotangent(): pl.pallas_call(weight_kernel, grid=(units // tile,), out_shape=jax.ShapeD...  12 us
    pallas_call x4, Pallas kernels, partial_input(): pl.pallas_call(functools.partial(partial_kernel, keys, bool(outs)), out_s...  11 us
    pallas_call x1, Pallas kernels, fetch(): pl.pallas_call(fetch_kernel, out_shape=pltpu.VMEM(array.shape, array.dtyp...  3.69 us
    pallas_call x1, Pallas kernels, hidden_cotangent(): pl.pallas_call(hidden_kernel, out_shape=pltpu.VMEM(shape, BF), in_specs=[...  2.02 us
  transfers between devices with their start and end apart: 19, of which 8 were waited for; matrix products, arithmetic and copies ran while one was open for 0% of the time, Pallas kernels for 32%

profile of v4, /device:TPU:0, one launch (start us, length us, event | category | flops | bytes accessed | tf_op | source)
XLA Modules:
  0.0 80.5 jit_solution(12332284138042895967)
XLA Ops:
  0.6 2.0 %shard_map.59.refs_0_ = bf16[128,3072]{1,0:T(8,128)(2,1)S(1)} custom-call(bf16[128,3072]{1,0:T(8,128)(2,1)} %pre_act.1, bf16[128,3072]{1,0:T(8,128)(2,1)} %grad_out.1), custom_call_target="tpu_custom_call" | custom-call | flops 1 | bytes 1 | tf_op jit(solution)/shard_map/pallas_call | solution.py:47
  2.7 1.7 %collective-permute-start.1 = (bf16[2,64,3072]{2,1,0:T(8,128)(2,1)S(1)}, bf16[2,64,3072]{2,1,0:T(8,128)(2,1)S(1)}, u32[]{:S(2)}, u32[]{:S(2)}) collective-permute-start(bf16[2,64,3072]{2,1,0:T(8,128)(2,1)S(1)} %bitcast.12), channel_id=1, source_target_pairs={{0,2},{1,7},{2,4},{3,1},{4,6},{5,3},{6,0},{7,5},{8,10},{9,15},{10,... | collective-permute-start | bytes 2359304 | tf_op jit(solution)/shard_map/ppermute | solution.py:70
  4.4 1.0 %collective-permute-start = (bf16[2,64,3072]{2,1,0:T(8,128)(2,1)S(1)}, bf16[2,64,3072]{2,1,0:T(8,128)(2,1)S(1)}, u32[]{:S(2)}, u32[]{:S(2)}) collective-permute-start(bf16[2,64,3072]{2,1,0:T(8,128)(2,1)S(1)} %bitcast.13), channel_id=1, source_target_pairs={{0,1},{1,0},{2,3},{3,2},{4,5},{5,4},{6,7},{7,6},{8,9},{9,8},{10,11... | collective-permute-start | bytes 2359304 | tf_op jit(solution)/shard_map/ppermute | solution.py:70
  5.4 3.9 %collective-permute-start.3 = (bf16[64,1536]{1,0:T(8,128)(2,1)}, bf16[64,1536]{1,0:T(8,128)(2,1)S(1)}, u32[]{:S(2)}, u32[]{:S(2)}) collective-permute-start(bf16[64,1536]{1,0:T(8,128)(2,1)} %param.4), channel_id=1, source_target_pairs={{0,16},{1,65},{2,18},{3,67},{4,20},{5,69},{6,22},{7,71},{8,24},{9,... | collective-permute-start | bytes 589832 | tf_op jit(solution)/shard_map/ppermute | solution.py:70
  9.3 0.7 collective-permute-start.2
  10.0 1.3 %collective-permute-start.4 = (bf16[64,1536]{1,0:T(8,128)(2,1)}, bf16[64,1536]{1,0:T(8,128)(2,1)S(1)}, u32[]{:S(2)}, u32[]{:S(2)}) collective-permute-start(bf16[64,1536]{1,0:T(8,128)(2,1)} %param.4), channel_id=1, source_target_pairs={{0,8},{1,33},{2,10},{3,35},{4,12},{5,37},{6,14},{7,39},{8,16},{9,4... | collective-permute-start | bytes 589832 | tf_op jit(solution)/shard_map/ppermute | solution.py:70
  11.3 3.7 %shard_map.60.refs_2_ = bf16[1536,3072]{1,0:T(8,128)(2,1)S(1)} custom-call(bf16[1536,3072]{1,0:T(8,128)(2,1)} %source), custom_call_target="tpu_custom_call" | custom-call | flops 1 | bytes 1 | tf_op jit(solution)/shard_map/pallas_call | solution.py:113
  15.0 1.3 %collective-permute-done.2 = bf16[64,1536]{1,0:T(8,128)(2,1)S(1)} collective-permute-done((bf16[64,1536]{1,0:T(8,128)(2,1)}, bf16[64,1536]{1,0:T(8,128)(2,1)S(1)}, u32[]{:S(2)}, u32[]{:S(2)}) %collective-permute-start.2) | collective-permute-done | bytes 196640 | tf_op jit(solution)/shard_map/ppermute | solution.py:70
  16.3 0.8 collective-permute-done.4
  17.1 0.8 %collective-permute-start.8 = (bf16[2,64,3072]{2,1,0:T(8,128)(2,1)S(1)}, bf16[2,64,3072]{2,1,0:T(8,128)(2,1)S(1)}, u32[]{:S(2)}, u32[]{:S(2)}) collective-permute-start(bf16[2,64,3072]{2,1,0:T(8,128)(2,1)S(1)} %bitcast.14), channel_id=1, source_target_pairs={{0,6},{1,3},{2,0},{3,5},{4,2},{5,7},{6,4},{7,1},{8,14},{9,11},{10,... | collective-permute-start | bytes 2359304 | tf_op jit(solution)/shard_map/ppermute | solution.py:70
  17.9 1.2 %collective-permute-start.9 = (bf16[2,64,3072]{2,1,0:T(8,128)(2,1)S(1)}, bf16[2,64,3072]{2,1,0:T(8,128)(2,1)S(1)}, u32[]{:S(2)}, u32[]{:S(2)}) collective-permute-start(bf16[2,64,3072]{2,1,0:T(8,128)(2,1)S(1)} %collective-permute-done.1.refs_0_), channel_id=1, source_target_pairs={{0,2},{1,7},{2,4},{3,1},{4,6},{5,3},{6,0},{7,5},{8,10},{9,15},{10,... | collective-permute-start | bytes 2359304 | tf_op jit(solution)/shard_map/ppermute | solution.py:70
  19.3 2.8 %collective-permute-start.7 = (bf16[4,64,1536]{2,1,0:T(8,128)(2,1)S(1)}, bf16[4,64,1536]{2,1,0:T(8,128)(2,1)S(1)}, u32[]{:S(2)}, u32[]{:S(2)}) collective-permute-start(bf16[4,64,1536]{2,1,0:T(8,128)(2,1)S(1)} %pad_maximum_fusion.refs_0_), channel_id=1, source_target_pairs={{0,96},{1,25},{2,98},{3,27},{4,100},{5,29},{6,102},{7,31},{8,104},... | collective-permute-start | bytes 2359304 | tf_op jit(solution)/shard_map/ppermute | solution.py:70
  22.1 2.8 %shard_map.61 = (bf16[4,64,1536]{2,1,0:T(8,128)(2,1)S(1)}, bf16[4,64,1536]{2,1,0:T(8,128)(2,1)S(1)}, bf16[4,64,1536]{2,1,0:T(8,128)(2,1)S(1)}, bf16[4,64,1536]{2,1,0:T(8,128)(2,1)S(1)}) custom-call(bf16[2,64,3072]{2,1,0:T(8,128)(2,1)S(1)} %bitcast.15, bf16[2,64,3072]{2,1,0:T(8,128)(2,1)S(1)} %collective-permute-done.refs_1_, ...), custom_call_target="tpu_custom_call" | custom-call | flops 1 | bytes 1 | tf_op jit(solution)/shard_map/pallas_call | solution.py:158
  24.9 2.4 %collective-permute-start.5 = (bf16[4,64,1536]{2,1,0:T(8,128)(2,1)S(1)}, bf16[4,64,1536]{2,1,0:T(8,128)(2,1)S(1)}, u32[]{:S(2)}, u32[]{:S(2)}) collective-permute-start(bf16[4,64,1536]{2,1,0:T(8,128)(2,1)S(1)} %pad_maximum_fusion.refs_0_), channel_id=1, source_target_pairs={{0,64},{1,17},{2,66},{3,19},{4,68},{5,21},{6,70},{7,23},{8,72},{9,... | collective-permute-start | bytes 2359304 | tf_op jit(solution)/shard_map/ppermute | solution.py:70
  27.3 2.8 %shard_map.62 = (bf16[4,64,1536]{2,1,0:T(8,128)(2,1)S(1)}, bf16[4,64,1536]{2,1,0:T(8,128)(2,1)S(1)}, bf16[4,64,1536]{2,1,0:T(8,128)(2,1)S(1)}, bf16[4,64,1536]{2,1,0:T(8,128)(2,1)S(1)}) custom-call(bf16[2,64,3072]{2,1,0:T(8,128)(2,1)S(1)} %collective-permute-done.1.refs_0_, ...), custom_call_target="tpu_custom_call", output_to_operand_aliasing={{0}: (3, {}), {1}: (4, {}), {2}: (5, {}), {3}: (6, {})} | custom-call | flops 1 | bytes 1 | tf_op jit(solution)/shard_map/pallas_call | solution.py:158
  30.0 7.3 %collective-permute-done.8.refs_1_ = bf16[2,64,3072]{2,1,0:T(8,128)(2,1)S(1)} collective-permute-done((bf16[2,64,3072]{2,1,0:T(8,128)(2,1)S(1)}, bf16[2,64,3072]{2,1,0:T(8,128)(2,1)S(1)}, u32[]{:S(2)}, u32[]{:S(2)}) %collective-permute-start.8) | collective-permute-done | bytes 786464 | tf_op jit(solution)/shard_map/ppermute | solution.py:70
  37.3 0.9 %collective-permute-done.9.refs_0_ = bf16[2,64,3072]{2,1,0:T(8,128)(2,1)S(1)} collective-permute-done((bf16[2,64,3072]{2,1,0:T(8,128)(2,1)S(1)}, bf16[2,64,3072]{2,1,0:T(8,128)(2,1)S(1)}, u32[]{:S(2)}, u32[]{:S(2)}) %collective-permute-start.9) | collective-permute-done | bytes 786464 | tf_op jit(solution)/shard_map/ppermute | solution.py:70
  38.3 0.5 collective-permute-start.12
  38.8 2.8 %shard_map.63 = (bf16[4,64,1536]{2,1,0:T(8,128)(2,1)S(1)}, bf16[4,64,1536]{2,1,0:T(8,128)(2,1)S(1)}, bf16[4,64,1536]{2,1,0:T(8,128)(2,1)S(1)}, bf16[4,64,1536]{2,1,0:T(8,128)(2,1)S(1)}) custom-call(bf16[2,64,3072]{2,1,0:T(8,128)(2,1)S(1)} %collective-permute-done.9.refs_0_, ...), custom_call_target="tpu_custom_call", output_to_operand_aliasing={{0}: (3, {}), {1}: (4, {}), {2}: (5, {}), {3}: (6, {})} | custom-call | flops 1 | bytes 1 | tf_op jit(solution)/shard_map/pallas_call | solution.py:158
  41.5 2.2 %collective-permute-done.6.refs_3_ = bf16[4,64,1536]{2,1,0:T(8,128)(2,1)S(1)} collective-permute-done((bf16[4,64,1536]{2,1,0:T(8,128)(2,1)S(1)}, bf16[4,64,1536]{2,1,0:T(8,128)(2,1)S(1)}, u32[]{:S(2)}, u32[]{:S(2)}) %collective-permute-start.6) | collective-permute-done | bytes 786464 | tf_op jit(solution)/shard_map/ppermute | solution.py:70
  43.8 2.8 %shard_map.67 = (bf16[4,64,1536]{2,1,0:T(8,128)(2,1)S(1)}, bf16[4,64,1536]{2,1,0:T(8,128)(2,1)S(1)}, bf16[4,64,1536]{2,1,0:T(8,128)(2,1)S(1)}, bf16[4,64,1536]{2,1,0:T(8,128)(2,1)S(1)}) custom-call(bf16[2,64,3072]{2,1,0:T(8,128)(2,1)S(1)} %collective-permute-done.11.refs_0_, ...), custom_call_target="tpu_custom_call", output_to_operand_aliasing={{0}: (3, {}), {1}: (4, {}), {2}: (5, {}), {3}: (6, {})} | custom-call | flops 1 | bytes 1 | tf_op jit(solution)/shard_map/pallas_call | solution.py:158
  46.5 0.9 %collective-permute-start.13 = (bf16[4,64,1536]{2,1,0:T(8,128)(2,1)S(1)}, bf16[4,64,1536]{2,1,0:T(8,128)(2,1)S(1)}, u32[]{:S(2)}, u32[]{:S(2)}) collective-permute-start(bf16[4,64,1536]{2,1,0:T(8,128)(2,1)S(1)} %get-tuple-element.108), channel_id=1, source_target_pairs={{0,8},{1,33},{2,10},{3,35},{4,12},{5,37},{6,14},{7,39},{8,16},{9,4... | collective-permute-start | bytes 2359304 | tf_op jit(solution)/shard_map/ppermute | solution.py:70
  47.4 3.6 %collective-permute-start.14 = (bf16[4,64,1536]{2,1,0:T(8,128)(2,1)S(1)}, bf16[4,64,1536]{2,1,0:T(8,128)(2,1)S(1)}, u32[]{:S(2)}, u32[]{:S(2)}) collective-permute-start(bf16[4,64,1536]{2,1,0:T(8,128)(2,1)S(1)} %get-tuple-element.109), channel_id=1, source_target_pairs={{0,16},{1,65},{2,18},{3,67},{4,20},{5,69},{6,22},{7,71},{8,24},{9,... | collective-permute-start | bytes 2359304 | tf_op jit(solution)/shard_map/ppermute | solution.py:70
  51.0 1.0 %collective-permute-start.15 = (bf16[4,64,1536]{2,1,0:T(8,128)(2,1)S(1)}, bf16[4,64,1536]{2,1,0:T(8,128)(2,1)S(1)}, u32[]{:S(2)}, u32[]{:S(2)}) collective-permute-start(bf16[4,64,1536]{2,1,0:T(8,128)(2,1)S(1)} %get-tuple-element.110), channel_id=1, source_target_pairs={{0,24},{1,97},{2,26},{3,99},{4,28},{5,101},{6,30},{7,103},{8,0},{9... | collective-permute-start | bytes 2359304 | tf_op jit(solution)/shard_map/ppermute | solution.py:70
  52.0 1.5 %shard_map.65.inputs_t = bf16[1536,1024]{1,0:T(8,128)(2,1)S(1)} custom-call(bf16[4,64,1536]{2,1,0:T(8,128)(2,1)S(1)} %pad_maximum_fusion.refs_0_, bf16[4,64,1536]{2,1,0:T(8,128)(2,1)S(1)} %collective-permute-done.7.refs_1_, bf16[4,64,1536]{2,1,0:T(8,128)(2,1)S(1)} %shard_map.64.refs_2_, bf16[4,64,1536]{2,1,0:T(8,128)(2,1)S(1)} %collective-permute-done.6.refs_3_), custom_call_target="tpu_custom_call" | custom-call | flops 1 | bytes 1 | tf_op jit(solution)/shard_map/pallas_call | solution.py:218
  53.5 12.0 %shard_map.66 = bf16[1536,3072]{1,0:T(8,128)(2,1)} custom-call(bf16[1536,1024]{1,0:T(8,128)(2,1)S(1)} %shard_map.65.inputs_t, bf16[128,3072]{1,0:T(8,128)(2,1)S(1)} %shard_map.59.refs_0_, bf16[128,3072]{1,0:T(8,128)(2,1)S(1)} %bitcast.22, bf16[128,3072]{1,0:T(8,128)(2,1)S(1)} %bitcast.16, bf16[128,3072]{1,0:T(8,128)(2,1)S(1)} %bitcast.17, ...), custom_call_target="tpu_custom_call" | custom-call | flops 1 | bytes 1 | tf_op jit(solution)/shard_map/pallas_call | solution.py:240
  65.5 3.9 %collective-permute-done.14.refs_2_ = bf16[4,64,1536]{2,1,0:T(8,128)(2,1)S(1)} collective-permute-done((bf16[4,64,1536]{2,1,0:T(8,128)(2,1)S(1)}, bf16[4,64,1536]{2,1,0:T(8,128)(2,1)S(1)}, u32[]{:S(2)}, u32[]{:S(2)}) %collective-permute-start.14) | collective-permute-done | bytes 786464 | tf_op jit(solution)/shard_map/ppermute | solution.py:70
  69.8 2.2 %collective-permute-start.17 = (bf16[64,1536]{1,0:T(8,128)(2,1)S(1)}, bf16[64,1536]{1,0:T(8,128)(2,1)S(1)}, u32[]{:S(2)}, u32[]{:S(2)}) collective-permute-start(bf16[64,1536]{1,0:T(8,128)(2,1)S(1)} %get-tuple-element.117), channel_id=1, source_target_pairs={{0,64},{1,17},{2,66},{3,19},{4,68},{5,21},{6,70},{7,23},{8,72},{9,... | collective-permute-start | bytes 589832 | tf_op jit(solution)/shard_map/ppermute | solution.py:70
  72.0 1.4 %collective-permute-start.18 = (bf16[64,1536]{1,0:T(8,128)(2,1)S(1)}, bf16[64,1536]{1,0:T(8,128)(2,1)S(1)}, u32[]{:S(2)}, u32[]{:S(2)}) collective-permute-start(bf16[64,1536]{1,0:T(8,128)(2,1)S(1)} %get-tuple-element.118), channel_id=1, source_target_pairs={{0,96},{1,25},{2,98},{3,27},{4,100},{5,29},{6,102},{7,31},{8,104},... | collective-permute-start | bytes 589832 | tf_op jit(solution)/shard_map/ppermute | solution.py:70
  73.4 5.4 %collective-permute-done.16 = bf16[64,1536]{1,0:T(8,128)(2,1)S(1)} collective-permute-done((bf16[64,1536]{1,0:T(8,128)(2,1)S(1)}, bf16[64,1536]{1,0:T(8,128)(2,1)S(1)}, u32[]{:S(2)}, u32[]{:S(2)}) %collective-permute-start.16) | collective-permute-done | bytes 196640 | tf_op jit(solution)/shard_map/ppermute | solution.py:70
  78.8 0.9 %collective-permute-done.18 = bf16[64,1536]{1,0:T(8,128)(2,1)S(1)} collective-permute-done((bf16[64,1536]{1,0:T(8,128)(2,1)S(1)}, bf16[64,1536]{1,0:T(8,128)(2,1)S(1)}, u32[]{:S(2)}, u32[]{:S(2)}) %collective-permute-start.18) | collective-permute-done | bytes 196640 | tf_op jit(solution)/shard_map/ppermute | solution.py:70
  79.7 0.8 add_convert_fusion
  (20 shorter events, 0.6 us)
Async XLA Ops:
  2.7 16.5 %copy-start = (bf16[64,1536]{1,0:T(8,128)(2,1)S(1)}, bf16[64,1536]{1,0:T(8,128)(2,1)}, u32[]{:S(2)}) copy-start(bf16[64,1536]{1,0:T(8,128)(2,1)} %param.4) | copy-start | bytes 589828
  2.7 14.4 %collective-permute-start.1 = (bf16[2,64,3072]{2,1,0:T(8,128)(2,1)S(1)}, bf16[2,64,3072]{2,1,0:T(8,128)(2,1)S(1)}, u32[]{:S(2)}, u32[]{:S(2)}) collective-permute-start(bf16[2,64,3072]{2,1,0:T(8,128)(2,1)S(1)} %bitcast.12), channel_id=1, source_target_pairs={{0,2},{1,7},{2,4},{3,1},{4,6},{5,3},{6,0},{7,5},{8,10},{9,15},{10,... | collective-permute-start | bytes 2359304 | tf_op jit(solution)/shard_map/ppermute | solution.py:70
  4.4 12.7 %collective-permute-start = (bf16[2,64,3072]{2,1,0:T(8,128)(2,1)S(1)}, bf16[2,64,3072]{2,1,0:T(8,128)(2,1)S(1)}, u32[]{:S(2)}, u32[]{:S(2)}) collective-permute-start(bf16[2,64,3072]{2,1,0:T(8,128)(2,1)S(1)} %bitcast.13), channel_id=1, source_target_pairs={{0,1},{1,0},{2,3},{3,2},{4,5},{5,4},{6,7},{7,6},{8,9},{9,8},{10,11... | collective-permute-start | bytes 2359304 | tf_op jit(solution)/shard_map/ppermute | solution.py:70
  5.4 9.6 %collective-permute-start.3 = (bf16[64,1536]{1,0:T(8,128)(2,1)}, bf16[64,1536]{1,0:T(8,128)(2,1)S(1)}, u32[]{:S(2)}, u32[]{:S(2)}) collective-permute-start(bf16[64,1536]{1,0:T(8,128)(2,1)} %param.4), channel_id=1, source_target_pairs={{0,16},{1,65},{2,18},{3,67},{4,20},{5,69},{6,22},{7,71},{8,24},{9,... | collective-permute-start | bytes 589832 | tf_op jit(solution)/shard_map/ppermute | solution.py:70
  9.3 7.0 %collective-permute-start.2 = (bf16[64,1536]{1,0:T(8,128)(2,1)}, bf16[64,1536]{1,0:T(8,128)(2,1)S(1)}, u32[]{:S(2)}, u32[]{:S(2)}) collective-permute-start(bf16[64,1536]{1,0:T(8,128)(2,1)} %param.4), channel_id=1, source_target_pairs={{0,24},{1,97},{2,26},{3,99},{4,28},{5,101},{6,30},{7,103},{8,0},{9... | collective-permute-start | bytes 589832 | tf_op jit(solution)/shard_map/ppermute | solution.py:70
  10.0 7.1 %collective-permute-start.4 = (bf16[64,1536]{1,0:T(8,128)(2,1)}, bf16[64,1536]{1,0:T(8,128)(2,1)S(1)}, u32[]{:S(2)}, u32[]{:S(2)}) collective-permute-start(bf16[64,1536]{1,0:T(8,128)(2,1)} %param.4), channel_id=1, source_target_pairs={{0,8},{1,33},{2,10},{3,35},{4,12},{5,37},{6,14},{7,39},{8,16},{9,4... | collective-permute-start | bytes 589832 | tf_op jit(solution)/shard_map/ppermute | solution.py:70
  17.1 7.8 %collective-permute-start.10 = (bf16[2,64,3072]{2,1,0:T(8,128)(2,1)S(1)}, bf16[2,64,3072]{2,1,0:T(8,128)(2,1)S(1)}, u32[]{:S(2)}, u32[]{:S(2)}) collective-permute-start(bf16[2,64,3072]{2,1,0:T(8,128)(2,1)S(1)} %collective-permute-done.1.refs_0_), channel_id=1, source_target_pairs={{0,1},{1,0},{2,3},{3,2},{4,5},{5,4},{6,7},{7,6},{8,9},{9,8},{10,11... | collective-permute-start | bytes 2359304 | tf_op jit(solution)/shard_map/ppermute | solution.py:70
  17.1 20.3 %collective-permute-start.8 = (bf16[2,64,3072]{2,1,0:T(8,128)(2,1)S(1)}, bf16[2,64,3072]{2,1,0:T(8,128)(2,1)S(1)}, u32[]{:S(2)}, u32[]{:S(2)}) collective-permute-start(bf16[2,64,3072]{2,1,0:T(8,128)(2,1)S(1)} %bitcast.14), channel_id=1, source_target_pairs={{0,6},{1,3},{2,0},{3,5},{4,2},{5,7},{6,4},{7,1},{8,14},{9,11},{10,... | collective-permute-start | bytes 2359304 | tf_op jit(solution)/shard_map/ppermute | solution.py:70
  17.9 20.3 %collective-permute-start.9 = (bf16[2,64,3072]{2,1,0:T(8,128)(2,1)S(1)}, bf16[2,64,3072]{2,1,0:T(8,128)(2,1)S(1)}, u32[]{:S(2)}, u32[]{:S(2)}) collective-permute-start(bf16[2,64,3072]{2,1,0:T(8,128)(2,1)S(1)} %collective-permute-done.1.refs_0_), channel_id=1, source_target_pairs={{0,2},{1,7},{2,4},{3,1},{4,6},{5,3},{6,0},{7,5},{8,10},{9,15},{10,... | collective-permute-start | bytes 2359304 | tf_op jit(solution)/shard_map/ppermute | solution.py:70
  19.3 22.2 %collective-permute-start.7 = (bf16[4,64,1536]{2,1,0:T(8,128)(2,1)S(1)}, bf16[4,64,1536]{2,1,0:T(8,128)(2,1)S(1)}, u32[]{:S(2)}, u32[]{:S(2)}) collective-permute-start(bf16[4,64,1536]{2,1,0:T(8,128)(2,1)S(1)} %pad_maximum_fusion.refs_0_), channel_id=1, source_target_pairs={{0,96},{1,25},{2,98},{3,27},{4,100},{5,29},{6,102},{7,31},{8,104},... | collective-permute-start | bytes 2359304 | tf_op jit(solution)/shard_map/ppermute | solution.py:70
  22.1 21.6 %collective-permute-start.6 = (bf16[4,64,1536]{2,1,0:T(8,128)(2,1)S(1)}, bf16[4,64,1536]{2,1,0:T(8,128)(2,1)S(1)}, u32[]{:S(2)}, u32[]{:S(2)}) collective-permute-start(bf16[4,64,1536]{2,1,0:T(8,128)(2,1)S(1)} %pad_maximum_fusion.refs_0_), channel_id=1, source_target_pairs={{0,32},{1,9},{2,34},{3,11},{4,36},{5,13},{6,38},{7,15},{8,40},{9,1... | collective-permute-start | bytes 2359304 | tf_op jit(solution)/shard_map/ppermute | solution.py:70
  24.9 18.9 %collective-permute-start.5 = (bf16[4,64,1536]{2,1,0:T(8,128)(2,1)S(1)}, bf16[4,64,1536]{2,1,0:T(8,128)(2,1)S(1)}, u32[]{:S(2)}, u32[]{:S(2)}) collective-permute-start(bf16[4,64,1536]{2,1,0:T(8,128)(2,1)S(1)} %pad_maximum_fusion.refs_0_), channel_id=1, source_target_pairs={{0,64},{1,17},{2,66},{3,19},{4,68},{5,21},{6,70},{7,23},{8,72},{9,... | collective-permute-start | bytes 2359304 | tf_op jit(solution)/shard_map/ppermute | solution.py:70
  38.2 5.5 %collective-permute-start.11 = (bf16[2,64,3072]{2,1,0:T(8,128)(2,1)S(1)}, bf16[2,64,3072]{2,1,0:T(8,128)(2,1)S(1)}, u32[]{:S(2)}, u32[]{:S(2)}) collective-permute-start(bf16[2,64,3072]{2,1,0:T(8,128)(2,1)S(1)} %collective-permute-done.9.refs_0_), channel_id=1, source_target_pairs={{0,1},{1,0},{2,3},{3,2},{4,5},{5,4},{6,7},{7,6},{8,9},{9,8},{10,11... | collective-permute-start | bytes 2359304 | tf_op jit(solution)/shard_map/ppermute | solution.py:70
  38.3 5.5 %collective-permute-start.12 = (bf16[2,64,3072]{2,1,0:T(8,128)(2,1)S(1)}, bf16[2,64,3072]{2,1,0:T(8,128)(2,1)S(1)}, u32[]{:S(2)}, u32[]{:S(2)}) collective-permute-start(bf16[2,64,3072]{2,1,0:T(8,128)(2,1)S(1)} %collective-permute-done.8.refs_1_), channel_id=1, source_target_pairs={{0,1},{1,0},{2,3},{3,2},{4,5},{5,4},{6,7},{7,6},{8,9},{9,8},{10,11... | collective-permute-start | bytes 2359304 | tf_op jit(solution)/shard_map/ppermute | solution.py:70
  46.5 19.0 %collective-permute-start.13 = (bf16[4,64,1536]{2,1,0:T(8,128)(2,1)S(1)}, bf16[4,64,1536]{2,1,0:T(8,128)(2,1)S(1)}, u32[]{:S(2)}, u32[]{:S(2)}) collective-permute-start(bf16[4,64,1536]{2,1,0:T(8,128)(2,1)S(1)} %get-tuple-element.108), channel_id=1, source_target_pairs={{0,8},{1,33},{2,10},{3,35},{4,12},{5,37},{6,14},{7,39},{8,16},{9,4... | collective-permute-start | bytes 2359304 | tf_op jit(solution)/shard_map/ppermute | solution.py:70
  47.4 22.0 %collective-permute-start.14 = (bf16[4,64,1536]{2,1,0:T(8,128)(2,1)S(1)}, bf16[4,64,1536]{2,1,0:T(8,128)(2,1)S(1)}, u32[]{:S(2)}, u32[]{:S(2)}) collective-permute-start(bf16[4,64,1536]{2,1,0:T(8,128)(2,1)S(1)} %get-tuple-element.109), channel_id=1, source_target_pairs={{0,16},{1,65},{2,18},{3,67},{4,20},{5,69},{6,22},{7,71},{8,24},{9,... | collective-permute-start | bytes 2359304 | tf_op jit(solution)/shard_map/ppermute | solution.py:70
  51.0 18.4 %collective-permute-start.15 = (bf16[4,64,1536]{2,1,0:T(8,128)(2,1)S(1)}, bf16[4,64,1536]{2,1,0:T(8,128)(2,1)S(1)}, u32[]{:S(2)}, u32[]{:S(2)}) collective-permute-start(bf16[4,64,1536]{2,1,0:T(8,128)(2,1)S(1)} %get-tuple-element.110), channel_id=1, source_target_pairs={{0,24},{1,97},{2,26},{3,99},{4,28},{5,101},{6,30},{7,103},{8,0},{9... | collective-permute-start | bytes 2359304 | tf_op jit(solution)/shard_map/ppermute | solution.py:70
  69.8 9.1 %collective-permute-start.16 = (bf16[64,1536]{1,0:T(8,128)(2,1)S(1)}, bf16[64,1536]{1,0:T(8,128)(2,1)S(1)}, u32[]{:S(2)}, u32[]{:S(2)}) collective-permute-start(bf16[64,1536]{1,0:T(8,128)(2,1)S(1)} %get-tuple-element.116), channel_id=1, source_target_pairs={{0,32},{1,9},{2,34},{3,11},{4,36},{5,13},{6,38},{7,15},{8,40},{9,1... | collective-permute-start | bytes 589832 | tf_op jit(solution)/shard_map/ppermute | solution.py:70
  69.8 9.0 %collective-permute-start.17 = (bf16[64,1536]{1,0:T(8,128)(2,1)S(1)}, bf16[64,1536]{1,0:T(8,128)(2,1)S(1)}, u32[]{:S(2)}, u32[]{:S(2)}) collective-permute-start(bf16[64,1536]{1,0:T(8,128)(2,1)S(1)} %get-tuple-element.117), channel_id=1, source_target_pairs={{0,64},{1,17},{2,66},{3,19},{4,68},{5,21},{6,70},{7,23},{8,72},{9,... | collective-permute-start | bytes 589832 | tf_op jit(solution)/shard_map/ppermute | solution.py:70
  72.0 7.7 %collective-permute-start.18 = (bf16[64,1536]{1,0:T(8,128)(2,1)S(1)}, bf16[64,1536]{1,0:T(8,128)(2,1)S(1)}, u32[]{:S(2)}, u32[]{:S(2)}) collective-permute-start(bf16[64,1536]{1,0:T(8,128)(2,1)S(1)} %get-tuple-element.118), channel_id=1, source_target_pairs={{0,96},{1,25},{2,98},{3,27},{4,100},{5,29},{6,102},{7,31},{8,104},... | collective-permute-start | bytes 589832 | tf_op jit(solution)/shard_map/ppermute | solution.py:70

commit v5 on v4

--- a/solution.py
+++ b/solution.py
@@ -132,8 +132,8 @@
 
 def partial_kernel(keys, has_outs, *refs):
     blocks, weight = refs[: len(keys)], refs[len(keys)]
-    outs, found = refs[-1 - SIDE : -1], refs[-1]
-    tokens = outs[0].shape[1]
+    own, up, down, up_rest, down_rest, found = refs[-6:]
+    tokens = own.shape[1]
     hidden = jnp.concatenate([block[...].reshape(2 * tokens, -1) for block in blocks])
     for d in range(0, weight.shape[0], TILE):
         found[:, d : d + TILE] = lax.dot_general(
@@ -143,11 +143,23 @@
         for h in range(2):
             n_off, f_off = block_offset(*key, h)
             at = (2 * i + h) * tokens
-            for k in range(SIDE):
-
-                @pl.when(n_off == k)
+            low = f_off < 2
+            for k, is_low, out, *index in (
+                (1, True, up_rest, f_off),
+                (1, False, up, 1, f_off - 2),
+                (2, True, up, 0, f_off),
+                (2, False, down, 0, f_off - 2),
+                (3, True, down, 1, f_off),
+                (3, False, down_rest, f_off - 2),
+            ):
+
+                @pl.when((n_off == k) & (low if is_low else ~low))
                 def _():
-                    outs[k][f_off] = found[at : at + tokens, :]
+                    out[tuple(index)] = found[at : at + tokens, :]
+
+            @pl.when(n_off == 0)
+            def _():
+                own[f_off] = found[at : at + tokens, :]
 
 
 def partial_input(keys, pieces, weight, outs):
@@ -157,9 +169,11 @@
     return list(
         pl.pallas_call(
             functools.partial(partial_kernel, keys, bool(outs)),
-            out_shape=[pltpu.VMEM((SIDE, tokens, weight.shape[0]), BF)] * SIDE,
+            out_shape=[
+                pltpu.VMEM((*lead, tokens, weight.shape[0]), BF) for lead in ((4,), (2, 2), (2, 2), (2,), (2,))
+            ],
             in_specs=[WHOLE] * (first + len(outs)),
-            out_specs=[WHOLE] * SIDE,
+            out_specs=[WHOLE] * 5,
             scratch_shapes=[pltpu.VMEM((2 * tokens * len(blocks), weight.shape[0]), BF)],
             input_output_aliases={first + i: i for i in range(len(outs))},
             compiler_params=pltpu.CompilerParams(vmem_limit_bytes=16 * 2**20),
@@ -168,25 +182,28 @@
     )
 
 
-def sum_kernel(*refs):
-    terms, outs = refs[:SIDE], refs[SIDE:]
-    for k in range(len(outs)):
-        total = terms[0][k].astype(F32)
-        for term in terms[1:]:
-            total += term[k].astype(F32)
-        outs[k][...] = total.astype(BF)
-
-
-def sum_terms(terms):
-    shape = terms[0].shape
-    return pl.pallas_call(
-        sum_kernel,
-        out_shape=[pltpu.VMEM(shape[1:], BF)] * shape[0],
-        in_specs=[WHOLE] * len(terms),
-        out_specs=[WHOLE] * shape[0],
+def rest_kernel(up_rest, down_rest, from_below, from_above, up, down):
+    for rest, share, out in ((up_rest, from_below, up), (down_rest, from_above, down)):
+        for i in range(2):
+            out[i] = (rest[i].astype(F32) + share[0, i].astype(F32)).astype(BF)
+
+
+def sum_kernel(own, from_below, from_above, last_below, last_above, *outs):
+    for f in range(SIDE):
+        direct, rest = (from_above, last_below) if f < 2 else (from_below, last_above)
+        total = own[f].astype(F32) + direct[1, f % 2].astype(F32) + rest[f % 2].astype(F32)
+        outs[f][...] = total.astype(BF)
+
+
+def in_vmem(kernel, shapes, *operands):
+    return pl.pallas_call(
+        kernel,
+        out_shape=[pltpu.VMEM(shape, BF) for shape in shapes],
+        in_specs=[WHOLE] * len(operands),
+        out_specs=[WHOLE] * len(shapes),
         compiler_params=pltpu.CompilerParams(vmem_limit_bytes=6 * 2**20),
         cost_estimate=CHEAP,
-    )(*terms)
+    )(*operands)
 
 
 def last_sum(terms):
@@ -226,26 +243,27 @@
     )(*blocks)
 
 
-def weight_kernel(inputs_t, *refs):
-    pieces, out = refs[:-1], refs[-1]
+def weight_kernel(first, inputs_t, *refs):
+    out = refs[-1]
     tile = out.shape[1]
-    columns = pl.ds(pl.multiple_of(pl.program_id(0) * tile, tile), tile)
-    hidden = jnp.concatenate([piece[:, columns] for piece in pieces])
+    columns = pl.ds(pl.multiple_of((first + pl.program_id(0)) * tile, tile), tile)
+    hidden = jnp.concatenate([piece[:, columns] for piece in refs[:8]])
     out[...] = jnp.dot(inputs_t[...], hidden, preferred_element_type=F32).astype(BF)
 
 
-def weight_cotangent(inputs_t, pieces, tile=512):
+def weight_cotangent(inputs_t, pieces, first, count, done, tile=512):
     wide, units = inputs_t.shape[0], pieces[0].shape[-1]
     pieces = [piece.reshape(-1, units) for piece in pieces]
     return pl.pallas_call(
-        weight_kernel,
-        grid=(units // tile,),
+        functools.partial(weight_kernel, first),
+        grid=(count,),
         out_shape=jax.ShapeDtypeStruct((wide, units), BF),
-        in_specs=[WHOLE] * (1 + len(pieces)),
-        out_specs=pl.BlockSpec((wide, tile), lambda i: (0, i)),
+        in_specs=[WHOLE] * (1 + len(pieces)) + [FAR] * len(done),
+        out_specs=pl.BlockSpec((wide, tile), lambda i: (0, first + i)),
+        input_output_aliases={1 + len(pieces): 0} if done else {},
         compiler_params=pltpu.CompilerParams(vmem_limit_bytes=18 * 2**20),
         cost_estimate=CHEAP,
-    )(inputs_t, *pieces)
+    )(inputs_t, *pieces, *done)
 
 
 def on_device(inputs, pre_act, grad_out, weight):
@@ -279,13 +297,22 @@
     swap2, swap3, gathered[2], *outs = barrier((swap2, swap3, gathered[2], *outs))
     pieces |= {(2, True): swap2, (3, True): swap3}
     outs = partial_input([(2, True), (3, True)], pieces, held_weight, outs)
-    terms = [outs[0]] + [near(outs[k], k) for k in (1, 2, 3)]
+    own, up, down, up_rest, down_rest = outs
+    from_below, from_above = near(up, 1), near(down, -1)
 
     inputs_t = transposed_inputs(list(pieces), [gathered[k] for k in range(SIDE)])
-    grad_weight = weight_cotangent(inputs_t, list(pieces.values()))
+    pieces = list(pieces.values())
+    grad_weight = weight_cotangent(inputs_t, pieces, 0, 3, [])
+    grad_weight, from_below, from_above = barrier((grad_weight, from_below, from_above))
+    up, down = in_vmem(rest_kernel, [up_rest.shape] * 2, up_rest, down_rest, from_below, from_above)
+    last_below, last_above = near(up, 1), near(down, -1)
+    grad_weight = weight_cotangent(inputs_t, pieces, 3, 2, [grad_weight])
+    grad_weight, last_below, last_above = barrier((grad_weight, last_below, last_above))
+    sums = in_vmem(sum_kernel, [own.shape[1:]] * SIDE, own, from_below, from_above, last_below, last_above)
+    terms = [sums[0]] + [far(sums[k], k) for k in (1, 2, 3)]
+    grad_weight = weight_cotangent(inputs_t, pieces, 5, 1, [grad_weight])
     grad_weight, *terms = barrier((grad_weight, *terms))
-    sums = sum_terms(terms)
-    grad_input = last_sum([sums[0]] + [far(sums[k], k) for k in (1, 2, 3)])
+    grad_input = last_sum(terms)
     return (grad_input, grad_weight)
 
 

time: 80.7 us -> 80.6 us (level)
  waiting for transfers between devices: 22.7 us -> 18.7 us
  Pallas kernels: 30.6 us -> 33.3 us
  starting transfers between devices: 25.6 us -> 26.8 us
    ppermute x19 -> x20, waiting for transfers between devices: 22.7 us -> 18.7 us  [move(): return lax.ppermute(array, ('row', 'col'), pairs)]
    pallas_call x2 -> x5, Pallas kernels: 12.4 us -> 14.7 us  [the longest x3 14.3 us: weight_cotangent(): pl.pallas_call(functools.partial(weight_kernel, first), grid=(count,), ou...]
    ppermute x19 -> x20, starting transfers between devices: 25.6 us -> 26.8 us  [move(): return lax.ppermute(array, ('row', 'col'), pairs)]
  transfers between devices with their start and end apart: 19 -> 20, of which waited for: 8 -> 10; matrix products, arithmetic and copies ran while one was open for 0% -> 0% of each run, Pallas kernels for 32% -> 35%
where the time goes in v5:
time: 80.6 us; the launch traced here: 80.4 us
  Pallas kernels  33.3 us (41%)
  starting transfers between devices  26.8 us (33%)
  waiting for transfers between devices  18.7 us (23%)
  other arithmetic  0.88 us (1%)
    ppermute x20, starting transfers between devices, move(): return lax.ppermute(array, ('row', 'col'), pairs)  26.8 us
    ppermute x20, waiting for transfers between devices, move(): return lax.ppermute(array, ('row', 'col'), pairs)  18.7 us
    pallas_call x3, Pallas kernels, weight_cotangent(): pl.pallas_call(functools.partial(weight_kernel, first), grid=(count,), ou...  14.3 us
    pallas_call x4, Pallas kernels, partial_input(): pl.pallas_call(functools.partial(partial_kernel, keys, bool(outs)), out_s...  11.3 us
    pallas_call x1, Pallas kernels, fetch(): pl.pallas_call(fetch_kernel, out_shape=pltpu.VMEM(array.shape, array.dtyp...  3.69 us
    pallas_call x1, Pallas kernels, hidden_cotangent(): pl.pallas_call(hidden_kernel, out_shape=pltpu.VMEM(shape, BF), in_specs=[...  2.02 us
  transfers between devices with their start and end apart: 20, of which 10 were waited for; matrix products, arithmetic and copies ran while one was open for 0% of the time, Pallas kernels for 35%

profile of v5, /device:TPU:0, one launch (start us, length us, event | category | flops | bytes accessed | tf_op | source)
XLA Modules:
  0.0 80.4 jit_solution(4069683432903363168)
XLA Ops:
  0.6 2.0 %shard_map.59.refs_0_ = bf16[128,3072]{1,0:T(8,128)(2,1)S(1)} custom-call(bf16[128,3072]{1,0:T(8,128)(2,1)} %pre_act.1, bf16[128,3072]{1,0:T(8,128)(2,1)} %grad_out.1), custom_call_target="tpu_custom_call" | custom-call | flops 1 | bytes 1 | tf_op jit(solution)/shard_map/pallas_call | solution.py:47
  2.7 1.7 %collective-permute-start.1 = (bf16[2,64,3072]{2,1,0:T(8,128)(2,1)S(1)}, bf16[2,64,3072]{2,1,0:T(8,128)(2,1)S(1)}, u32[]{:S(2)}, u32[]{:S(2)}) collective-permute-start(bf16[2,64,3072]{2,1,0:T(8,128)(2,1)S(1)} %bitcast.12), channel_id=1, source_target_pairs={{0,2},{1,7},{2,4},{3,1},{4,6},{5,3},{6,0},{7,5},{8,10},{9,15},{10,... | collective-permute-start | bytes 2359304 | tf_op jit(solution)/shard_map/ppermute | solution.py:70
  4.4 1.0 %collective-permute-start = (bf16[2,64,3072]{2,1,0:T(8,128)(2,1)S(1)}, bf16[2,64,3072]{2,1,0:T(8,128)(2,1)S(1)}, u32[]{:S(2)}, u32[]{:S(2)}) collective-permute-start(bf16[2,64,3072]{2,1,0:T(8,128)(2,1)S(1)} %bitcast.13), channel_id=1, source_target_pairs={{0,1},{1,0},{2,3},{3,2},{4,5},{5,4},{6,7},{7,6},{8,9},{9,8},{10,11... | collective-permute-start | bytes 2359304 | tf_op jit(solution)/shard_map/ppermute | solution.py:70
  5.4 3.9 %collective-permute-start.3 = (bf16[64,1536]{1,0:T(8,128)(2,1)}, bf16[64,1536]{1,0:T(8,128)(2,1)S(1)}, u32[]{:S(2)}, u32[]{:S(2)}) collective-permute-start(bf16[64,1536]{1,0:T(8,128)(2,1)} %param.4), channel_id=1, source_target_pairs={{0,16},{1,65},{2,18},{3,67},{4,20},{5,69},{6,22},{7,71},{8,24},{9,... | collective-permute-start | bytes 589832 | tf_op jit(solution)/shard_map/ppermute | solution.py:70
  10.0 1.3 %collective-permute-start.4 = (bf16[64,1536]{1,0:T(8,128)(2,1)}, bf16[64,1536]{1,0:T(8,128)(2,1)S(1)}, u32[]{:S(2)}, u32[]{:S(2)}) collective-permute-start(bf16[64,1536]{1,0:T(8,128)(2,1)} %param.4), channel_id=1, source_target_pairs={{0,8},{1,33},{2,10},{3,35},{4,12},{5,37},{6,14},{7,39},{8,16},{9,4... | collective-permute-start | bytes 589832 | tf_op jit(solution)/shard_map/ppermute | solution.py:70
  11.3 3.7 %shard_map.60.refs_2_ = bf16[1536,3072]{1,0:T(8,128)(2,1)S(1)} custom-call(bf16[1536,3072]{1,0:T(8,128)(2,1)} %source), custom_call_target="tpu_custom_call" | custom-call | flops 1 | bytes 1 | tf_op jit(solution)/shard_map/pallas_call | solution.py:113
  15.0 1.3 %collective-permute-done.2 = bf16[64,1536]{1,0:T(8,128)(2,1)S(1)} collective-permute-done((bf16[64,1536]{1,0:T(8,128)(2,1)}, bf16[64,1536]{1,0:T(8,128)(2,1)S(1)}, u32[]{:S(2)}, u32[]{:S(2)}) %collective-permute-start.2) | collective-permute-done | bytes 196640 | tf_op jit(solution)/shard_map/ppermute | solution.py:70
  17.1 0.8 %collective-permute-start.8 = (bf16[2,64,3072]{2,1,0:T(8,128)(2,1)S(1)}, bf16[2,64,3072]{2,1,0:T(8,128)(2,1)S(1)}, u32[]{:S(2)}, u32[]{:S(2)}) collective-permute-start(bf16[2,64,3072]{2,1,0:T(8,128)(2,1)S(1)} %bitcast.14), channel_id=1, source_target_pairs={{0,6},{1,3},{2,0},{3,5},{4,2},{5,7},{6,4},{7,1},{8,14},{9,11},{10,... | collective-permute-start | bytes 2359304 | tf_op jit(solution)/shard_map/ppermute | solution.py:70
  17.9 1.2 %collective-permute-start.9 = (bf16[2,64,3072]{2,1,0:T(8,128)(2,1)S(1)}, bf16[2,64,3072]{2,1,0:T(8,128)(2,1)S(1)}, u32[]{:S(2)}, u32[]{:S(2)}) collective-permute-start(bf16[2,64,3072]{2,1,0:T(8,128)(2,1)S(1)} %collective-permute-done.1.refs_0_), channel_id=1, source_target_pairs={{0,2},{1,7},{2,4},{3,1},{4,6},{5,3},{6,0},{7,5},{8,10},{9,15},{10,... | collective-permute-start | bytes 2359304 | tf_op jit(solution)/shard_map/ppermute | solution.py:70
  19.3 2.8 %collective-permute-start.7 = (bf16[4,64,1536]{2,1,0:T(8,128)(2,1)S(1)}, bf16[4,64,1536]{2,1,0:T(8,128)(2,1)S(1)}, u32[]{:S(2)}, u32[]{:S(2)}) collective-permute-start(bf16[4,64,1536]{2,1,0:T(8,128)(2,1)S(1)} %pad_maximum_fusion.refs_0_), channel_id=1, source_target_pairs={{0,96},{1,25},{2,98},{3,27},{4,100},{5,29},{6,102},{7,31},{8,104},... | collective-permute-start | bytes 2359304 | tf_op jit(solution)/shard_map/ppermute | solution.py:70
  22.1 2.8 %shard_map.61 = (bf16[4,64,1536]{2,1,0:T(8,128)(2,1)S(1)}, bf16[2,2,64,1536]{3,2,1,0:T(8,128)(2,1)S(1)}, bf16[2,2,64,1536]{3,2,1,0:T(8,128)(2,1)S(1)}, bf16[2,64...) custom-call(bf16[2,64,3072]{2,1,0:T(8,128)(2,1)S(1)} %bitcast.15, bf16[2,64,3072]{2,1,0:T(8,128)(2,1)S(1)} %collective-permute-done.refs_1_, ...), custom_call_target="tpu_custom_call" | custom-call | flops 1 | bytes 1 | tf_op jit(solution)/shard_map/pallas_call | solution.py:170
  25.0 2.4 %collective-permute-start.5 = (bf16[4,64,1536]{2,1,0:T(8,128)(2,1)S(1)}, bf16[4,64,1536]{2,1,0:T(8,128)(2,1)S(1)}, u32[]{:S(2)}, u32[]{:S(2)}) collective-permute-start(bf16[4,64,1536]{2,1,0:T(8,128)(2,1)S(1)} %pad_maximum_fusion.refs_0_), channel_id=1, source_target_pairs={{0,64},{1,17},{2,66},{3,19},{4,68},{5,21},{6,70},{7,23},{8,72},{9,... | collective-permute-start | bytes 2359304 | tf_op jit(solution)/shard_map/ppermute | solution.py:70
  27.3 2.8 %shard_map.62 = (bf16[4,64,1536]{2,1,0:T(8,128)(2,1)S(1)}, bf16[2,2,64,1536]{3,2,1,0:T(8,128)(2,1)S(1)}, bf16[2,2,64,1536]{3,2,1,0:T(8,128)(2,1)S(1)}, bf16[2,64...) custom-call(bf16[2,64,3072]{2,1,0:T(8,128)(2,1)S(1)} %collective-per, ...), custom_call_target="tpu_custom_call", output_to_operand_aliasing={{0}: (3, {}), {1}: (4, {}), {2}: (5, {}), {3}: (6, {}), {4}... | custom-call | flops 1 | bytes 1 | tf_op jit(solution)/shard_map/pallas_call | solution.py:170
  30.2 7.2 %collective-permute-done.8.refs_1_ = bf16[2,64,3072]{2,1,0:T(8,128)(2,1)S(1)} collective-permute-done((bf16[2,64,3072]{2,1,0:T(8,128)(2,1)S(1)}, bf16[2,64,3072]{2,1,0:T(8,128)(2,1)S(1)}, u32[]{:S(2)}, u32[]{:S(2)}) %collective-permute-start.8) | collective-permute-done | bytes 786464 | tf_op jit(solution)/shard_map/ppermute | solution.py:70
  37.3 0.9 %collective-permute-done.9.refs_0_ = bf16[2,64,3072]{2,1,0:T(8,128)(2,1)S(1)} collective-permute-done((bf16[2,64,3072]{2,1,0:T(8,128)(2,1)S(1)}, bf16[2,64,3072]{2,1,0:T(8,128)(2,1)S(1)}, u32[]{:S(2)}, u32[]{:S(2)}) %collective-permute-start.9) | collective-permute-done | bytes 786464 | tf_op jit(solution)/shard_map/ppermute | solution.py:70
  38.8 2.8 %shard_map.63 = (bf16[4,64,1536]{2,1,0:T(8,128)(2,1)S(1)}, bf16[2,2,64,1536]{3,2,1,0:T(8,128)(2,1)S(1)}, bf16[2,2,64,1536]{3,2,1,0:T(8,128)(2,1)S(1)}, bf16[2,64...) custom-call(bf16[2,64,3072]{2,1,0:T(8,128)(2,1)S(1)} %collective-per, ...), custom_call_target="tpu_custom_call", output_to_operand_aliasing={{0}: (3, {}), {1}: (4, {}), {2}: (5, {}), {3}: (6, {}), {4}... | custom-call | flops 1 | bytes 1 | tf_op jit(solution)/shard_map/pallas_call | solution.py:170
  41.6 2.1 %collective-permute-done.6.refs_3_ = bf16[4,64,1536]{2,1,0:T(8,128)(2,1)S(1)} collective-permute-done((bf16[4,64,1536]{2,1,0:T(8,128)(2,1)S(1)}, bf16[4,64,1536]{2,1,0:T(8,128)(2,1)S(1)}, u32[]{:S(2)}, u32[]{:S(2)}) %collective-permute-start.6) | collective-permute-done | bytes 786464 | tf_op jit(solution)/shard_map/ppermute | solution.py:70
  43.8 2.8 %shard_map.67 = (bf16[4,64,1536]{2,1,0:T(8,128)(2,1)S(1)}, bf16[2,2,64,1536]{3,2,1,0:T(8,128)(2,1)S(1)}, bf16[2,2,64,1536]{3,2,1,0:T(8,128)(2,1)S(1)}, bf16[2,64...) custom-call(bf16[2,64,3072]{2,1,0:T(8,128)(2,1)S(1)} %collective-per, ...), custom_call_target="tpu_custom_call", output_to_operand_aliasing={{0}: (3, {}), {1}: (4, {}), {2}: (5, {}), {3}: (6, {}), {4}... | custom-call | flops 1 | bytes 1 | tf_op jit(solution)/shard_map/pallas_call | solution.py:170
  46.6 0.9 %collective-permute-start.13 = (bf16[2,2,64,1536]{3,2,1,0:T(8,128)(2,1)S(1)}, bf16[2,2,64,1536]{3,2,1,0:T(8,128)(2,1)S(1)}, u32[]{:S(2)}, u32[]{:S(2)}) collective-permute-start(bf16[2,2,64,1536]{3,2,1,0:T(8,128)(2,1)S(1)} %get-tuple-element.130), channel_id=1, source_target_pairs={{0,8},{1,33},{2,10},{3,35},{4,12},{5,37},{6,14},{7,39},{8,16},{9,4... | collective-permute-start | bytes 2359304 | tf_op jit(solution)/shard_map/ppermute | solution.py:70
  47.5 2.4 %collective-permute-start.14 = (bf16[2,2,64,1536]{3,2,1,0:T(8,128)(2,1)S(1)}, bf16[2,2,64,1536]{3,2,1,0:T(8,128)(2,1)S(1)}, u32[]{:S(2)}, u32[]{:S(2)}) collective-permute-start(bf16[2,2,64,1536]{3,2,1,0:T(8,128)(2,1)S(1)} %get-tuple-element.131), channel_id=1, source_target_pairs={{0,24},{1,97},{2,26},{3,99},{4,28},{5,101},{6,30},{7,103},{8,0},{9... | collective-permute-start | bytes 2359304 | tf_op jit(solution)/shard_map/ppermute | solution.py:70
  49.9 1.5 %shard_map.65.inputs_t = bf16[1536,1024]{1,0:T(8,128)(2,1)S(1)} custom-call(bf16[4,64,1536]{2,1,0:T(8,128)(2,1)S(1)} %pad_maximum_fusion.refs_0_, bf16[4,64,1536]{2,1,0:T(8,128)(2,1)S(1)} %collective-permute-done.7.refs_1_, bf16[4,64,1536]{2,1,0:T(8,128)(2,1)S(1)} %shard_map.64.refs_2_, bf16[4,64,1536]{2,1,0:T(8,128)(2,1)S(1)} %collective-permute-done.6.refs_3_), custom_call_target="tpu_custom_call" | custom-call | flops 1 | bytes 1 | tf_op jit(solution)/shard_map/pallas_call | solution.py:235
  51.4 6.6 %shard_map.66.refs_8_ = bf16[1536,3072]{1,0:T(8,128)(2,1)} custom-call(bf16[1536,1024]{1,0:T(8,128)(2,1)S(1)} %shard_map.65.inputs_t, bf16[128,3072]{1,0:T(8,128)(2,1)S(1)} %shard_map.59.refs_0_, bf16[128,3072]{1,0:T(8,128)(2,1)S(1)} %bitcast.34, bf16[128,3072]{1,0:T(8,128)(2,1)S(1)} %bitcast.16, bf16[128,3072]{1,0:T(8,128)(2,1)S(1)} %bitcast.19, ...), custom_call_target="tpu_custom_call" | custom-call | flops 1 | bytes 1 | tf_op jit(solution)/shard_map/pallas_call | solution.py:257
  58.0 1.9 %collective-permute-done.13.from_below = bf16[2,2,64,1536]{3,2,1,0:T(8,128)(2,1)S(1)} collective-permute-done((bf16[2,2,64,1536]{3,2,1,0:T(8,128)(2,1)S(1)}, bf16[2,2,64,1536]{3,2,1,0:T(8,128)(2,1)S(1)}, u32[]{:S(2)}, u32[]{:S(2)}) %collective-permute-start.13) | collective-permute-done | bytes 786464 | tf_op jit(solution)/shard_map/ppermute | solution.py:70
  60.1 1.6 %collective-permute-start.15 = (bf16[2,64,1536]{2,1,0:T(8,128)(2,1)S(1)}, bf16[2,64,1536]{2,1,0:T(8,128)(2,1)S(1)}, u32[]{:S(2)}, u32[]{:S(2)}) collective-permute-start(bf16[2,64,1536]{2,1,0:T(8,128)(2,1)S(1)} %get-tuple-element.137), channel_id=1, source_target_pairs={{0,8},{1,33},{2,10},{3,35},{4,12},{5,37},{6,14},{7,39},{8,16},{9,4... | collective-permute-start | bytes 1179656 | tf_op jit(solution)/shard_map/ppermute | solution.py:70
  61.6 1.8 %collective-permute-start.16 = (bf16[2,64,1536]{2,1,0:T(8,128)(2,1)S(1)}, bf16[2,64,1536]{2,1,0:T(8,128)(2,1)S(1)}, u32[]{:S(2)}, u32[]{:S(2)}) collective-permute-start(bf16[2,64,1536]{2,1,0:T(8,128)(2,1)S(1)} %get-tuple-element.138), channel_id=1, source_target_pairs={{0,24},{1,97},{2,26},{3,99},{4,28},{5,101},{6,30},{7,103},{8,0},{9... | collective-permute-start | bytes 1179656 | tf_op jit(solution)/shard_map/ppermute | solution.py:70
  63.4 4.8 %shard_map.68.refs_8_ = bf16[1536,3072]{1,0:T(8,128)(2,1)} custom-call(bf16[1536,1024]{1,0:T(8,128)(2,1)S(1)} %shard_map.65.inputs_t, bf16[128,3072]{1,0:T(8,128)(2,1)S(1)} %shard_map.59.refs_0_, bf16[128,3072]{1,0:T(8,128)(2,1)S(1)} %bitcast.35, bf16[128,3072]{1,0:T(8,128)(2,1)S(1)} %bitcast.17, ...), custom_call_target="tpu_custom_call", output_to_operand_aliasing={{}: (9, {})} | custom-call | flops 1 | bytes 1 | tf_op jit(solution)/shard_map/pallas_call | solution.py:257
  68.2 0.9 %collective-permute-done.15.last_below = bf16[2,64,1536]{2,1,0:T(8,128)(2,1)S(1)} collective-permute-done((bf16[2,64,1536]{2,1,0:T(8,128)(2,1)S(1)}, bf16[2,64,1536]{2,1,0:T(8,128)(2,1)S(1)}, u32[]{:S(2)}, u32[]{:S(2)}) %collective-permute-start.15) | collective-permute-done | bytes 393248 | tf_op jit(solution)/shard_map/ppermute | solution.py:70
  69.8 2.2 %collective-permute-start.18 = (bf16[64,1536]{1,0:T(8,128)(2,1)S(1)}, bf16[64,1536]{1,0:T(8,128)(2,1)S(1)}, u32[]{:S(2)}, u32[]{:S(2)}) collective-permute-start(bf16[64,1536]{1,0:T(8,128)(2,1)S(1)} %get-tuple-element.145), channel_id=1, source_target_pairs={{0,64},{1,17},{2,66},{3,19},{4,68},{5,21},{6,70},{7,23},{8,72},{9,... | collective-permute-start | bytes 589832 | tf_op jit(solution)/shard_map/ppermute | solution.py:70
  72.0 1.4 %collective-permute-start.19 = (bf16[64,1536]{1,0:T(8,128)(2,1)S(1)}, bf16[64,1536]{1,0:T(8,128)(2,1)S(1)}, u32[]{:S(2)}, u32[]{:S(2)}) collective-permute-start(bf16[64,1536]{1,0:T(8,128)(2,1)S(1)} %get-tuple-element.146), channel_id=1, source_target_pairs={{0,96},{1,25},{2,98},{3,27},{4,100},{5,29},{6,102},{7,31},{8,104},... | collective-permute-start | bytes 589832 | tf_op jit(solution)/shard_map/ppermute | solution.py:70
  73.4 2.9 %shard_map.70 = bf16[1536,3072]{1,0:T(8,128)(2,1)} custom-call(bf16[1536,1024]{1,0:T(8,128)(2,1)S(1)} %shard_map.65.inputs_t, bf16[128,3072]{1,0:T(8,128)(2,1)S(1)} %shard_map.59.refs_0_, bf16[128,3072]{1,0:T(8,128)(2,1)S(1)} %bitcast.36, bf16[128,3072]{1,0:T(8,128)(2,1)S(1)} %bitcast.18, ...), custom_call_target="tpu_custom_call", output_to_operand_aliasing={{}: (9, {})} | custom-call | flops 1 | bytes 1 | tf_op jit(solution)/shard_map/pallas_call | solution.py:257
  76.3 2.4 %collective-permute-done.17 = bf16[64,1536]{1,0:T(8,128)(2,1)S(1)} collective-permute-done((bf16[64,1536]{1,0:T(8,128)(2,1)S(1)}, bf16[64,1536]{1,0:T(8,128)(2,1)S(1)}, u32[]{:S(2)}, u32[]{:S(2)}) %collective-permute-start.17) | collective-permute-done | bytes 196640 | tf_op jit(solution)/shard_map/ppermute | solution.py:70
  78.7 0.9 %collective-permute-done.19 = bf16[64,1536]{1,0:T(8,128)(2,1)S(1)} collective-permute-done((bf16[64,1536]{1,0:T(8,128)(2,1)S(1)}, bf16[64,1536]{1,0:T(8,128)(2,1)S(1)}, u32[]{:S(2)}, u32[]{:S(2)}) %collective-permute-start.19) | collective-permute-done | bytes 196640 | tf_op jit(solution)/shard_map/ppermute | solution.py:70
  (25 shorter events, 3.7 us)
Async XLA Ops:
  2.7 16.5 %copy-start = (bf16[64,1536]{1,0:T(8,128)(2,1)S(1)}, bf16[64,1536]{1,0:T(8,128)(2,1)}, u32[]{:S(2)}) copy-start(bf16[64,1536]{1,0:T(8,128)(2,1)} %param.4) | copy-start | bytes 589828
  2.7 14.4 %collective-permute-start.1 = (bf16[2,64,3072]{2,1,0:T(8,128)(2,1)S(1)}, bf16[2,64,3072]{2,1,0:T(8,128)(2,1)S(1)}, u32[]{:S(2)}, u32[]{:S(2)}) collective-permute-start(bf16[2,64,3072]{2,1,0:T(8,128)(2,1)S(1)} %bitcast.12), channel_id=1, source_target_pairs={{0,2},{1,7},{2,4},{3,1},{4,6},{5,3},{6,0},{7,5},{8,10},{9,15},{10,... | collective-permute-start | bytes 2359304 | tf_op jit(solution)/shard_map/ppermute | solution.py:70
  4.4 12.7 %collective-permute-start = (bf16[2,64,3072]{2,1,0:T(8,128)(2,1)S(1)}, bf16[2,64,3072]{2,1,0:T(8,128)(2,1)S(1)}, u32[]{:S(2)}, u32[]{:S(2)}) collective-permute-start(bf16[2,64,3072]{2,1,0:T(8,128)(2,1)S(1)} %bitcast.13), channel_id=1, source_target_pairs={{0,1},{1,0},{2,3},{3,2},{4,5},{5,4},{6,7},{7,6},{8,9},{9,8},{10,11... | collective-permute-start | bytes 2359304 | tf_op jit(solution)/shard_map/ppermute | solution.py:70
  5.4 9.6 %collective-permute-start.3 = (bf16[64,1536]{1,0:T(8,128)(2,1)}, bf16[64,1536]{1,0:T(8,128)(2,1)S(1)}, u32[]{:S(2)}, u32[]{:S(2)}) collective-permute-start(bf16[64,1536]{1,0:T(8,128)(2,1)} %param.4), channel_id=1, source_target_pairs={{0,16},{1,65},{2,18},{3,67},{4,20},{5,69},{6,22},{7,71},{8,24},{9,... | collective-permute-start | bytes 589832 | tf_op jit(solution)/shard_map/ppermute | solution.py:70
  9.3 7.0 %collective-permute-start.2 = (bf16[64,1536]{1,0:T(8,128)(2,1)}, bf16[64,1536]{1,0:T(8,128)(2,1)S(1)}, u32[]{:S(2)}, u32[]{:S(2)}) collective-permute-start(bf16[64,1536]{1,0:T(8,128)(2,1)} %param.4), channel_id=1, source_target_pairs={{0,24},{1,97},{2,26},{3,99},{4,28},{5,101},{6,30},{7,103},{8,0},{9... | collective-permute-start | bytes 589832 | tf_op jit(solution)/shard_map/ppermute | solution.py:70
  10.0 7.1 %collective-permute-start.4 = (bf16[64,1536]{1,0:T(8,128)(2,1)}, bf16[64,1536]{1,0:T(8,128)(2,1)S(1)}, u32[]{:S(2)}, u32[]{:S(2)}) collective-permute-start(bf16[64,1536]{1,0:T(8,128)(2,1)} %param.4), channel_id=1, source_target_pairs={{0,8},{1,33},{2,10},{3,35},{4,12},{5,37},{6,14},{7,39},{8,16},{9,4... | collective-permute-start | bytes 589832 | tf_op jit(solution)/shard_map/ppermute | solution.py:70
  17.1 7.9 %collective-permute-start.10 = (bf16[2,64,3072]{2,1,0:T(8,128)(2,1)S(1)}, bf16[2,64,3072]{2,1,0:T(8,128)(2,1)S(1)}, u32[]{:S(2)}, u32[]{:S(2)}) collective-permute-start(bf16[2,64,3072]{2,1,0:T(8,128)(2,1)S(1)} %collective-permute-done.1.refs_0_), channel_id=1, source_target_pairs={{0,1},{1,0},{2,3},{3,2},{4,5},{5,4},{6,7},{7,6},{8,9},{9,8},{10,11... | collective-permute-start | bytes 2359304 | tf_op jit(solution)/shard_map/ppermute | solution.py:70
  17.1 20.3 %collective-permute-start.8 = (bf16[2,64,3072]{2,1,0:T(8,128)(2,1)S(1)}, bf16[2,64,3072]{2,1,0:T(8,128)(2,1)S(1)}, u32[]{:S(2)}, u32[]{:S(2)}) collective-permute-start(bf16[2,64,3072]{2,1,0:T(8,128)(2,1)S(1)} %bitcast.14), channel_id=1, source_target_pairs={{0,6},{1,3},{2,0},{3,5},{4,2},{5,7},{6,4},{7,1},{8,14},{9,11},{10,... | collective-permute-start | bytes 2359304 | tf_op jit(solution)/shard_map/ppermute | solution.py:70
  17.9 20.3 %collective-permute-start.9 = (bf16[2,64,3072]{2,1,0:T(8,128)(2,1)S(1)}, bf16[2,64,3072]{2,1,0:T(8,128)(2,1)S(1)}, u32[]{:S(2)}, u32[]{:S(2)}) collective-permute-start(bf16[2,64,3072]{2,1,0:T(8,128)(2,1)S(1)} %collective-permute-done.1.refs_0_), channel_id=1, source_target_pairs={{0,2},{1,7},{2,4},{3,1},{4,6},{5,3},{6,0},{7,5},{8,10},{9,15},{10,... | collective-permute-start | bytes 2359304 | tf_op jit(solution)/shard_map/ppermute | solution.py:70
  19.3 22.3 %collective-permute-start.7 = (bf16[4,64,1536]{2,1,0:T(8,128)(2,1)S(1)}, bf16[4,64,1536]{2,1,0:T(8,128)(2,1)S(1)}, u32[]{:S(2)}, u32[]{:S(2)}) collective-permute-start(bf16[4,64,1536]{2,1,0:T(8,128)(2,1)S(1)} %pad_maximum_fusion.refs_0_), channel_id=1, source_target_pairs={{0,96},{1,25},{2,98},{3,27},{4,100},{5,29},{6,102},{7,31},{8,104},... | collective-permute-start | bytes 2359304 | tf_op jit(solution)/shard_map/ppermute | solution.py:70
  22.1 21.6 %collective-permute-start.6 = (bf16[4,64,1536]{2,1,0:T(8,128)(2,1)S(1)}, bf16[4,64,1536]{2,1,0:T(8,128)(2,1)S(1)}, u32[]{:S(2)}, u32[]{:S(2)}) collective-permute-start(bf16[4,64,1536]{2,1,0:T(8,128)(2,1)S(1)} %pad_maximum_fusion.refs_0_), channel_id=1, source_target_pairs={{0,32},{1,9},{2,34},{3,11},{4,36},{5,13},{6,38},{7,15},{8,40},{9,1... | collective-permute-start | bytes 2359304 | tf_op jit(solution)/shard_map/ppermute | solution.py:70
  25.0 18.8 %collective-permute-start.5 = (bf16[4,64,1536]{2,1,0:T(8,128)(2,1)S(1)}, bf16[4,64,1536]{2,1,0:T(8,128)(2,1)S(1)}, u32[]{:S(2)}, u32[]{:S(2)}) collective-permute-start(bf16[4,64,1536]{2,1,0:T(8,128)(2,1)S(1)} %pad_maximum_fusion.refs_0_), channel_id=1, source_target_pairs={{0,64},{1,17},{2,66},{3,19},{4,68},{5,21},{6,70},{7,23},{8,72},{9,... | collective-permute-start | bytes 2359304 | tf_op jit(solution)/shard_map/ppermute | solution.py:70
  38.2 5.5 %collective-permute-start.11 = (bf16[2,64,3072]{2,1,0:T(8,128)(2,1)S(1)}, bf16[2,64,3072]{2,1,0:T(8,128)(2,1)S(1)}, u32[]{:S(2)}, u32[]{:S(2)}) collective-permute-start(bf16[2,64,3072]{2,1,0:T(8,128)(2,1)S(1)} %collective-permute-done.9.refs_0_), channel_id=1, source_target_pairs={{0,1},{1,0},{2,3},{3,2},{4,5},{5,4},{6,7},{7,6},{8,9},{9,8},{10,11... | collective-permute-start | bytes 2359304 | tf_op jit(solution)/shard_map/ppermute | solution.py:70
  38.3 5.5 %collective-permute-start.12 = (bf16[2,64,3072]{2,1,0:T(8,128)(2,1)S(1)}, bf16[2,64,3072]{2,1,0:T(8,128)(2,1)S(1)}, u32[]{:S(2)}, u32[]{:S(2)}) collective-permute-start(bf16[2,64,3072]{2,1,0:T(8,128)(2,1)S(1)} %collective-permute-done.8.refs_1_), channel_id=1, source_target_pairs={{0,1},{1,0},{2,3},{3,2},{4,5},{5,4},{6,7},{7,6},{8,9},{9,8},{10,11... | collective-permute-start | bytes 2359304 | tf_op jit(solution)/shard_map/ppermute | solution.py:70
  46.6 13.3 %collective-permute-start.13 = (bf16[2,2,64,1536]{3,2,1,0:T(8,128)(2,1)S(1)}, bf16[2,2,64,1536]{3,2,1,0:T(8,128)(2,1)S(1)}, u32[]{:S(2)}, u32[]{:S(2)}) collective-permute-start(bf16[2,2,64,1536]{3,2,1,0:T(8,128)(2,1)S(1)} %get-tuple-element.130), channel_id=1, source_target_pairs={{0,8},{1,33},{2,10},{3,35},{4,12},{5,37},{6,14},{7,39},{8,16},{9,4... | collective-permute-start | bytes 2359304 | tf_op jit(solution)/shard_map/ppermute | solution.py:70
  47.5 12.4 %collective-permute-start.14 = (bf16[2,2,64,1536]{3,2,1,0:T(8,128)(2,1)S(1)}, bf16[2,2,64,1536]{3,2,1,0:T(8,128)(2,1)S(1)}, u32[]{:S(2)}, u32[]{:S(2)}) collective-permute-start(bf16[2,2,64,1536]{3,2,1,0:T(8,128)(2,1)S(1)} %get-tuple-element.131), channel_id=1, source_target_pairs={{0,24},{1,97},{2,26},{3,99},{4,28},{5,101},{6,30},{7,103},{8,0},{9... | collective-permute-start | bytes 2359304 | tf_op jit(solution)/shard_map/ppermute | solution.py:70
  60.1 9.1 %collective-permute-start.15 = (bf16[2,64,1536]{2,1,0:T(8,128)(2,1)S(1)}, bf16[2,64,1536]{2,1,0:T(8,128)(2,1)S(1)}, u32[]{:S(2)}, u32[]{:S(2)}) collective-permute-start(bf16[2,64,1536]{2,1,0:T(8,128)(2,1)S(1)} %get-tuple-element.137), channel_id=1, source_target_pairs={{0,8},{1,33},{2,10},{3,35},{4,12},{5,37},{6,14},{7,39},{8,16},{9,4... | collective-permute-start | bytes 1179656 | tf_op jit(solution)/shard_map/ppermute | solution.py:70
  61.6 7.8 %collective-permute-start.16 = (bf16[2,64,1536]{2,1,0:T(8,128)(2,1)S(1)}, bf16[2,64,1536]{2,1,0:T(8,128)(2,1)S(1)}, u32[]{:S(2)}, u32[]{:S(2)}) collective-permute-start(bf16[2,64,1536]{2,1,0:T(8,128)(2,1)S(1)} %get-tuple-element.138), channel_id=1, source_target_pairs={{0,24},{1,97},{2,26},{3,99},{4,28},{5,101},{6,30},{7,103},{8,0},{9... | collective-permute-start | bytes 1179656 | tf_op jit(solution)/shard_map/ppermute | solution.py:70
  69.7 9.1 %collective-permute-start.17 = (bf16[64,1536]{1,0:T(8,128)(2,1)S(1)}, bf16[64,1536]{1,0:T(8,128)(2,1)S(1)}, u32[]{:S(2)}, u32[]{:S(2)}) collective-permute-start(bf16[64,1536]{1,0:T(8,128)(2,1)S(1)} %get-tuple-element.144), channel_id=1, source_target_pairs={{0,32},{1,9},{2,34},{3,11},{4,36},{5,13},{6,38},{7,15},{8,40},{9,1... | collective-permute-start | bytes 589832 | tf_op jit(solution)/shard_map/ppermute | solution.py:70
  69.8 9.0 %collective-permute-start.18 = (bf16[64,1536]{1,0:T(8,128)(2,1)S(1)}, bf16[64,1536]{1,0:T(8,128)(2,1)S(1)}, u32[]{:S(2)}, u32[]{:S(2)}) collective-permute-start(bf16[64,1536]{1,0:T(8,128)(2,1)S(1)} %get-tuple-element.145), channel_id=1, source_target_pairs={{0,64},{1,17},{2,66},{3,19},{4,68},{5,21},{6,70},{7,23},{8,72},{9,... | collective-permute-start | bytes 589832 | tf_op jit(solution)/shard_map/ppermute | solution.py:70
  72.0 7.7 %collective-permute-start.19 = (bf16[64,1536]{1,0:T(8,128)(2,1)S(1)}, bf16[64,1536]{1,0:T(8,128)(2,1)S(1)}, u32[]{:S(2)}, u32[]{:S(2)}) collective-permute-start(bf16[64,1536]{1,0:T(8,128)(2,1)S(1)} %get-tuple-element.146), channel_id=1, source_target_pairs={{0,96},{1,25},{2,98},{3,27},{4,100},{5,29},{6,102},{7,31},{8,104},... | collective-permute-start | bytes 589832 | tf_op jit(solution)/shard_map/ppermute | solution.py:70
